TPU v7x, 128 devices: a whole 4x4x4 slice. The times are simulated.
128 devices in a mesh: batch: 16 (over y, z), tensor: 8 (over x, core).
Axes of the slice: x: 4, y: 4, z: 4, core: 2. Of those that a mesh axis runs over, the one named last changes fastest.
Arguments:
- layer_input: bfloat16 [2, 192, 12288], P(None, None, 'batch'), may hold values from -100 to 100
- attn_gain: bfloat16 [12288], P('batch'), may hold values from 0.099609375 to 1.8984375
- ffn_gain: bfloat16 [12288], P('batch'), may hold values from 0.099609375 to 1.8984375
- query_weight: bfloat16 [12288, 12288], P('batch', 'tensor'), may hold values from -0.0546875 to 0.0546875
- keyval_weight: bfloat16 [2, 12288, 1024], P(None, 'batch', 'tensor'), may hold values from -0.0546875 to 0.0546875
- output_weight: bfloat16 [12288, 12288], P('tensor', 'batch'), may hold values from -0.0546875 to 0.0546875
- gateup_weight: bfloat16 [2, 12288, 21504], P(None, 'batch', 'tensor'), may hold values from -0.0546875 to 0.0546875
- down_weight: bfloat16 [21504, 12288], P('tensor', 'batch'), may hold values from -0.0390625 to 0.0390625
- past_cache: bfloat16 [2, 192, 256, 1024], P(None, 'batch', None, 'tensor'), may hold values from -103 to 103
- parent_rows: int32 [2, 192], replicated, may hold values from 0 to 191, as said below
Outputs:
- layer_out: bfloat16 [2, 192, 12288], P(None, 'tensor', 'batch')
- cache_out: bfloat16 [2, 192, 256, 1024], P(None, 'batch', None, 'tensor')
- fresh_out: bfloat16 [2, 192, 2, 1024], P(None, 'batch', None, 'tensor')
Inputs may be any that keep to these rules, and one draw needn't show every extreme that they name: `parent_rows`: rows of one batch index are 12 consecutive rows. At every step, each batch index's child rows continue rows held by exactly 6 batch indices, exactly 2 child rows for each of them, in no fixed order among the child rows; a parent row may have any number of children.
All inputs are finite; a program needn't handle non-finite values.
Results may differ from a plain program's by a relative error of at most 0.0088.
Values may be sent and summed in bfloat16 or wider, within the bound.
No kernel may reach another device: no remote copies, remote signals or barrier semaphores. Data moves between devices by JAX's collectives and lax.ppermute only.
A program may use at most 128 MiB of HBM per device.

v0:
```python
import math

import jax
import jax.numpy as jnp
from jax import lax
from jax.sharding import PartitionSpec as P

D = 12288
HD = 128
SLOTS = 2
STEPS = 2


rope_base = 1000000.0
norm_eps = 1e-05


def rotate(values, position, head_count):
    row_total = values.shape[0]
    shaped = values.reshape(row_total, head_count, HD)
    half_dim = HD // 2
    inverse = jnp.exp(-math.log(rope_base) * jnp.arange(half_dim, dtype=jnp.float32) * (2.0 / HD))
    angles = position * inverse
    cosine = jnp.cos(angles)
    sines = jnp.sin(angles)
    first_half = shaped[..., :half_dim]
    second_half = shaped[..., half_dim:]
    turned = jnp.concatenate(
        [first_half * cosine - second_half * sines, second_half * cosine + first_half * sines],
        axis=-1,
    )
    return turned.reshape(row_total, head_count * HD)


def attend(queries, key_pages, positions):
    row_total = queries.shape[0]
    kv_heads = key_pages.shape[3] // HD
    group_size = queries.shape[1] // (kv_heads * HD)
    used_pages = key_pages[:, :, :positions]
    query_heads = queries.reshape(row_total, kv_heads, group_size, HD)
    key_heads = used_pages[0].reshape(row_total, positions, kv_heads, HD)
    value_heads = used_pages[1].reshape(row_total, positions, kv_heads, HD)
    scores = jnp.einsum(
        "nkgd,ntkd->nkgt", query_heads, key_heads, preferred_element_type=jnp.float32
    ) * (1.0 / math.sqrt(HD))
    weights = jax.nn.softmax(scores, axis=-1).astype(jnp.bfloat16)
    mixed = jnp.einsum("nkgt,ntkd->nkgd", weights, value_heads, preferred_element_type=jnp.float32)
    return mixed.astype(jnp.bfloat16).reshape(row_total, kv_heads * group_size * HD)


def on_device(
    layer_input,
    attn_gain,
    ffn_gain,
    query_weight,
    keyval_weight,
    output_weight,
    gateup_weight,
    down_weight,
    past_cache,
    parent_rows,
):
    my_index = lax.axis_index("batch")
    batch_count = lax.axis_size("batch")
    tensor_index = lax.axis_index("tensor")
    tensor_count = lax.axis_size("tensor")
    local_rows = past_cache.shape[1]
    cache_len = past_cache.shape[2]
    all_rows = parent_rows.shape[1]
    share_rows = all_rows // tensor_count
    head_width = query_weight.shape[1]
    kv_width = keyval_weight.shape[2]
    ffn_width = gateup_weight.shape[2]
    caches = jnp.concatenate(
        [past_cache, jnp.zeros((2, local_rows, STEPS, kv_width), jnp.bfloat16)], axis=2
    )
    slot_ids = jnp.arange(SLOTS, dtype=jnp.int32)
    row_ids = jnp.arange(local_rows, dtype=jnp.int32)
    outputs = []
    for step_index in range(STEPS):
        position = cache_len + step_index
        inputs = layer_input[step_index].astype(jnp.float32)
        squares = lax.psum(jnp.sum(inputs * inputs, axis=1), "batch")
        normed = (
            inputs * lax.rsqrt(squares / D + norm_eps)[:, None] * attn_gain.astype(jnp.float32)
        ).astype(jnp.bfloat16)
        projected = lax.psum_scatter(
            jnp.concatenate(
                [
                    jnp.dot(normed, query_weight, preferred_element_type=jnp.float32),
                    jnp.dot(normed, keyval_weight[0], preferred_element_type=jnp.float32),
                    jnp.dot(normed, keyval_weight[1], preferred_element_type=jnp.float32),
                ],
                axis=1,
            ),
            "batch",
            scatter_dimension=0,
            tiled=True,
        )
        queries = rotate(projected[:, :head_width], position, head_width // HD).astype(jnp.bfloat16)
        new_keys = rotate(
            projected[:, head_width : head_width + kv_width], position, kv_width // HD
        ).astype(jnp.bfloat16)
        new_values = projected[:, head_width + kv_width :].astype(jnp.bfloat16)
        fresh_pair = jnp.stack([new_keys, new_values])
        route_now = parent_rows[step_index]
        owners = route_now // local_rows
        sources = route_now - owners * local_rows
        my_owners = lax.dynamic_slice_in_dim(owners, my_index * local_rows, local_rows)
        earlier = (my_owners[:, None] == my_owners[None, :]) & (row_ids[None, :] < row_ids[:, None])
        my_rank = jnp.sum(earlier.astype(jnp.int32), axis=1)
        arrival = my_owners * SLOTS + my_rank
        grid_owners = owners.reshape(batch_count, local_rows)
        held_mask = (grid_owners == my_index).astype(jnp.int32)
        held_rank = jnp.cumsum(held_mask, axis=1) - 1
        matched = (held_mask[:, :, None] == 1) & (held_rank[:, :, None] == slot_ids[None, None, :])
        chosen = jnp.sum(
            matched.astype(jnp.int32) * sources.reshape(batch_count, local_rows)[:, :, None], axis=1
        ).reshape(-1)
        outgoing = jnp.take(caches, chosen, axis=1)
        arrived = lax.all_to_all(outgoing, "batch", split_axis=1, concat_axis=1, tiled=True)
        caches = jnp.take(arrived, arrival, axis=1)
        caches = caches.at[:, :, position].set(fresh_pair)
        attended = attend(queries, caches, position + 1)
        gathered_heads = lax.all_gather(attended, "batch", axis=0, tiled=True)
        mixed_all = lax.psum(
            jnp.dot(gathered_heads, output_weight, preferred_element_type=jnp.float32), "tensor"
        )
        residual = inputs + mixed_all
        all_squares = lax.psum(jnp.sum(residual * residual, axis=1), "batch")
        hidden_in = (
            residual * lax.rsqrt(all_squares / D + norm_eps)[:, None] * ffn_gain.astype(jnp.float32)
        ).astype(jnp.bfloat16)
        residual_share = lax.dynamic_slice_in_dim(
            residual, tensor_index * share_rows, share_rows, 0
        )
        gateup_all = lax.psum(
            jnp.concatenate(
                [
                    jnp.dot(hidden_in, gateup_weight[0], preferred_element_type=jnp.float32),
                    jnp.dot(hidden_in, gateup_weight[1], preferred_element_type=jnp.float32),
                ],
                axis=1,
            ),
            "batch",
        )
        activated = (jax.nn.silu(gateup_all[:, :ffn_width]) * gateup_all[:, ffn_width:]).astype(
            jnp.bfloat16
        )
        down_share = lax.psum_scatter(
            jnp.dot(activated, down_weight, preferred_element_type=jnp.float32),
            "tensor",
            scatter_dimension=0,
            tiled=True,
        )
        outputs.append((residual_share + down_share).astype(jnp.bfloat16))
    return (jnp.stack(outputs), caches[:, :, :cache_len], caches[:, :, cache_len:])


def solution(mesh):
    return jax.shard_map(
        on_device,
        mesh=mesh,
        in_specs=(
            P(None, None, "batch"),
            P("batch"),
            P("batch"),
            P("batch", "tensor"),
            P(None, "batch", "tensor"),
            P("tensor", "batch"),
            P(None, "batch", "tensor"),
            P("tensor", "batch"),
            P(None, "batch", None, "tensor"),
            P(),
        ),
        out_specs=(
            P(None, "tensor", "batch"),
            P(None, "batch", None, "tensor"),
            P(None, "batch", None, "tensor"),
        ),
        check_vma=False,
    )
```

profile of v0, /device:TPU:1, one launch (start us, length us, event | category | flops | bytes accessed | tf_op | source)
XLA Modules:
  0.0 711.6 jit_solution(7499906627185448773)
XLA Ops:
  14.4 11.5 %gather_fusion = bf16[32,2,258,128]{3,1,2,0:T(2,128)(2,1)} fusion(bf16[2,12,258,128]{3,0,2,1:T(2,128)(2,1)} %concatenate.37, s32[1024]{0:T(1024)S(1)} %pad_clamp_fusion.3), kind=kCustom, calls=%fused_computation.clone | custom fusion | bytes 8454272 | tf_op jit(solution)/shard_map/jit(_take)/gather | solution.py:120
  25.9 7.9 %fusion.2 = bf16[2,32,258,128]{3,0,2,1:T(2,128)(2,1)} fusion(bf16[32,2,258,128]{3,1,2,0:T(2,128)(2,1)} %gather_fusion, pred[32]{0:T(512)(128)(4,1)S(1)} %compare_and_fusion.3), kind=kLoop, calls=%fused_computation.8 | loop fusion | flops 2113536 | bytes 8454176 | tf_op jit(solution)/shard_map/jit(_take)/select_n | solution.py:120
  33.8 8.9 %all-to-all-start = ((bf16[2,32,258,128]{3,0,2,1:T(2,128)(2,1)}), bf16[2,32,258,128]{3,0,2,1:T(2,128)(2,1)}, u32[]{:S(2)}, u32[]{:S(2)}) async-start(bf16[2,32,258,128]{3,0,2,1:T(2,128)(2,1)} %fusion.2), calls=%async_computation | async-start | bytes 8454144 | tf_op jit(solution)/shard_map/all_to_all | solution.py:121
  43.0 85.6 %all-reduce.4 = (f32[192]{0:T(256)S(1)}, f32[192]{0:T(256)S(1)}) all-reduce(f32[192]{0:T(256)S(1)} %get-tuple-element.39, f32[192]{0:T(256)S(1)} %get-tuple-element.38), channel_id=1, replica_groups=mesh['batch'=16,'tensor'=8] {'batch'}, use_global_device_ids=true, to_apply=%region_1.0 | all-reduce | flops 384 | bytes 3072 | tf_op jit(solution)/shard_map/psum | solution.py:83
  136.1 98.1 %all-reduce.14.cloned.1.call-done = (f32[192,1792]{1,0:T(8,128)}, f32[192,1792]{1,0:T(8,128)}) async-done(((f32[192,1792]{1,0:T(8,128)}, f32[192,1792]{1,0:T(8,128)}), (f32[192,1792]{1,0:T(8,128)}, f32[192,1792]{1,0:T(8,128)})) %all-reduce.14.cloned.1.call-update) | async-done | bytes 2752528
  236.0 7.9 %gather_fusion.1 = bf16[12,2,258,128]{3,1,2,0:T(2,128)(2,1)} fusion(bf16[2,32,258,128]{3,0,2,1:T(2,128)(2,1)} %all-to-all-done, s32[1024]{0:T(1024)S(1)} %pad_clamp_fusion.2), kind=kCustom, calls=%fused_computation.1.clone | custom fusion | bytes 3170352 | tf_op jit(solution)/shard_map/jit(_take)/gather | solution.py:122
  248.7 4.7 select_bitcast_fusion
  253.4 7.5 %copy.55 = bf16[2,32,258,128]{3,0,2,1:T(2,128)(2,1)} copy(bf16[2,32,258,128]{3,2,0,1:T(8,128)(2,1)} %select_bitcast_fusion) | data formatting | bytes 8454144 | tf_op jit(solution)/shard_map/jit(_take)/select_n | solution.py:120
  260.9 4.5 all-to-all-start.1
  270.9 65.0 %all-gather = bf16[16,12,1536]{2,1,0:T(8,128)(2,1)S(1)} all-gather(bf16[1,12,1536]{2,1,0:T(8,128)(2,1)S(1)} %reshape.459), channel_id=1, replica_groups=mesh['batch'=16,'tensor'=8] {'batch'}, dimensions={0}, use_global_device_ids=true | all-gather | bytes 626688 | tf_op jit(solution)/shard_map/all_gather | solution.py:125
  336.1 3.2 fusion.105
  339.2 7.9 %gather_fusion.3 = bf16[12,2,258,128]{3,1,2,0:T(2,128)(2,1)} fusion(bf16[2,32,258,128]{3,0,2,1:T(2,128)(2,1)} %all-to-all-done.1, s32[1024]{0:T(1024)S(1)} %pad_clamp_fusion), kind=kCustom, calls=%fused_computation.3.clone | custom fusion | bytes 3170352 | tf_op jit(solution)/shard_map/jit(_take)/gather | solution.py:122
  350.0 19.2 %all-gather.1 = bf16[16,12,1536]{2,1,0:T(8,128)(2,1)S(1)} all-gather(bf16[1,12,1536]{2,1,0:T(8,128)(2,1)S(1)} %reshape.461), channel_id=1, replica_groups=mesh['batch'=16,'tensor'=8] {'batch'}, dimensions={0}, use_global_device_ids=true | all-gather | bytes 626688 | tf_op jit(solution)/shard_map/all_gather | solution.py:125
  369.4 3.2 fusion.106
  372.6 70.9 %all-reduce.16.cloned.1.call-done = (f32[192,768]{1,0:T(8,128)}, f32[192,768]{1,0:T(8,128)}) async-done(((f32[192,768]{1,0:T(8,128)}, f32[192,768]{1,0:T(8,128)}), (f32[192,768]{1,0:T(8,128)}, f32[192,768]{1,0:T(8,128)})) %all-reduce.16.cloned.1.call-update) | async-done | bytes 1179664 | tf_op jit(solution)/shard_map/psum | solution.py:126
  445.0 33.5 %all-reduce.3 = (f32[192]{0:T(256)S(1)}, f32[192]{0:T(256)S(1)}) all-reduce(f32[192]{0:T(256)S(1)} %get-tuple-element.66, f32[192]{0:T(256)S(1)} %get-tuple-element.54), channel_id=1, replica_groups=mesh['batch'=16,'tensor'=8] {'batch'}, use_global_device_ids=true, to_apply=%region_23.26 | all-reduce | flops 384 | bytes 3072 | tf_op jit(solution)/shard_map/psum | solution.py:130
  478.5 3.4 fusion.5
  481.9 3.4 fusion.9
  485.3 3.2 fusion.3
  494.1 143.2 %all-reduce.12.cloned.1.call-done = (f32[192,5376]{1,0:T(8,128)}, f32[192,5376]{1,0:T(8,128)}) async-done(((f32[192,5376]{1,0:T(8,128)}, f32[192,5376]{1,0:T(8,128)}), (f32[192,5376]{1,0:T(8,128)}, f32[192,5376]{1,0:T(8,128)})) %all-reduce.12.cloned.1.call-update) | async-done | bytes 8257552 | tf_op jit(solution)/shard_map/psum | solution.py:137
  637.3 5.6 fusion.23
  643.0 5.5 fusion.25
  652.8 17.8 %reduce-scatter.3.cloned.1.call-done = f32[24,768]{1,0:T(8,128)} async-done(((f32[192,768]{1,0:T(8,128)}), f32[24,768]{1,0:T(8,128)}) %reduce-scatter.3.cloned.1.call-update) | async-done | bytes 73744 | tf_op jit(solution)/shard_map/reduce_scatter | solution.py:150
  672.1 30.6 %reduce-scatter.5.cloned.1.call-done = f32[24,768]{1,0:T(8,128)} async-done(((f32[192,768]{1,0:T(8,128)}), f32[24,768]{1,0:T(8,128)}) %reduce-scatter.5.cloned.1.call-update) | async-done | bytes 73744 | tf_op jit(solution)/shard_map/reduce_scatter | solution.py:150
  (136 shorter events, 44.4 us)
Async XLA Ops:
  7.2 122.4 %copy-start = (bf16[768,1536]{1,0:T(8,128)(2,1)S(1)}, bf16[768,1536]{1,0:T(8,128)(2,1)}, u32[]{:S(2)}) copy-start(bf16[768,1536]{1,0:T(8,128)(2,1)} %param.21) | copy-start | bytes 7077892
  33.8 9.0 %copy-start.3 = (bf16[2,192,768]{2,1,0:T(8,128)(2,1)S(1)}, bf16[2,192,768]{2,1,0:T(8,128)(2,1)}, u32[]{:S(2)}) copy-start(bf16[2,192,768]{2,1,0:T(8,128)(2,1)} %param.18) | copy-start | bytes 1769476
  33.8 9.2 %copy-start.6 = (bf16[768]{0:T(1024)(128)(2,1)S(1)}, bf16[768]{0:T(1024)(128)(2,1)}, u32[]{:S(2)}) copy-start(bf16[768]{0:T(1024)(128)(2,1)} %param.19) | copy-start | bytes 4612
  33.8 94.8 %copy-start.8 = (bf16[2,768,128]{2,1,0:T(8,128)(2,1)S(1)}, bf16[2,768,128]{2,1,0:T(8,128)(2,1)}, u32[]{:S(2)}) copy-start(bf16[2,768,128]{2,1,0:T(8,128)(2,1)} %param.22) | copy-start | bytes 1179652
  33.8 202.1 %all-to-all-start = ((bf16[2,32,258,128]{3,0,2,1:T(2,128)(2,1)}), bf16[2,32,258,128]{3,0,2,1:T(2,128)(2,1)}, u32[]{:S(2)}, u32[]{:S(2)}) async-start(bf16[2,32,258,128]{3,0,2,1:T(2,128)(2,1)} %fusion.2), calls=%async_computation | async-start | bytes 8454144 | tf_op jit(solution)/shard_map/all_to_all | solution.py:121
  42.7 191.4 %all-reduce.14.cloned.1.call-start = ((), (), s32[]{:S(2)}) async-start(), calls=%async_computation.7 | async-start | bytes 5505024
  133.6 0.7 copy-start.9
  133.6 2.0 copy-start.5
  260.9 78.3 %all-to-all-start.1 = ((bf16[2,32,258,128]{3,0,2,1:T(2,128)(2,1)}), bf16[2,32,258,128]{3,0,2,1:T(2,128)(2,1)}, u32[]{:S(2)}, u32[]{:S(2)}) async-start(bf16[2,32,258,128]{3,0,2,1:T(2,128)(2,1)} %copy.55), calls=%async_computation.2 | async-start | bytes 8454144 | tf_op jit(solution)/shard_map/all_to_all | solution.py:121
  265.4 178.1 %all-reduce.16.cloned.1.call-start = ((), (), s32[]{:S(2)}) async-start(), calls=%async_computation.8 | async-start | bytes 2359296 | tf_op jit(solution)/shard_map/psum | solution.py:126
  348.9 20.3 %copy-start.2 = (bf16[2,12,258,128]{3,2,1,0:T(8,128)(2,1)}, bf16[2,12,258,128]{3,2,1,0:T(8,128)(2,1)S(1)}, u32[]{:S(2)}) copy-start(bf16[2,12,258,128]{3,2,1,0:T(8,128)(2,1)S(1)} %scatter.9) | copy-start | bytes 4755460
  369.3 3.3 copy-start.7
  369.4 74.1 %copy-start.4 = (bf16[2,192,768]{2,1,0:T(8,128)(2,1)S(1)}, bf16[2,192,768]{2,1,0:T(8,128)(2,1)}, u32[]{:S(2)}) copy-start(bf16[2,192,768]{2,1,0:T(8,128)(2,1)} %param.18) | copy-start | bytes 1769476
  372.6 264.8 %all-reduce.12.cloned.1.call-start = ((), (), s32[]{:S(2)}) async-start(), calls=%async_computation.6 | async-start | bytes 16515072 | tf_op jit(solution)/shard_map/psum | solution.py:137
  478.5 10.0 %slice-start = ((s8[8257536]{0:T(1024)(128)(4,1)}), s8[4194304]{0:T(1024)(128)(4,1)S(1)}, s32[]{:S(2)}) async-start(s8[8257536]{0:T(1024)(128)(4,1)} %bitcast.115), calls=%async_computation.9 | async-start | bytes 8388608
  481.9 6.7 slice-start.1
  494.1 176.6 %reduce-scatter.3.cloned.1.call-start = ((), (), s32[]{:S(2)}) async-start(), calls=%async_computation.4 | async-start | bytes 663552 | tf_op jit(solution)/shard_map/reduce_scatter | solution.py:150
  642.9 59.8 %reduce-scatter.5.cloned.1.call-start = ((), (), s32[]{:S(2)}) async-start(), calls=%async_computation.5 | async-start | bytes 663552 | tf_op jit(solution)/shard_map/reduce_scatter | solution.py:150
  648.5 56.6 %copy-start.1 = (bf16[768,1536]{1,0:T(8,128)(2,1)S(1)}, bf16[768,1536]{1,0:T(8,128)(2,1)}, u32[]{:S(2)}) copy-start(bf16[768,1536]{1,0:T(8,128)(2,1)} %param.21) | copy-start | bytes 7077892
Sparse Core Ops, SparseCore 0:
  133.8 100.3 all-reduce.13
  372.7 70.7 all-reduce.15
  494.2 143.0 all-reduce.11
  643.0 27.5 reduce-scatter.2
  672.9 29.8 reduce-scatter.4
where the time goes:
time: 715 us; the launch traced here: 712 us
  waiting for transfers between devices  361 us (50%)
  blocking collectives  203 us (28%)
  local copies, waits for them, and re-layouts  55.2 us (8%)
  matrix products  32.6 us (5%)
  other arithmetic  31.2 us (4%)
  between operations  15 us (2%)
  starting transfers between devices  13.7 us (2%)
    psum x1, waiting for transfers between devices, on_device(): lax.psum(jnp.concatenate([jnp.dot(hidden_in, gateup_weight[0], preferred_...  143 us
    unnamed x6, waiting for transfers between devices  98.2 us
    psum x1, blocking collectives, on_device(): squares = lax.psum(jnp.sum(inputs * inputs, axis=1), 'batch')  85.6 us
    all_gather x2, blocking collectives, on_device(): gathered_heads = lax.all_gather(attended, 'batch', axis=0, tiled=True)  84.2 us
    psum x1, waiting for transfers between devices, on_device(): lax.psum(jnp.dot(gathered_heads, output_weight, preferred_element_type=jn...  70.9 us
    reduce_scatter x2, waiting for transfers between devices, on_device(): lax.psum_scatter(jnp.dot(activated, down_weight, preferred_element_type=j...  48.4 us
    psum x1, blocking collectives, on_device(): all_squares = lax.psum(jnp.sum(residual * residual, axis=1), 'batch')  33.5 us
    gather x2, local copies, waits for them, and re-layouts, on_device(): caches = jnp.take(arrived, arrival, axis=1)  15.9 us
  transfers between devices with their start and end apart: 7, of which 5 were waited for; matrix products, arithmetic and copies ran while one was open for 4% of the time, Pallas kernels for 0%

commit v1 on v0

v1 whole, which is shorter than its diff:
```python
import functools
import math

import jax
import jax.numpy as jnp
from jax import lax
from jax.experimental import pallas as pl
from jax.experimental.pallas import tpu as pltpu
from jax.sharding import PartitionSpec as P

HD = 128
LANES = 128
STEPS = 2

rope_base = 1000000.0
norm_eps = 1e-05


def exchange(blocks, axis):
    return lax.all_to_all(blocks, axis, split_axis=0, concat_axis=0, tiled=True)


def gather_all(block, axis):
    copies = jnp.broadcast_to(block[None], (lax.axis_size(axis),) + block.shape)
    return exchange(lax.optimization_barrier(copies), axis)


def split_pair(values):
    high = values.astype(jnp.bfloat16)
    low = (values - high.astype(jnp.float32)).astype(jnp.bfloat16)
    return high, low


def rotary(steps, first_position):
    inverse = jnp.exp(
        -math.log(rope_base) * jnp.arange(HD // 2, dtype=jnp.float32) * (2.0 / HD)
    )
    angles = (first_position + steps).astype(jnp.float32)[:, None] * inverse[None, :]
    cosine, sine = jnp.cos(angles), jnp.sin(angles)
    return jnp.concatenate([cosine, cosine], axis=1), jnp.concatenate([-sine, sine], axis=1)


def rotate(heads, cosine, sine):
    swapped = jnp.concatenate([heads[..., HD // 2 :], heads[..., : HD // 2]], axis=-1)
    return heads * cosine + swapped * sine


def pick_kernel(index_ref, table_ref, out_ref):
    def body(row, carry):
        out_ref[row] = table_ref[index_ref[row]]
        return carry

    lax.fori_loop(0, out_ref.shape[0], body, 0, unroll=8)


def pick_rows(table, index):
    return pl.pallas_call(
        pick_kernel,
        out_shape=jax.ShapeDtypeStruct((index.shape[0],) + table.shape[1:], table.dtype),
        in_specs=[
            pl.BlockSpec(memory_space=pltpu.SMEM),
            pl.BlockSpec(memory_space=pltpu.VMEM),
        ],
        out_specs=pl.BlockSpec(memory_space=pltpu.VMEM),
        compiler_params=pltpu.CompilerParams(vmem_limit_bytes=32 * 1024 * 1024),
        cost_estimate=pl.CostEstimate(
            flops=0, bytes_accessed=3 * index.shape[0] * table[0].size, transcendentals=0
        ),
        name="pick_rows",
    )(index, table)


def on_device(
    layer_input,
    attn_gain,
    ffn_gain,
    query_weight,
    keyval_weight,
    output_weight,
    gateup_weight,
    down_weight,
    past_cache,
    parent_rows,
):
    batches = lax.axis_size("batch")
    tensors = lax.axis_size("tensor")
    tensor_index = lax.axis_index("tensor")
    _, rows, past, kv_width = past_cache.shape
    width = layer_input.shape[2]
    model = width * batches
    head_width = query_weight.shape[1]
    heads = head_width // HD
    hidden = gateup_weight.shape[2]
    both = STEPS * rows
    total = batches * both
    share = total // tensors
    span = past // batches

    parents = parent_rows.reshape(STEPS, batches, rows)
    origin = jnp.take(parent_rows[0], parent_rows[1], axis=0)
    wanted = jnp.stack([parents[0], origin.reshape(batches, rows)], axis=1).reshape(total)

    with jax.named_scope("cache_spread"):
        pieces = past_cache.reshape(2, rows, batches, span, kv_width).transpose(2, 1, 0, 3, 4)
        spread = exchange(pieces, "batch").reshape(batches * rows, 2, span, kv_width)

    with jax.named_scope("project"):
        inputs = (
            layer_input.reshape(STEPS, batches, rows, width)
            .transpose(1, 0, 2, 3)
            .reshape(total, width)
        )
        wide = inputs.astype(jnp.float32)
        squares = jnp.sum(wide * wide, axis=1)
        scaled = (wide * attn_gain.astype(jnp.float32)).astype(jnp.bfloat16)
        chosen = (
            parent_rows[1][:, None] == jnp.arange(batches * rows, dtype=jnp.int32)[None, :]
        ).astype(jnp.bfloat16)
        first_step = scaled.reshape(batches, STEPS, rows, width)[:, 0].reshape(-1, width)
        parent_scaled = jnp.dot(
            chosen, first_step, preferred_element_type=jnp.float32
        ).astype(jnp.bfloat16)
        parent_squares = jnp.dot(
            chosen.astype(jnp.float32),
            squares.reshape(batches, STEPS, rows)[:, 0].reshape(-1),
            precision=lax.Precision.HIGHEST,
        )
        project = functools.partial(jnp.dot, preferred_element_type=jnp.float32)
        parent_pair = jnp.stack(
            [
                project(parent_scaled, keyval_weight[0]).reshape(batches, rows, kv_width),
                project(parent_scaled, keyval_weight[1]).reshape(batches, rows, kv_width),
            ],
            axis=1,
        ).reshape(total, kv_width)
        parent_squares = jnp.concatenate(
            [parent_squares.reshape(batches, 1, rows)] * STEPS, axis=1
        ).reshape(total)
        statistics = jnp.stack(split_pair(squares) + split_pair(parent_squares), axis=1)
        sums = jnp.concatenate(
            [
                project(scaled, query_weight).astype(jnp.bfloat16),
                project(scaled, keyval_weight[0]).astype(jnp.bfloat16),
                project(scaled, keyval_weight[1]).astype(jnp.bfloat16),
                parent_pair.astype(jnp.bfloat16),
                jnp.pad(statistics, ((0, 0), (0, LANES - statistics.shape[1]))),
            ],
            axis=1,
        ).reshape(batches, both, -1)
        summed = jnp.sum(exchange(sums, "batch").astype(jnp.float32), axis=0)

    with jax.named_scope("cache_return"):
        picked = pick_rows(spread, wanted).reshape(batches, both, 2, span, kv_width)
        returned = exchange(picked, "batch").transpose(2, 1, 0, 3, 4)
        caches = returned.reshape(2, both, past, kv_width)
        cache_out = caches[:, rows:]

    with jax.named_scope("attention"):
        edge = head_width + 3 * kv_width
        mean = (summed[:, edge] + summed[:, edge + 1]) / model
        parent_mean = (summed[:, edge + 2] + summed[:, edge + 3]) / model
        scale = lax.rsqrt(mean + norm_eps)[:, None]
        parent_scale = lax.rsqrt(parent_mean + norm_eps)[:, None]
        step_of = jnp.arange(both, dtype=jnp.int32) // rows
        cosine, sine = rotary(step_of, past)
        queries = rotate(
            (summed[:, :head_width] * scale).reshape(both, heads, HD),
            cosine[:, None],
            sine[:, None],
        ).astype(jnp.bfloat16)
        new_keys = rotate(
            summed[:, head_width : head_width + kv_width] * scale, cosine, sine
        ).astype(jnp.bfloat16)
        new_values = (
            summed[:, head_width + kv_width : head_width + 2 * kv_width] * scale
        ).astype(jnp.bfloat16)
        parent_sums = summed[:, head_width + 2 * kv_width : edge] * parent_scale
        parent_keys = rotate(parent_sums[:rows], cosine[:rows], sine[:rows]).astype(jnp.bfloat16)
        parent_values = parent_sums[rows:].astype(jnp.bfloat16)
        fresh_keys = jnp.stack(
            [jnp.concatenate([new_keys[:rows], parent_keys]), new_keys], axis=1
        )
        fresh_values = jnp.stack(
            [jnp.concatenate([new_values[:rows], parent_values]), new_values], axis=1
        )
        fresh_out = jnp.stack([fresh_keys[rows:], fresh_values[rows:]])
        old_scores = jnp.einsum(
            "ngd,ntd->ngt", queries, caches[0], preferred_element_type=jnp.float32
        )
        fresh_scores = jnp.einsum(
            "ngd,ntd->ngt", queries, fresh_keys, preferred_element_type=jnp.float32
        )
        scores = jnp.concatenate([old_scores, fresh_scores], axis=2) * (1.0 / math.sqrt(HD))
        place = jnp.arange(past + STEPS, dtype=jnp.int32)
        seen = place[None, :] <= (past + step_of)[:, None]
        scores = jnp.where(seen[:, None, :], scores, -jnp.inf)
        weights = jax.nn.softmax(scores, axis=-1).astype(jnp.bfloat16)
        attended = jnp.einsum(
            "ngt,ntd->ngd", weights[..., :past], caches[1], preferred_element_type=jnp.float32
        ) + jnp.einsum(
            "ngt,ntd->ngd", weights[..., past:], fresh_values, preferred_element_type=jnp.float32
        )
        attended = attended.astype(jnp.bfloat16).reshape(both, head_width)
        attended = gather_all(attended, "batch").reshape(total, head_width)

    with jax.named_scope("output_projection"):
        mixed = jnp.dot(attended, output_weight, preferred_element_type=jnp.float32)
        mixed = exchange(mixed.astype(jnp.bfloat16).reshape(tensors, share, width), "tensor")
        own_inputs = lax.dynamic_slice_in_dim(inputs, tensor_index * share, share, 0)
        residual = own_inputs.astype(jnp.float32) + jnp.sum(mixed.astype(jnp.float32), axis=0)
        gain = ffn_gain.astype(jnp.float32)
        lifted = gather_all((residual * gain).astype(jnp.bfloat16), "tensor")
        lifted = lifted.reshape(total, width)

    with jax.named_scope("gate_up"):
        plain = lifted.astype(jnp.float32) * (1.0 / gain)
        squares = jnp.stack(split_pair(jnp.sum(plain * plain, axis=1)), axis=1)
        sums = jnp.concatenate(
            [
                project(lifted, gateup_weight[0]).astype(jnp.bfloat16),
                project(lifted, gateup_weight[1]).astype(jnp.bfloat16),
                jnp.pad(squares, ((0, 0), (0, LANES - squares.shape[1]))),
            ],
            axis=1,
        ).reshape(batches, both, -1)
        summed = jnp.sum(exchange(sums, "batch").astype(jnp.float32), axis=0)
        mean = (summed[:, 2 * hidden] + summed[:, 2 * hidden + 1]) / model
        summed = summed[:, : 2 * hidden] * lax.rsqrt(mean + norm_eps)[:, None]
        activated = (jax.nn.silu(summed[:, :hidden]) * summed[:, hidden:]).astype(jnp.bfloat16)
        activated = gather_all(activated, "batch").reshape(total, hidden)

    with jax.named_scope("down_projection"):
        lowered = jnp.dot(activated, down_weight, preferred_element_type=jnp.float32)
        lowered = exchange(lowered.astype(jnp.bfloat16).reshape(tensors, share, width), "tensor")
        final = (residual + jnp.sum(lowered.astype(jnp.float32), axis=0)).astype(jnp.bfloat16)
        layer_out = (
            final.reshape(share // both, STEPS, rows, width)
            .transpose(1, 0, 2, 3)
            .reshape(STEPS, share // STEPS, width)
        )
    return layer_out, cache_out, fresh_out


def solution(mesh):
    return jax.shard_map(
        on_device,
        mesh=mesh,
        in_specs=(
            P(None, None, "batch"),
            P("batch"),
            P("batch"),
            P("batch", "tensor"),
            P(None, "batch", "tensor"),
            P("tensor", "batch"),
            P(None, "batch", "tensor"),
            P("tensor", "batch"),
            P(None, "batch", None, "tensor"),
            P(),
        ),
        out_specs=(
            P(None, "tensor", "batch"),
            P(None, "batch", None, "tensor"),
            P(None, "batch", None, "tensor"),
        ),
        check_vma=False,
    )
```

time: 715 us -> 295 us (0.41)
  waiting for transfers between devices: 361 us -> 72.8 us
  blocking collectives: 203 us -> 106 us
  local copies, waits for them, and re-layouts: 55.2 us -> 24.6 us
  starting transfers between devices: 13.7 us -> 41.1 us
  between operations: 15 us -> 1.17 us
  other arithmetic: 31.2 us -> 19.5 us
  matrix products: 32.6 us -> 24.9 us
    psum x2 -> x0, waiting for transfers between devices: 214 us -> none  [the longest x1 143 us: on_device(): lax.psum(jnp.concatenate([jnp.dot(hidden_in, gateup_weight[0], preferred_...]
    psum x2 -> x0, blocking collectives: 119 us -> none  [the longest x1 85.6 us: on_device(): squares = lax.psum(jnp.sum(inputs * inputs, axis=1), 'batch')]
    all_to_all x0 -> x3, blocking collectives: none -> 106 us  [exchange(): return lax.all_to_all(blocks, axis, split_axis=0, concat_axis=0, tiled=True)]
    unnamed x6 -> x0, waiting for transfers between devices: 98.2 us -> none
    all_gather x2 -> x0, blocking collectives: 84.2 us -> none  [on_device(): gathered_heads = lax.all_gather(attended, 'batch', axis=0, tiled=True)]
    all_to_all x2 -> x6, waiting for transfers between devices: 0.01 us -> 72.8 us  [exchange(): return lax.all_to_all(blocks, axis, split_axis=0, concat_axis=0, tiled=True)]
    reduce_scatter x2 -> x0, waiting for transfers between devices: 48.4 us -> none  [on_device(): lax.psum_scatter(jnp.dot(activated, down_weight, preferred_element_type=j...]
    gather x4 -> x2, local copies, waits for them, and re-layouts: 30.5 us -> 1.69 us  [on_device(): origin = jnp.take(parent_rows[0], parent_rows[1], axis=0)]
  transfers between devices with their start and end apart: 7 -> 6, of which waited for: 5 -> 5; matrix products, arithmetic and copies ran while one was open for 4% -> 11% of each run, Pallas kernels for 0% -> 1%
where the time goes in v1:
time: 295 us; the launch traced here: 294 us
  blocking collectives  106 us (36%)
  waiting for transfers between devices  72.8 us (25%)
  starting transfers between devices  41.1 us (14%)
  matrix products  24.9 us (8%)
  local copies, waits for them, and re-layouts  24.6 us (8%)
  other arithmetic  19.5 us (7%)
  Pallas kernels  3.74 us (1%)
    all_to_all x3, blocking collectives, exchange(): return lax.all_to_all(blocks, axis, split_axis=0, concat_axis=0, tiled=True)  106 us
    all_to_all x6, waiting for transfers between devices, exchange(): return lax.all_to_all(blocks, axis, split_axis=0, concat_axis=0, tiled=True)  72.8 us
    all_to_all x6, starting transfers between devices, exchange(): return lax.all_to_all(blocks, axis, split_axis=0, concat_axis=0, tiled=True)  41.1 us
  transfers between devices with their start and end apart: 6, of which 5 were waited for; matrix products, arithmetic and copies ran while one was open for 11% of the time, Pallas kernels for 1%

profile of v1, /device:TPU:1, one launch (start us, length us, event | category | flops | bytes accessed | tf_op | source)
XLA Modules:
  0.0 294.2 jit_solution(14944094623413219684)
XLA Ops:
  0.6 3.1 %copy.222 = bf16[2,12,16,16,128]{4,3,0,1,2:T(8,128)(2,1)} copy(bf16[2,12,16,16,128]{4,3,2,1,0:T(8,128)(2,1)} %bitcast.104) | data formatting | bytes 3145728 | tf_op jit(solution)/shard_map/cache_spread/reshape | solution.py:104
  3.8 8.8 %all-to-all-start.1 = ((bf16[16,12,2,16,128]{4,3,2,1,0:T(8,128)(2,1)}), bf16[16,12,2,16,128]{4,3,2,1,0:T(8,128)(2,1)}, u32[]{:S(2)}, u32[]{:S(2)}) async-start(bf16[16,12,2,16,128]{4,3,2,1,0:T(8,128)(2,1)} %bitcast.97), calls=%async_computation.1 | async-start | bytes 3145728 | tf_op jit(solution)/shard_map/cache_spread/all_to_all | solution.py:20
  20.8 2.1 copy.183
  27.7 2.1 convert_element_type.228
  29.8 2.1 fusion.7
  35.1 6.7 %all-to-all-start = ((bf16[16,24,2048]{2,1,0:T(8,128)(2,1)}), bf16[16,24,2048]{2,1,0:T(8,128)(2,1)}, u32[]{:S(2)}, u32[]{:S(2)}) async-start(bf16[16,24,2048]{2,1,0:T(8,128)(2,1)} %bitcast.13), calls=%async_computation | async-start | bytes 3145728 | tf_op jit(solution)/shard_map/project/all_to_all | solution.py:20
  44.0 3.7 %pick_rows.1 = bf16[384,2,16,128]{3,2,1,0:T(8,128)(2,1)} custom-call(s32[384]{0:T(512)S(1)} %reshape.363.index_ref, bf16[192,2,16,128]{3,2,1,0:T(8,128)(2,1)} %bitcast.19.table_ref), custom_call_target="tpu_custom_call" | custom-call | bytes 4718592 | tf_op jit(solution)/shard_map/cache_return/pick_rows/pallas_call | solution.py:57
  47.7 14.5 %all-to-all-done = bf16[16,24,2048]{2,1,0:T(8,128)(2,1)} async-done(((bf16[16,24,2048]{2,1,0:T(8,128)(2,1)}), bf16[16,24,2048]{2,1,0:T(8,128)(2,1)}, u32[]{:S(2)}, u32[]{:S(2)}) %all-to-all-start) | async-done | bytes 1572896 | tf_op jit(solution)/shard_map/project/all_to_all | solution.py:20
  62.3 4.4 %all-to-all-start.2 = ((bf16[16,24,2,16,128]{4,3,2,1,0:T(8,128)(2,1)}), bf16[16,24,2,16,128]{4,3,2,1,0:T(8,128)(2,1)S(1)}, u32[]{:S(2)}, u32[]{:S(2)}) async-start(bf16[16,24,2,16,128]{4,3,2,1,0:T(8,128)(2,1)} %bitcast.20), calls=%async_computation.2 | async-start | bytes 6291456 | tf_op jit(solution)/shard_map/cache_return/all_to_all | solution.py:20
  71.6 30.2 %all-to-all-done.2 = bf16[16,24,2,16,128]{4,3,2,1,0:T(8,128)(2,1)S(1)} async-done(((bf16[16,24,2,16,128]{4,3,2,1,0:T(8,128)(2,1)}), bf16[16,24,2,16,128]{4,3,2,1,0:T(8,128)(2,1)S(1)}, u32[]{:S(2)}, u32[]{:S(2)}) %all-to-all-start.2) | async-done | bytes 3145760 | tf_op jit(solution)/shard_map/cache_return/all_to_all | solution.py:20
  104.2 4.3 %fusion.85 = (f32[24,12]{1,0:T(8,128)S(1)}, f32[24,12,258]{2,1,0:T(8,128)S(1)}) fusion(f32[24,12,2]{2,1,0:T(8,128)S(1)} %fusion.58, f32[24,12,256]{2,1,0:T(8,128)S(1)} %fusion.86, pred[24,258]{1,0:T(8,128)(4,1)S(1)} %copy-done.5), kind=kOutput, calls=%fused_computation.163 | output fusion | flops 371777 | bytes 601776 | tf_op jit(solution)/shard_map/attention/sub | solution.py:197
  109.3 23.6 %all_to_all.45 = bf16[16,24,1536]{2,1,0:T(8,128)(2,1)S(1)} all-to-all(bf16[16,24,1536]{2,1,0:T(8,128)(2,1)S(1)} %broadcast_in_dim.30), channel_id=1, replica_groups=mesh['batch'=16,'tensor'=8] {'batch'}, dimensions={0} | all-to-all | bytes 2359296 | tf_op jit(solution)/shard_map/attention/all_to_all | solution.py:20
  134.8 9.2 %all-to-all-start.4 = ((bf16[8,48,768]{2,1,0:T(8,128)(2,1)}), bf16[8,48,768]{2,1,0:T(8,128)(2,1)}, u32[]{:S(2)}, u32[]{:S(2)}) async-start(bf16[8,48,768]{2,1,0:T(8,128)(2,1)} %bitcast.106), calls=%async_computation.4 | async-start | bytes 1179648 | tf_op jit(solution)/shard_map/output_projection/all_to_all | solution.py:20
  144.0 10.3 %all-to-all-done.4 = bf16[8,48,768]{2,1,0:T(8,128)(2,1)} async-done(((bf16[8,48,768]{2,1,0:T(8,128)(2,1)}), bf16[8,48,768]{2,1,0:T(8,128)(2,1)}, u32[]{:S(2)}, u32[]{:S(2)}) %all-to-all-start.4) | async-done | bytes 589856 | tf_op jit(solution)/shard_map/output_projection/all_to_all | solution.py:20
  157.2 4.9 %all-to-all-start.5 = ((bf16[8,48,768]{2,1,0:T(8,128)(2,1)}), bf16[8,48,768]{2,1,0:T(8,128)(2,1)}, u32[]{:S(2)}, u32[]{:S(2)}) async-start(bf16[8,48,768]{2,1,0:T(8,128)(2,1)} %broadcast_in_dim.31), calls=%async_computation.5 | async-start | bytes 1179648 | tf_op jit(solution)/shard_map/output_projection/all_to_all | solution.py:20
  162.2 10.3 %all-to-all-done.5 = bf16[8,48,768]{2,1,0:T(8,128)(2,1)} async-done(((bf16[8,48,768]{2,1,0:T(8,128)(2,1)}), bf16[8,48,768]{2,1,0:T(8,128)(2,1)}, u32[]{:S(2)}, u32[]{:S(2)}) %all-to-all-start.5) | async-done | bytes 589856 | tf_op jit(solution)/shard_map/output_projection/all_to_all | solution.py:20
  172.5 5.5 %convolution_convert_fusion = bf16[384,2688]{1,0:T(8,128)(2,1)} fusion(bf16[384,768]{1,0:T(8,128)(2,1)} %bitcast.30, bf16[2,768,2688]{2,1,0:T(8,128)(2,1)} %param.16), kind=kOutput, calls=%fused_computation.6 | convolution fusion | flops 1586479104 | bytes 6782976 | tf_op jit(solution)/shard_map/gate_up/dot_general | solution.py:221
  178.0 5.5 %convolution_convert_fusion.1 = bf16[384,2688]{1,0:T(8,128)(2,1)} fusion(bf16[384,768]{1,0:T(8,128)(2,1)} %bitcast.30, bf16[2,768,2688]{2,1,0:T(8,128)(2,1)} %param.16), kind=kOutput, calls=%fused_computation.7 | convolution fusion | flops 1586479104 | bytes 6782976 | tf_op jit(solution)/shard_map/gate_up/dot_general | solution.py:220
  185.1 2.3 fusion.2
  187.4 53.0 %all_to_all.46 = bf16[16,24,5504]{2,1,0:T(8,128)(2,1)S(1)} all-to-all(bf16[16,24,5504]{2,1,0:T(8,128)(2,1)S(1)} %bitcast.95), channel_id=1, replica_groups=mesh['batch'=16,'tensor'=8] {'batch'}, dimensions={0} | all-to-all | bytes 8454144 | tf_op jit(solution)/shard_map/gate_up/all_to_all | solution.py:20
  241.5 29.7 %all_to_all.47 = bf16[16,24,2688]{2,1,0:T(8,128)(2,1)S(1)} all-to-all(bf16[16,24,2688]{2,1,0:T(8,128)(2,1)S(1)} %broadcast_in_dim.32), channel_id=1, replica_groups=mesh['batch'=16,'tensor'=8] {'batch'}, dimensions={0} | all-to-all | bytes 4128768 | tf_op jit(solution)/shard_map/gate_up/all_to_all | solution.py:20
  271.3 2.7 convolution_convert_fusion.4
  273.9 7.1 %all-to-all-start.8 = ((bf16[8,48,768]{2,1,0:T(8,128)(2,1)}), bf16[8,48,768]{2,1,0:T(8,128)(2,1)}, u32[]{:S(2)}, u32[]{:S(2)}) async-start(bf16[8,48,768]{2,1,0:T(8,128)(2,1)} %bitcast.107), calls=%async_computation.8 | async-start | bytes 1179648 | tf_op jit(solution)/shard_map/down_projection/all_to_all | solution.py:20
  283.9 7.4 %all-to-all-done.8 = bf16[8,48,768]{2,1,0:T(8,128)(2,1)} async-done(((bf16[8,48,768]{2,1,0:T(8,128)(2,1)}), bf16[8,48,768]{2,1,0:T(8,128)(2,1)}, u32[]{:S(2)}, u32[]{:S(2)}) %all-to-all-start.8) | async-done | bytes 589856 | tf_op jit(solution)/shard_map/down_projection/all_to_all | solution.py:20
  (128 shorter events, 39.2 us)
Async XLA Ops:
  0.6 29.1 %copy-start = (bf16[768,1536]{1,0:T(8,128)(2,1)S(1)}, bf16[768,1536]{1,0:T(8,128)(2,1)}, u32[]{:S(2)}) copy-start(bf16[768,1536]{1,0:T(8,128)(2,1)} %param.13) | copy-start | bytes 7077892
  3.8 8.8 %copy-start.8 = (bf16[768]{0:T(1024)(128)(2,1)S(1)}, bf16[768]{0:T(1024)(128)(2,1)}, u32[]{:S(2)}) copy-start(bf16[768]{0:T(1024)(128)(2,1)} %param.11) | copy-start | bytes 4612
  3.8 11.6 %copy-start.7 = (s32[2,192]{1,0:T(2,128)S(1)}, s32[2,192]{1,0:T(2,128)}, u32[]{:S(2)}) copy-start(s32[2,192]{1,0:T(2,128)} %param.19) | copy-start | bytes 4612
  3.8 31.3 %all-to-all-start.1 = ((bf16[16,12,2,16,128]{4,3,2,1,0:T(8,128)(2,1)}), bf16[16,12,2,16,128]{4,3,2,1,0:T(8,128)(2,1)}, u32[]{:S(2)}, u32[]{:S(2)}) async-start(bf16[16,12,2,16,128]{4,3,2,1,0:T(8,128)(2,1)} %bitcast.97), calls=%async_computation.1 | async-start | bytes 3145728 | tf_op jit(solution)/shard_map/cache_spread/all_to_all | solution.py:20
  27.6 2.2 copy-start.2
  29.7 2.1 copy-start.3
  29.8 2.1 copy-start.4
  35.1 27.2 %all-to-all-start = ((bf16[16,24,2048]{2,1,0:T(8,128)(2,1)}), bf16[16,24,2048]{2,1,0:T(8,128)(2,1)}, u32[]{:S(2)}, u32[]{:S(2)}) async-start(bf16[16,24,2048]{2,1,0:T(8,128)(2,1)} %bitcast.13), calls=%async_computation | async-start | bytes 3145728 | tf_op jit(solution)/shard_map/project/all_to_all | solution.py:20
  62.3 39.6 %all-to-all-start.2 = ((bf16[16,24,2,16,128]{4,3,2,1,0:T(8,128)(2,1)}), bf16[16,24,2,16,128]{4,3,2,1,0:T(8,128)(2,1)S(1)}, u32[]{:S(2)}, u32[]{:S(2)}) async-start(bf16[16,24,2,16,128]{4,3,2,1,0:T(8,128)(2,1)} %bitcast.20), calls=%async_computation.2 | async-start | bytes 6291456 | tf_op jit(solution)/shard_map/cache_return/all_to_all | solution.py:20
  103.2 1.0 copy-start.5
  109.1 23.8 %copy-start.10 = (bf16[1536,768]{1,0:T(8,128)(2,1)S(1)}, bf16[1536,768]{1,0:T(8,128)(2,1)}, u32[]{:S(2)}) copy-start(bf16[1536,768]{1,0:T(8,128)(2,1)} %param.15) | copy-start | bytes 7077892
  132.9 11.1 %copy-start.6 = (bf16[768]{0:T(1024)(128)(2,1)S(1)}, bf16[768]{0:T(1024)(128)(2,1)}, u32[]{:S(2)}) copy-start(bf16[768]{0:T(1024)(128)(2,1)} %param.12) | copy-start | bytes 4612
  134.8 19.5 %all-to-all-start.4 = ((bf16[8,48,768]{2,1,0:T(8,128)(2,1)}), bf16[8,48,768]{2,1,0:T(8,128)(2,1)}, u32[]{:S(2)}, u32[]{:S(2)}) async-start(bf16[8,48,768]{2,1,0:T(8,128)(2,1)} %bitcast.106), calls=%async_computation.4 | async-start | bytes 1179648 | tf_op jit(solution)/shard_map/output_projection/all_to_all | solution.py:20
  157.2 15.2 %all-to-all-start.5 = ((bf16[8,48,768]{2,1,0:T(8,128)(2,1)}), bf16[8,48,768]{2,1,0:T(8,128)(2,1)}, u32[]{:S(2)}, u32[]{:S(2)}) async-start(bf16[8,48,768]{2,1,0:T(8,128)(2,1)} %broadcast_in_dim.31), calls=%async_computation.5 | async-start | bytes 1179648 | tf_op jit(solution)/shard_map/output_projection/all_to_all | solution.py:20
  241.5 29.8 %copy-start.9 = (bf16[2688,768]{1,0:T(8,128)(2,1)S(1)}, bf16[2688,768]{1,0:T(8,128)(2,1)}, u32[]{:S(2)}) copy-start(bf16[2688,768]{1,0:T(8,128)(2,1)} %param.17) | copy-start | bytes 12386308
  273.9 17.4 %all-to-all-start.8 = ((bf16[8,48,768]{2,1,0:T(8,128)(2,1)}), bf16[8,48,768]{2,1,0:T(8,128)(2,1)}, u32[]{:S(2)}, u32[]{:S(2)}) async-start(bf16[8,48,768]{2,1,0:T(8,128)(2,1)} %bitcast.107), calls=%async_computation.8 | async-start | bytes 1179648 | tf_op jit(solution)/shard_map/down_projection/all_to_all | solution.py:20
  282.6 11.5 %copy-start.1 = (bf16[768,1536]{1,0:T(8,128)(2,1)S(1)}, bf16[768,1536]{1,0:T(8,128)(2,1)}, u32[]{:S(2)}) copy-start(bf16[768,1536]{1,0:T(8,128)(2,1)} %param.13) | copy-start | bytes 7077892

commit v2 on v1

v2 whole, which is shorter than its diff:
```python
import functools
import math

import jax
import jax.numpy as jnp
from jax import lax
from jax.experimental import pallas as pl
from jax.experimental.pallas import tpu as pltpu
from jax.sharding import PartitionSpec as P

HD = 128
LANES = 128
STEPS = 2
MIB = 1024 * 1024

rope_base = 1000000.0
norm_eps = 1e-05


def exchange(blocks, axis):
    return lax.all_to_all(blocks, axis, split_axis=0, concat_axis=0, tiled=True)


def gather_all(block, axis):
    copies = jnp.broadcast_to(block[None], (lax.axis_size(axis),) + block.shape)
    gathered = exchange(lax.optimization_barrier(copies), axis)
    return gathered.reshape((-1,) + block.shape[1:])


def after(value, earlier):
    return lax.optimization_barrier((value, earlier))[0]


def shift_along(block, minor_axis, count):
    side = math.isqrt(lax.axis_size("batch"))
    pairs = []
    for major in range(side):
        for minor in range(side):
            target = (
                (major, (minor + count) % side) if minor_axis else ((major + count) % side, minor)
            )
            pairs.append((major * side + minor, target[0] * side + target[1]))
    return lax.ppermute(block, "batch", pairs)


def shift_chips(block, count):
    size = lax.axis_size("tensor")
    return lax.ppermute(block, "tensor", [(at, (at + 2 * count) % size) for at in range(size)])


def swap_cores(block):
    size = lax.axis_size("tensor")
    return lax.ppermute(block, "tensor", [(at, at ^ 1) for at in range(size)])


def shift_both(first, second, first_minor):
    side = len(first)
    middle = side // 2
    others = [count for count in range(1, side) if count != middle]
    first_moved, second_moved = {0: first[0]}, {0: second[0]}
    for count in others + [middle]:
        first_moved[count] = shift_along(first[count], first_minor, count)
    for count in others:
        second_moved[count] = shift_along(second[count], 1 - first_minor, count)
    second_moved[middle] = shift_along(
        after(second[middle], second_moved[1]), 1 - first_minor, middle
    )
    return [first_moved[at] for at in range(side)], [second_moved[at] for at in range(side)]


def fold_kernel(count, *refs):
    sources, targets = refs[:count], refs[count:]
    terms = []
    for source in sources:
        terms += [source] if len(source.shape) == 2 else [source.at[at] for at in range(source.shape[0])]
    total = terms[0][...].astype(jnp.float32)
    for term in terms[1:]:
        total = total + term[...].astype(jnp.float32)
    rows = total.shape[0] // len(targets)
    for place, target in enumerate(targets):
        target[...] = total[place * rows : (place + 1) * rows].astype(target.dtype)


def fold(sources, pieces):
    rows, columns = sources[0].shape[-2:]
    kinds = [jnp.float32] + [jnp.bfloat16] * (pieces - 1)
    whole = pl.BlockSpec(memory_space=pltpu.VMEM)
    return pl.pallas_call(
        functools.partial(fold_kernel, len(sources)),
        out_shape=[jax.ShapeDtypeStruct((rows // pieces, columns), kind) for kind in kinds],
        in_specs=[whole] * len(sources),
        out_specs=[whole] * pieces,
        compiler_params=pltpu.CompilerParams(vmem_limit_bytes=32 * MIB),
        cost_estimate=pl.CostEstimate(flops=1, bytes_accessed=1, transcendentals=0),
        name="fold",
    )(*sources)


def add_over_batch(first, second, earlier):
    side = len(first)
    first, second = shift_both(first, second, 1)
    first, second = after((first, second), earlier)
    first, second = fold(first, side), fold(second, side)
    first, second = shift_both(first, second, 0)
    return [functools.reduce(lambda a, b: a + b.astype(jnp.float32), own) for own in (first, second)]


def exchange_minor(blocks):
    side = math.isqrt(lax.axis_size("batch"))
    groups = [[major * side + minor for minor in range(side)] for major in range(side)]
    return lax.all_to_all(
        blocks, "batch", split_axis=0, concat_axis=0, tiled=True, axis_index_groups=groups
    )


def add_along(own, terms):
    return functools.reduce(lambda total, term: total + term.astype(jnp.float32), terms, own)


def add_crossed(first, second):
    side = len(second)
    others = range(1, side)
    moved = [second[0]] + [shift_along(second[count], 0, count) for count in others]
    arrived = exchange_minor(first)
    summed = fold([arrived], side)
    first = add_along(summed[0], [shift_along(summed[count], 0, count) for count in others])
    crossed = add_along(moved[0].astype(jnp.float32), moved[1:]).astype(jnp.bfloat16)
    crossed = exchange_minor(crossed.reshape((side, -1) + crossed.shape[1:]))
    return first, jnp.sum(crossed.astype(jnp.float32), axis=0)


def add_over_tensor(kept, sent):
    chips = lax.axis_size("tensor") // 2
    pieces = fold([kept, swap_cores(sent)], chips)
    total = pieces[0]
    for count in range(1, chips):
        total = total + shift_chips(pieces[count], count).astype(jnp.float32)
    return total


def blocks_along(values, side, place):
    rows = values.shape[0] // (side * side)
    return jnp.concatenate(
        [
            values[(major * side + place) * rows : (major * side + place + 1) * rows]
            for major in range(side)
        ],
        axis=0,
    )


def one_hot(index, count):
    places = lax.broadcasted_iota(jnp.int32, (index.shape[0], count), 1)
    return jnp.where(places == index, 1.0, 0.0).astype(jnp.bfloat16)


def dot(left, right):
    return jnp.dot(left, right, preferred_element_type=jnp.float32)


def split_pair(values):
    high = values.astype(jnp.bfloat16).astype(jnp.float32)
    return [high, values - high]


def in_lanes(columns):
    lanes = lax.broadcasted_iota(jnp.int32, (columns[0].shape[0], LANES), 1)
    packed = jnp.zeros(lanes.shape, jnp.float32)
    for place, value in enumerate(columns):
        packed = jnp.where(lanes == place, value, packed)
    return packed


def project_kernel(
    side, order_ref, parent_ref, input_ref, gain_ref, query_ref, keyval_ref, *out_refs
):
    steps, count, width = input_ref.shape
    source = input_ref[...].reshape(steps * count, width)
    gain = gain_ref[...].astype(jnp.float32)
    order = order_ref[...]
    is_key = order < count
    own = dot(one_hot(order, steps * count), source)
    parents = dot(one_hot(parent_ref[...], count), input_ref[0]).astype(jnp.bfloat16)
    parents = dot(one_hot(jnp.where(is_key, order, order - count), count), parents)
    statistics = split_pair(jnp.sum(own * own, axis=1, keepdims=True)) + split_pair(
        jnp.sum(parents * parents, axis=1, keepdims=True)
    )
    own = (own * gain).astype(jnp.bfloat16)
    parents = (parents * gain).astype(jnp.bfloat16)
    values = jnp.concatenate(
        [
            dot(own, query_ref[...]),
            dot(own, keyval_ref[0]),
            dot(own, keyval_ref[1]),
            jnp.where(is_key, dot(parents, keyval_ref[0]), dot(parents, keyval_ref[1])),
            in_lanes(statistics),
        ],
        axis=1,
    ).astype(jnp.float32)
    half = values.shape[1] // 2
    rows = values.shape[0] // side
    for place in range(side):
        out_refs[place][...] = blocks_along(values[:, :half], side, place).astype(jnp.bfloat16)
        out_refs[side + place][...] = values[place * rows : (place + 1) * rows, half:].astype(
            jnp.bfloat16
        )


def project_rows(side, order, parents, layer_input, gain, query_weight, keyval_weight):
    total = order.shape[0]
    columns = query_weight.shape[1] + 3 * keyval_weight.shape[2] + LANES
    block = jax.ShapeDtypeStruct((total // side, columns // 2), jnp.bfloat16)
    whole = pl.BlockSpec(memory_space=pltpu.VMEM)
    return pl.pallas_call(
        functools.partial(project_kernel, side),
        out_shape=[block] * (2 * side),
        in_specs=[whole] * 6,
        out_specs=[whole] * (2 * side),
        compiler_params=pltpu.CompilerParams(vmem_limit_bytes=48 * MIB),
        cost_estimate=pl.CostEstimate(
            flops=2 * total * columns * gain.shape[0],
            bytes_accessed=2 * (gain.shape[0] + total) * columns,
            transcendentals=0,
        ),
        name="project_rows",
    )(order, parents, layer_input, gain.reshape(1, -1), query_weight, keyval_weight)


def gate_up_kernel(side, tile, order_ref, near_ref, far_ref, gain_ref, weight_ref, *out_refs):
    first_ref, second_refs = out_refs[0], out_refs[1:]
    lifted = jnp.concatenate([near_ref[...], far_ref[...]], axis=0)
    ordered = dot(one_hot(order_ref[...], lifted.shape[0]), lifted)
    plain = ordered * (1.0 / gain_ref[...].astype(jnp.float32))
    statistics = in_lanes(split_pair(jnp.sum(plain * plain, axis=1, keepdims=True)))
    ordered = ordered.astype(jnp.bfloat16)
    hidden = weight_ref.shape[2]
    rows = ordered.shape[0] // side
    for place in range(side):
        first_ref[place, :, hidden:] = blocks_along(statistics, side, place).astype(jnp.bfloat16)

    def one_tile(columns):
        gates = dot(ordered, weight_ref[0, :, columns])
        for place in range(side):
            first_ref[place, :, columns] = blocks_along(gates, side, place).astype(jnp.bfloat16)
        ups = dot(ordered, weight_ref[1, :, columns])
        for place in range(side):
            second_refs[place][:, columns] = ups[place * rows : (place + 1) * rows].astype(
                jnp.bfloat16
            )

    @pl.loop(0, hidden // tile)
    def _(step):
        one_tile(pl.ds(pl.multiple_of(step * tile, LANES), tile))

    if hidden % tile:
        one_tile(pl.ds(hidden // tile * tile, hidden % tile))


def gate_up(side, order, near, far, gain, weight, tile):
    total, width = order.shape[0], near.shape[1]
    hidden = weight.shape[2]
    whole = pl.BlockSpec(memory_space=pltpu.VMEM)
    return pl.pallas_call(
        functools.partial(gate_up_kernel, side, tile),
        out_shape=[jax.ShapeDtypeStruct((side, total // side, hidden + LANES), jnp.bfloat16)]
        + [jax.ShapeDtypeStruct((total // side, hidden), jnp.bfloat16)] * side,
        in_specs=[whole] * 5,
        out_specs=[whole] * (1 + side),
        compiler_params=pltpu.CompilerParams(vmem_limit_bytes=48 * MIB),
        cost_estimate=pl.CostEstimate(
            flops=4 * total * width * hidden,
            bytes_accessed=4 * hidden * (width + total),
            transcendentals=0,
        ),
        name="gate_up",
    )(order, near, far, gain.reshape(1, -1), weight)


def spread_dot_kernel(place_ref, rows_ref, weight_ref, kept_ref, sent_ref, total_ref):
    values = dot(rows_ref[...], weight_ref[...])
    blocks = place_ref.shape[0]
    rows = values.shape[0] // blocks
    for at in range(blocks):
        target = pl.ds(pl.multiple_of(place_ref[at], 8), rows)
        total_ref[target, :] = values[at * rows : (at + 1) * rows]
    half = kept_ref.shape[0]
    kept_ref[...] = total_ref[:half]
    sent_ref[...] = total_ref[half:]


def spread_dot(places, values, weight):
    total, width = values.shape[0], weight.shape[1]
    whole = pl.BlockSpec(memory_space=pltpu.VMEM)
    return pl.pallas_call(
        spread_dot_kernel,
        out_shape=[jax.ShapeDtypeStruct((total // 2, width), jnp.float32)] * 2,
        in_specs=[pl.BlockSpec(memory_space=pltpu.SMEM), whole, whole],
        out_specs=[whole] * 2,
        scratch_shapes=[pltpu.VMEM((total, width), jnp.float32)],
        compiler_params=pltpu.CompilerParams(vmem_limit_bytes=48 * MIB),
        cost_estimate=pl.CostEstimate(
            flops=2 * total * weight.size,
            bytes_accessed=2 * weight.size + 2 * total * (weight.shape[0] + 4 * width),
            transcendentals=0,
        ),
        name="spread_dot",
    )(places, values, weight)


def rotary(steps, first_position):
    inverse = jnp.exp(
        -math.log(rope_base) * jnp.arange(HD // 2, dtype=jnp.float32) * (2.0 / HD)
    )
    angles = (first_position + steps).astype(jnp.float32)[:, None] * inverse[None, :]
    cosine, sine = jnp.cos(angles), jnp.sin(angles)
    return jnp.concatenate([cosine, cosine], axis=1), jnp.concatenate([-sine, sine], axis=1)


def rotate(heads, cosine, sine):
    swapped = jnp.concatenate([heads[..., HD // 2 :], heads[..., : HD // 2]], axis=-1)
    return heads * cosine + swapped * sine


def pick_kernel(index_ref, table_ref, out_ref):
    def body(row, carry):
        out_ref[row] = table_ref[index_ref[row]]
        return carry

    lax.fori_loop(0, out_ref.shape[0], body, 0, unroll=8)


def pick_rows(table, index):
    return pl.pallas_call(
        pick_kernel,
        out_shape=jax.ShapeDtypeStruct((index.shape[0],) + table.shape[1:], table.dtype),
        in_specs=[
            pl.BlockSpec(memory_space=pltpu.SMEM),
            pl.BlockSpec(memory_space=pltpu.VMEM),
        ],
        out_specs=pl.BlockSpec(memory_space=pltpu.VMEM),
        compiler_params=pltpu.CompilerParams(vmem_limit_bytes=32 * MIB),
        cost_estimate=pl.CostEstimate(
            flops=0, bytes_accessed=3 * index.shape[0] * table[0].size, transcendentals=0
        ),
        name="pick_rows",
    )(index, table)


def on_device(
    layer_input,
    attn_gain,
    ffn_gain,
    query_weight,
    keyval_weight,
    output_weight,
    gateup_weight,
    down_weight,
    past_cache,
    parent_rows,
):
    batches = lax.axis_size("batch")
    tensors = lax.axis_size("tensor")
    side = math.isqrt(batches)
    chips = tensors // 2
    batch_index = lax.axis_index("batch")
    tensor_index = lax.axis_index("tensor")
    my_major, my_minor = batch_index // side, batch_index % side
    my_chip, my_core = tensor_index // 2, tensor_index % 2
    _, rows, past, kv_width = past_cache.shape
    width = layer_input.shape[2]
    model = width * batches
    head_width = query_weight.shape[1]
    heads = head_width // HD
    hidden = gateup_weight.shape[2]
    both = STEPS * rows
    total = batches * both
    share = total // tensors
    span = past // batches

    with jax.named_scope("cache_spread"):
        pieces = past_cache.reshape(2, rows, batches, span, kv_width).transpose(2, 1, 0, 3, 4)
        spread = exchange(pieces, "batch").reshape(batches * rows, 2, span, kv_width)

    with jax.named_scope("places"):
        parents = parent_rows.reshape(STEPS, batches, rows)
        origin = jnp.take(parent_rows[0], parent_rows[1], axis=0)
        wanted = jnp.stack([parents[0], origin.reshape(batches, rows)], axis=1).reshape(total)
        place = jnp.arange(total, dtype=jnp.int32)
        inner = place % both
        ahead = (my_major + place // (side * both)) % side * side
        ahead = ahead + (my_minor + place // both) % side
        input_order = ((inner // rows) * (batches * rows) + ahead * rows + inner % rows)[:, None]
        row = (my_major + place // (side * both)) % side * side + place // both % side
        row = row * both + inner
        owner = row // share
        lifted_order = (owner % 2 != my_core).astype(jnp.int32) * (total // 2)
        lifted_order = lifted_order + (my_chip - owner // 2 + chips) % chips * share
        lifted_order = (lifted_order + row % share)[:, None]
        block = jnp.arange(batches, dtype=jnp.int32)
        owner = block * both // share
        targets = (owner % 2 != my_core).astype(jnp.int32) * (total // 2)
        targets = targets + (owner // 2 - my_chip + chips) % chips * share
        targets = targets + block * both % share

    with jax.named_scope("project"):
        blocks = project_rows(
            side,
            input_order,
            parent_rows[1][:, None],
            after(layer_input, pieces),
            attn_gain,
            query_weight,
            keyval_weight,
        )
        picked = pick_rows(spread, wanted).reshape(batches, both, 2, span, kv_width)
        summed = jnp.concatenate(add_over_batch(blocks[:side], blocks[side:], picked), axis=1)

    with jax.named_scope("cache_return"):
        returned = exchange(picked, "batch").transpose(2, 1, 0, 3, 4)
        caches = returned.reshape(2, both, past, kv_width)
        cache_out = caches[:, rows:]

    with jax.named_scope("attention"):
        edge = head_width + 3 * kv_width
        mean = (summed[:, edge] + summed[:, edge + 1]) / model
        parent_mean = (summed[:, edge + 2] + summed[:, edge + 3]) / model
        scale = lax.rsqrt(mean + norm_eps)[:, None]
        parent_scale = lax.rsqrt(parent_mean + norm_eps)[:, None]
        step_of = jnp.arange(both, dtype=jnp.int32) // rows
        cosine, sine = rotary(step_of, past)
        queries = rotate(
            (summed[:, :head_width] * scale).reshape(both, heads, HD),
            cosine[:, None],
            sine[:, None],
        ).astype(jnp.bfloat16)
        new_keys = rotate(
            summed[:, head_width : head_width + kv_width] * scale, cosine, sine
        ).astype(jnp.bfloat16)
        new_values = (
            summed[:, head_width + kv_width : head_width + 2 * kv_width] * scale
        ).astype(jnp.bfloat16)
        parent_sums = summed[:, head_width + 2 * kv_width : edge] * parent_scale
        parent_keys = rotate(parent_sums[:rows], cosine[:rows], sine[:rows]).astype(jnp.bfloat16)
        parent_values = parent_sums[rows:].astype(jnp.bfloat16)
        fresh_keys = jnp.stack(
            [jnp.concatenate([new_keys[:rows], parent_keys]), new_keys], axis=1
        )
        fresh_values = jnp.stack(
            [jnp.concatenate([new_values[:rows], parent_values]), new_values], axis=1
        )
        fresh_out = jnp.stack([fresh_keys[rows:], fresh_values[rows:]])
        old_scores = jnp.einsum(
            "ngd,ntd->ngt", queries, caches[0], preferred_element_type=jnp.float32
        )
        fresh_scores = jnp.einsum(
            "ngd,ntd->ngt", queries, fresh_keys, preferred_element_type=jnp.float32
        )
        scores = jnp.concatenate([old_scores, fresh_scores], axis=2) * (1.0 / math.sqrt(HD))
        position = jnp.arange(past + STEPS, dtype=jnp.int32)
        seen = position[None, :] <= (past + step_of)[:, None]
        scores = jnp.where(seen[:, None, :], scores, -jnp.inf)
        weights = jax.nn.softmax(scores, axis=-1).astype(jnp.bfloat16)
        attended = jnp.einsum(
            "ngt,ntd->ngd", weights[..., :past], caches[1], preferred_element_type=jnp.float32
        ) + jnp.einsum(
            "ngt,ntd->ngd", weights[..., past:], fresh_values, preferred_element_type=jnp.float32
        )
        attended = attended.astype(jnp.bfloat16).reshape(both, head_width)
        attended = gather_all(attended, "batch")

    with jax.named_scope("output_projection"):
        own_inputs = lax.dynamic_slice_in_dim(
            layer_input, tensor_index * (share // STEPS), share // STEPS, 1
        )
        own_inputs = (
            own_inputs.reshape(STEPS, share // both, rows, width)
            .transpose(1, 0, 2, 3)
            .reshape(share, width)
        )
        mixed = add_over_tensor(*spread_dot(targets, attended, output_weight))
        residual = own_inputs.astype(jnp.float32) + mixed
        lifted = (residual * ffn_gain.astype(jnp.float32)).astype(jnp.bfloat16)
        near = jnp.concatenate(
            [lifted] + [shift_chips(lifted, count) for count in range(1, chips)], axis=0
        )
        far = swap_cores(near)

    with jax.named_scope("gate_up"):
        blocks = gate_up(side, lifted_order, near, far, ffn_gain, gateup_weight, 768)
        gates, ups = add_crossed(blocks[0], blocks[1:])
        mean = (gates[:, hidden] + gates[:, hidden + 1]) / model
        scale = lax.rsqrt(mean + norm_eps)[:, None]
        gates, ups = gates[:, :hidden] * scale, ups * scale
        activated = (jax.nn.silu(gates) * ups).astype(jnp.bfloat16)
        activated = gather_all(activated, "batch")

    with jax.named_scope("down_projection"):
        lowered = add_over_tensor(*spread_dot(targets, activated, down_weight))
        final = (residual + lowered).astype(jnp.bfloat16)
        layer_out = (
            final.reshape(share // both, STEPS, rows, width)
            .transpose(1, 0, 2, 3)
            .reshape(STEPS, share // STEPS, width)
        )
    return layer_out, cache_out, fresh_out


def solution(mesh):
    return jax.shard_map(
        on_device,
        mesh=mesh,
        in_specs=(
            P(None, None, "batch"),
            P("batch"),
            P("batch"),
            P("batch", "tensor"),
            P(None, "batch", "tensor"),
            P("tensor", "batch"),
            P(None, "batch", "tensor"),
            P("tensor", "batch"),
            P(None, "batch", None, "tensor"),
            P(),
        ),
        out_specs=(
            P(None, "tensor", "batch"),
            P(None, "batch", None, "tensor"),
            P(None, "batch", None, "tensor"),
        ),
        check_vma=False,
    )
```

time: 295 us -> 259 us (0.88)
  blocking collectives: 106 us -> 29.8 us
  starting transfers between devices: 41.1 us -> 70.6 us
  waiting for transfers between devices: 72.8 us -> 102 us
  matrix products: 24.9 us -> 1.15 us
  Pallas kernels: 3.74 us -> 21.4 us
  other arithmetic: 19.5 us -> 10.4 us
    all_to_all x3 -> x1, blocking collectives: 106 us -> 29.8 us  [exchange(): return lax.all_to_all(blocks, axis, split_axis=0, concat_axis=0, tiled=True)]
    ppermute x0 -> x30, waiting for transfers between devices: none -> 61.2 us  [the longest x18 47.3 us: shift_along(): return lax.ppermute(block, 'batch', pairs)]
    all_to_all x6 -> x3, waiting for transfers between devices: 72.8 us -> 33.9 us  [exchange(): return lax.all_to_all(blocks, axis, split_axis=0, concat_axis=0, tiled=True)]
    ppermute x0 -> x30, starting transfers between devices: none -> 37.3 us  [the longest x18 17.3 us: shift_along(): return lax.ppermute(block, 'batch', pairs)]
    dot_general x11 -> x0, matrix products: 23.7 us -> none  [the longest x1 5.54 us: on_device(): project(lifted, gateup_weight[1]).astype(jnp.bfloat16)]
    pallas_call x0 -> x9, Pallas kernels: none -> 18.5 us  [the longest x1 7.95 us: gate_up(): pl.pallas_call(functools.partial(gate_up_kernel, side, tile), out_shape=[...]
    all_to_all x6 -> x3, starting transfers between devices: 41.1 us -> 25.6 us  [exchange(): return lax.all_to_all(blocks, axis, split_axis=0, concat_axis=0, tiled=True)]
    all_to_all x0 -> x2, starting transfers between devices: none -> 7.75 us  [exchange_minor(): lax.all_to_all(blocks, 'batch', split_axis=0, concat_axis=0, tiled=True,...]
  transfers between devices with their start and end apart: 6 -> 35, of which waited for: 5 -> 21; matrix products, arithmetic and copies ran while one was open for 11% -> 5% of each run, Pallas kernels for 1% -> 3%
where the time goes in v2:
time: 259 us
  waiting for transfers between devices  102 us (39%)
  starting transfers between devices  70.6 us (27%)
  blocking collectives  29.8 us (12%)
  local copies, waits for them, and re-layouts  22.2 us (9%)
  Pallas kernels  21.4 us (8%)
  other arithmetic  10.4 us (4%)
    ppermute x18, waiting for transfers between devices, shift_along(): return lax.ppermute(block, 'batch', pairs)  47.3 us
    all_to_all x3, waiting for transfers between devices, exchange(): return lax.all_to_all(blocks, axis, split_axis=0, concat_axis=0, tiled=True)  33.9 us
    all_to_all x1, blocking collectives, exchange(): return lax.all_to_all(blocks, axis, split_axis=0, concat_axis=0, tiled=True)  29.8 us
    all_to_all x3, starting transfers between devices, exchange(): return lax.all_to_all(blocks, axis, split_axis=0, concat_axis=0, tiled=True)  25.6 us
    ppermute x18, starting transfers between devices, shift_along(): return lax.ppermute(block, 'batch', pairs)  17.3 us
    ppermute x3, starting transfers between devices, swap_cores(): return lax.ppermute(block, 'tensor', [(at, at ^ 1) for at in range(size)])  12.9 us
    ppermute x9, waiting for transfers between devices, shift_chips(): lax.ppermute(block, 'tensor', [(at, (at + 2 * count) % size) for at in ra...  9.99 us
    pallas_call x1, Pallas kernels, gate_up(): pl.pallas_call(functools.partial(gate_up_kernel, side, tile), out_shape=[...  7.95 us
  transfers between devices with their start and end apart: 35, of which 21 were waited for; matrix products, arithmetic and copies ran while one was open for 5% of the time, Pallas kernels for 3%

profile of v2, /device:TPU:1, one launch (start us, length us, event | category | flops | bytes accessed | tf_op | source)
XLA Modules:
  0.0 258.7 jit_solution(7542857101089810915)
XLA Ops:
  0.6 3.0 %copy.48 = bf16[2,12,16,16,128]{4,3,0,1,2:T(8,128)(2,1)} copy(bf16[2,12,16,16,128]{4,3,2,1,0:T(8,128)(2,1)} %bitcast.50) | data formatting | bytes 3145728 | tf_op jit(solution)/shard_map/cache_spread/reshape | solution.py:381
  3.6 8.7 %all-to-all-start = ((bf16[16,12,2,16,128]{4,3,2,1,0:T(8,128)(2,1)}), bf16[16,12,2,16,128]{4,3,2,1,0:T(8,128)(2,1)S(1)}, u32[]{:S(2)}, u32[]{:S(2)}) async-start(bf16[16,12,2,16,128]{4,3,2,1,0:T(8,128)(2,1)} %bitcast.47), calls=%async_computation | async-start | bytes 3145728 | tf_op jit(solution)/shard_map/cache_spread/all_to_all | solution.py:21
  14.7 3.3 %project_rows.1 = (bf16[96,1024]{1,0:T(8,128)(2,1)S(1)}, bf16[96,1024]{1,0:T(8,128)(2,1)}, bf16[96,1024]{1,0:T(8,128)(2,1)}, bf16[96,1024]{1,0:T(8,128)(2,1)}, b...) custom-call(s32[384,1]{1,0:T(8,128)S(1)} %fusion.13.order_ref, ...), custom_call_target="tpu_custom_call" | custom-call | flops 1207959552 | bytes 4718592 | tf_op jit(solution)/shard_map/project/project_rows/pallas_call | solution.py:214
  28.2 7.8 %collective-permute-done.3.refs_1_ = bf16[96,1024]{1,0:T(8,128)(2,1)S(1)} collective-permute-done((bf16[96,1024]{1,0:T(8,128)(2,1)}, bf16[96,1024]{1,0:T(8,128)(2,1)S(1)}, u32[]{:S(2)}, u32[]{:S(2)}) %collective-permute-start.3) | collective-permute-done | bytes 196640 | tf_op jit(solution)/shard_map/project/ppermute | solution.py:43
  37.6 2.9 %pick_rows.1 = bf16[384,2,16,128]{3,2,1,0:T(8,128)(2,1)} custom-call(s32[384]{0:T(512)S(1)} %reshape.582.index_ref, bf16[192,2,16,128]{3,2,1,0:T(8,128)(2,1)S(1)} %bitcast.43), custom_call_target="tpu_custom_call" | custom-call | bytes 4718592 | tf_op jit(solution)/shard_map/project/pick_rows/pallas_call | solution.py:333
  45.4 6.8 %all-to-all-start.1 = ((bf16[16,24,2,16,128]{4,3,2,1,0:T(8,128)(2,1)}), bf16[16,24,2,16,128]{4,3,2,1,0:T(8,128)(2,1)}, u32[]{:S(2)}, u32[]{:S(2)}) async-start(bf16[16,24,2,16,128]{4,3,2,1,0:T(8,128)(2,1)} %bitcast.8), calls=%async_computation.1 | async-start | bytes 6291456 | tf_op jit(solution)/shard_map/cache_return/all_to_all | solution.py:21
  55.4 7.8 %collective-permute-done.11 = bf16[24,1024]{1,0:T(8,128)(2,1)S(1)} collective-permute-done((bf16[24,1024]{1,0:T(8,128)(2,1)S(1)}, bf16[24,1024]{1,0:T(8,128)(2,1)S(1)}, u32[]{:S(2)}, u32[]{:S(2)}) %collective-permute-start.11) | collective-permute-done | bytes 49184 | tf_op jit(solution)/shard_map/project/ppermute | solution.py:43
  63.2 2.8 %collective-permute-done.10 = bf16[24,1024]{1,0:T(8,128)(2,1)S(1)} collective-permute-done((bf16[24,1024]{1,0:T(8,128)(2,1)S(1)}, bf16[24,1024]{1,0:T(8,128)(2,1)S(1)}, u32[]{:S(2)}, u32[]{:S(2)}) %collective-permute-start.10) | collective-permute-done | bytes 49184 | tf_op jit(solution)/shard_map/project/ppermute | solution.py:43
  67.3 21.0 %all-to-all-done.1 = bf16[16,24,2,16,128]{4,3,2,1,0:T(8,128)(2,1)} async-done(((bf16[16,24,2,16,128]{4,3,2,1,0:T(8,128)(2,1)}), bf16[16,24,2,16,128]{4,3,2,1,0:T(8,128)(2,1)}, u32[]{:S(2)}, u32[]{:S(2)}) %all-to-all-start.1) | async-done | bytes 3145760 | tf_op jit(solution)/shard_map/cache_return/all_to_all | solution.py:21
  92.4 4.3 %fusion.92 = (f32[24,12]{1,0:T(8,128)S(1)}, f32[24,12,258]{2,1,0:T(8,128)S(1)}) fusion(f32[24,12,2]{2,1,0:T(8,128)S(1)} %fusion.67, f32[24,12,256]{2,1,0:T(8,128)S(1)} %fusion.93, pred[24,258]{1,0:T(8,128)(4,1)S(1)} %iota_compare_fusion), kind=kOutput, calls=%fused_computation.192 | output fusion | flops 371777 | bytes 601776 | tf_op jit(solution)/shard_map/attention/sub | solution.py:462
  98.5 10.0 %all-to-all-start.2 = ((bf16[16,24,1536]{2,1,0:T(8,128)(2,1)}), bf16[16,24,1536]{2,1,0:T(8,128)(2,1)S(1)}, u32[]{:S(2)}, u32[]{:S(2)}) async-start(bf16[16,24,1536]{2,1,0:T(8,128)(2,1)} %broadcast_in_dim.28), calls=%async_computation.2 | async-start | bytes 2359296 | tf_op jit(solution)/shard_map/attention/all_to_all | solution.py:21
  108.6 12.8 %all-to-all-done.2 = bf16[16,24,1536]{2,1,0:T(8,128)(2,1)S(1)} async-done(((bf16[16,24,1536]{2,1,0:T(8,128)(2,1)}), bf16[16,24,1536]{2,1,0:T(8,128)(2,1)S(1)}, u32[]{:S(2)}, u32[]{:S(2)}) %all-to-all-start.2) | async-done | bytes 1179680 | tf_op jit(solution)/shard_map/attention/all_to_all | solution.py:21
  124.8 7.0 %collective-permute-start.12 = (f32[192,768]{1,0:T(8,128)}, f32[192,768]{1,0:T(8,128)S(1)}, u32[]{:S(2)}, u32[]{:S(2)}) collective-permute-start(f32[192,768]{1,0:T(8,128)} %get-tuple-element.79), channel_id=1, source_target_pairs={{0,1},{1,0},{2,3},{3,2},{4,5},{5,4},{6,7},{7,6},{8,9},{9,8},{10,11... | collective-permute-start | bytes 1769480 | tf_op jit(solution)/shard_map/output_projection/ppermute | solution.py:53
  149.8 3.0 %collective-permute-start.19 = (bf16[192,768]{1,0:T(8,128)(2,1)S(1)}, bf16[192,768]{1,0:T(8,128)(2,1)S(1)}, u32[]{:S(2)}, u32[]{:S(2)}) collective-permute-start(bf16[192,768]{1,0:T(8,128)(2,1)S(1)} %pad_maximum_fusion.near_ref), channel_id=1, source_target_pairs={{0,1},{1,0},{2,3},{3,2},{4,5},{5,4},{6,7},{7,6},{8,9},{9,8},{10,11... | collective-permute-start | bytes 884744 | tf_op jit(solution)/shard_map/output_projection/ppermute | solution.py:53
  154.0 8.0 %gate_up.1 = (bf16[4,96,2816]{2,1,0:T(8,128)(2,1)S(1)}, bf16[96,2688]{1,0:T(8,128)(2,1)S(1)}, bf16[96,2688]{1,0:T(8,128)(2,1)S(1)}, bf16[96,2688]{1,0:T(8,128)(2,1)S(1)}, bf16[96,2688]{1,0:T(8,128)(2,1)S(1)}) custom-call(s32[384,1]{1,0:T(8,128)S(1)} %fusion.29.order_ref, bf16[192,768]{1,0:T(8,128)(2,1)S(1)} %pad_maximum_fusion.near_ref, ...), custom_call_target="tpu_custom_call" | custom-call | flops 3170893824 | bytes 12386304 | tf_op jit(solution)/shard_map/gate_up/gate_up/pallas_call | solution.py:263
  164.9 3.6 %all-to-all-start.3 = ((bf16[4,96,2816]{2,1,0:T(8,128)(2,1)}), bf16[4,96,2816]{2,1,0:T(8,128)(2,1)S(1)}, u32[]{:S(2)}, u32[]{:S(2)}) async-start(bf16[4,96,2816]{2,1,0:T(8,128)(2,1)} %copy-done.1), calls=%async_computation.3 | async-start | bytes 4325376 | tf_op jit(solution)/shard_map/gate_up/all_to_all | solution.py:111
  170.1 11.7 %collective-permute-done.25 = bf16[96,2688]{1,0:T(8,128)(2,1)S(1)} collective-permute-done((bf16[96,2688]{1,0:T(8,128)(2,1)}, bf16[96,2688]{1,0:T(8,128)(2,1)S(1)}, u32[]{:S(2)}, u32[]{:S(2)}) %collective-permute-start.25) | collective-permute-done | bytes 516128 | tf_op jit(solution)/shard_map/gate_up/ppermute | solution.py:43
  183.7 12.0 %collective-permute-done.23 = bf16[96,2688]{1,0:T(8,128)(2,1)S(1)} collective-permute-done((bf16[96,2688]{1,0:T(8,128)(2,1)S(1)}, bf16[96,2688]{1,0:T(8,128)(2,1)S(1)}, u32[]{:S(2)}, u32[]{:S(2)}) %collective-permute-start.23) | collective-permute-done | bytes 516128 | tf_op jit(solution)/shard_map/gate_up/ppermute | solution.py:43
  196.8 4.1 %all-to-all-start.4 = ((bf16[4,24,2688]{2,1,0:T(8,128)(2,1)}), bf16[4,24,2688]{2,1,0:T(8,128)(2,1)S(1)}, u32[]{:S(2)}, u32[]{:S(2)}) async-start(bf16[4,24,2688]{2,1,0:T(8,128)(2,1)} %bitcast.17), calls=%async_computation.4 | async-start | bytes 1032192 | tf_op jit(solution)/shard_map/gate_up/all_to_all | solution.py:111
  202.8 6.8 %all-to-all-done.4 = bf16[4,24,2688]{2,1,0:T(8,128)(2,1)S(1)} async-done(((bf16[4,24,2688]{2,1,0:T(8,128)(2,1)}), bf16[4,24,2688]{2,1,0:T(8,128)(2,1)S(1)}, u32[]{:S(2)}, u32[]{:S(2)}) %all-to-all-start.4) | async-done | bytes 516128 | tf_op jit(solution)/shard_map/gate_up/all_to_all | solution.py:111
  211.4 29.8 %all_to_all.30 = bf16[16,24,2688]{2,1,0:T(8,128)(2,1)S(1)} all-to-all(bf16[16,24,2688]{2,1,0:T(8,128)(2,1)S(1)} %broadcast_in_dim.29), channel_id=1, replica_groups=mesh['batch'=16,'tensor'=8] {'batch'}, dimensions={0} | all-to-all | bytes 4128768 | tf_op jit(solution)/shard_map/gate_up/all_to_all | solution.py:21
  241.2 4.1 %spread_dot.3 = (f32[192,768]{1,0:T(8,128)S(1)}, f32[192,768]{1,0:T(8,128)S(1)}) custom-call(s32[16]{0:T(128)S(1)} %fusion.80.place_ref, bf16[384,2688]{1,0:T(8,128)(2,1)S(1)} %bitcast.42, bf16[2688,768]{1,0:T(8,128)(2,1)} %weight_ref.5), custom_call_target="tpu_custom_call" | custom-call | flops 1585446912 | bytes 8552448 | tf_op jit(solution)/shard_map/down_projection/spread_dot/pallas_call | solution.py:294
  245.3 2.9 %collective-permute-start.26 = (f32[192,768]{1,0:T(8,128)S(1)}, f32[192,768]{1,0:T(8,128)S(1)}, u32[]{:S(2)}, u32[]{:S(2)}) collective-permute-start(f32[192,768]{1,0:T(8,128)S(1)} %get-tuple-element.94), channel_id=1, source_target_pairs={{0,1},{1,0},{2,3},{3,2},{4,5},{5,4},{6,7},{7,6},{8,9},{9,8},{10,11... | collective-permute-start | bytes 1769480 | tf_op jit(solution)/shard_map/down_projection/ppermute | solution.py:53
  252.5 2.8 %copy.36 = bf16[2,24,16,16,128]{4,3,2,1,0:T(8,128)(2,1)S(1)} copy(bf16[2,24,16,16,128]{4,3,0,1,2:T(8,128)(2,1)} %bitcast.9) | data formatting | bytes 6291456 | tf_op jit(solution)/shard_map/cache_return/transpose | solution.py:419
  (174 shorter events, 70.3 us)
Async XLA Ops:
  3.6 34.0 %all-to-all-start = ((bf16[16,12,2,16,128]{4,3,2,1,0:T(8,128)(2,1)}), bf16[16,12,2,16,128]{4,3,2,1,0:T(8,128)(2,1)S(1)}, u32[]{:S(2)}, u32[]{:S(2)}) async-start(bf16[16,12,2,16,128]{4,3,2,1,0:T(8,128)(2,1)} %bitcast.47), calls=%async_computation | async-start | bytes 3145728 | tf_op jit(solution)/shard_map/cache_spread/all_to_all | solution.py:21
  18.0 22.5 %collective-permute-start = (bf16[96,1024]{1,0:T(8,128)(2,1)}, bf16[96,1024]{1,0:T(8,128)(2,1)S(1)}, u32[]{:S(2)}, u32[]{:S(2)}) collective-permute-start(bf16[96,1024]{1,0:T(8,128)(2,1)} %get-tuple-element.53), channel_id=1, source_target_pairs={{0,8},{8,16},{16,24},{24,0},{32,40},{40,48},{48,56},{56,32},{64,72... | collective-permute-start | bytes 589832 | tf_op jit(solution)/shard_map/project/ppermute | solution.py:43
  19.4 22.6 %collective-permute-start.1 = (bf16[96,1024]{1,0:T(8,128)(2,1)}, bf16[96,1024]{1,0:T(8,128)(2,1)S(1)}, u32[]{:S(2)}, u32[]{:S(2)}) collective-permute-start(bf16[96,1024]{1,0:T(8,128)(2,1)} %get-tuple-element.54), channel_id=1, source_target_pairs={{0,16},{8,24},{16,0},{24,8},{32,48},{40,56},{48,32},{56,40},{64,80... | collective-permute-start | bytes 589832 | tf_op jit(solution)/shard_map/project/ppermute | solution.py:43
  21.8 20.9 %collective-permute-start.2 = (bf16[96,1024]{1,0:T(8,128)(2,1)}, bf16[96,1024]{1,0:T(8,128)(2,1)S(1)}, u32[]{:S(2)}, u32[]{:S(2)}) collective-permute-start(bf16[96,1024]{1,0:T(8,128)(2,1)} %get-tuple-element.55), channel_id=1, source_target_pairs={{0,24},{8,0},{16,8},{24,16},{32,56},{40,32},{48,40},{56,48},{64,88... | collective-permute-start | bytes 589832 | tf_op jit(solution)/shard_map/project/ppermute | solution.py:43
  22.9 13.0 %collective-permute-start.3 = (bf16[96,1024]{1,0:T(8,128)(2,1)}, bf16[96,1024]{1,0:T(8,128)(2,1)S(1)}, u32[]{:S(2)}, u32[]{:S(2)}) collective-permute-start(bf16[96,1024]{1,0:T(8,128)(2,1)} %get-tuple-element.57), channel_id=1, source_target_pairs={{0,32},{8,40},{16,48},{24,56},{32,64},{40,72},{48,80},{56,88},{64,... | collective-permute-start | bytes 589832 | tf_op jit(solution)/shard_map/project/ppermute | solution.py:43
  24.1 18.5 %collective-permute-start.5 = (bf16[96,1024]{1,0:T(8,128)(2,1)S(1)}, bf16[96,1024]{1,0:T(8,128)(2,1)S(1)}, u32[]{:S(2)}, u32[]{:S(2)}) collective-permute-start(bf16[96,1024]{1,0:T(8,128)(2,1)S(1)} %get-tuple-element.60), channel_id=1, source_target_pairs={{0,96},{8,104},{16,112},{24,120},{32,0},{40,8},{48,16},{56,24},{64... | collective-permute-start | bytes 589832 | tf_op jit(solution)/shard_map/project/ppermute | solution.py:43
  42.7 12.1 %collective-permute-start.9 = (bf16[24,1024]{1,0:T(8,128)(2,1)S(1)}, bf16[24,1024]{1,0:T(8,128)(2,1)S(1)}, u32[]{:S(2)}, u32[]{:S(2)}) collective-permute-start(bf16[24,1024]{1,0:T(8,128)(2,1)S(1)} %get-tuple-element.74), channel_id=1, source_target_pairs={{0,8},{8,16},{16,24},{24,0},{32,40},{40,48},{48,56},{56,32},{64,72... | collective-permute-start | bytes 147464 | tf_op jit(solution)/shard_map/project/ppermute | solution.py:43
  43.5 12.0 %collective-permute-start.8 = (bf16[24,1024]{1,0:T(8,128)(2,1)S(1)}, bf16[24,1024]{1,0:T(8,128)(2,1)S(1)}, u32[]{:S(2)}, u32[]{:S(2)}) collective-permute-start(bf16[24,1024]{1,0:T(8,128)(2,1)S(1)} %get-tuple-element.68), channel_id=1, source_target_pairs={{0,96},{8,104},{16,112},{24,120},{32,0},{40,8},{48,16},{56,24},{64... | collective-permute-start | bytes 147464 | tf_op jit(solution)/shard_map/project/ppermute | solution.py:43
  44.7 10.7 %collective-permute-start.7 = (bf16[24,1024]{1,0:T(8,128)(2,1)S(1)}, bf16[24,1024]{1,0:T(8,128)(2,1)S(1)}, u32[]{:S(2)}, u32[]{:S(2)}) collective-permute-start(bf16[24,1024]{1,0:T(8,128)(2,1)S(1)} %get-tuple-element.67), channel_id=1, source_target_pairs={{0,64},{8,72},{16,80},{24,88},{32,96},{40,104},{48,112},{56,120},{... | collective-permute-start | bytes 147464 | tf_op jit(solution)/shard_map/project/ppermute | solution.py:43
  44.7 10.7 %collective-permute-start.6 = (bf16[24,1024]{1,0:T(8,128)(2,1)S(1)}, bf16[24,1024]{1,0:T(8,128)(2,1)S(1)}, u32[]{:S(2)}, u32[]{:S(2)}) collective-permute-start(bf16[24,1024]{1,0:T(8,128)(2,1)S(1)} %get-tuple-element.66), channel_id=1, source_target_pairs={{0,32},{8,40},{16,48},{24,56},{32,64},{40,72},{48,80},{56,88},{64,... | collective-permute-start | bytes 147464 | tf_op jit(solution)/shard_map/project/ppermute | solution.py:43
  45.4 43.0 %all-to-all-start.1 = ((bf16[16,24,2,16,128]{4,3,2,1,0:T(8,128)(2,1)}), bf16[16,24,2,16,128]{4,3,2,1,0:T(8,128)(2,1)}, u32[]{:S(2)}, u32[]{:S(2)}) async-start(bf16[16,24,2,16,128]{4,3,2,1,0:T(8,128)(2,1)} %bitcast.8), calls=%async_computation.1 | async-start | bytes 6291456 | tf_op jit(solution)/shard_map/cache_return/all_to_all | solution.py:21
  52.2 11.0 %collective-permute-start.11 = (bf16[24,1024]{1,0:T(8,128)(2,1)S(1)}, bf16[24,1024]{1,0:T(8,128)(2,1)S(1)}, u32[]{:S(2)}, u32[]{:S(2)}) collective-permute-start(bf16[24,1024]{1,0:T(8,128)(2,1)S(1)} %get-tuple-element.77), channel_id=1, source_target_pairs={{0,24},{8,0},{16,8},{24,16},{32,56},{40,32},{48,40},{56,48},{64,88... | collective-permute-start | bytes 147464 | tf_op jit(solution)/shard_map/project/ppermute | solution.py:43
  54.8 11.2 %collective-permute-start.10 = (bf16[24,1024]{1,0:T(8,128)(2,1)S(1)}, bf16[24,1024]{1,0:T(8,128)(2,1)S(1)}, u32[]{:S(2)}, u32[]{:S(2)}) collective-permute-start(bf16[24,1024]{1,0:T(8,128)(2,1)S(1)} %get-tuple-element.76), channel_id=1, source_target_pairs={{0,16},{8,24},{16,0},{24,8},{32,48},{40,56},{48,32},{56,40},{64,80... | collective-permute-start | bytes 147464 | tf_op jit(solution)/shard_map/project/ppermute | solution.py:43
  98.5 22.9 %all-to-all-start.2 = ((bf16[16,24,1536]{2,1,0:T(8,128)(2,1)}), bf16[16,24,1536]{2,1,0:T(8,128)(2,1)S(1)}, u32[]{:S(2)}, u32[]{:S(2)}) async-start(bf16[16,24,1536]{2,1,0:T(8,128)(2,1)} %broadcast_in_dim.28), calls=%async_computation.2 | async-start | bytes 2359296 | tf_op jit(solution)/shard_map/attention/all_to_all | solution.py:21
  124.8 8.8 %collective-permute-start.12 = (f32[192,768]{1,0:T(8,128)}, f32[192,768]{1,0:T(8,128)S(1)}, u32[]{:S(2)}, u32[]{:S(2)}) collective-permute-start(f32[192,768]{1,0:T(8,128)} %get-tuple-element.79), channel_id=1, source_target_pairs={{0,1},{1,0},{2,3},{3,2},{4,5},{5,4},{6,7},{7,6},{8,9},{9,8},{10,11... | collective-permute-start | bytes 1769480 | tf_op jit(solution)/shard_map/output_projection/ppermute | solution.py:53
  164.9 31.9 %all-to-all-start.3 = ((bf16[4,96,2816]{2,1,0:T(8,128)(2,1)}), bf16[4,96,2816]{2,1,0:T(8,128)(2,1)S(1)}, u32[]{:S(2)}, u32[]{:S(2)}) async-start(bf16[4,96,2816]{2,1,0:T(8,128)(2,1)} %copy-done.1), calls=%async_computation.3 | async-start | bytes 4325376 | tf_op jit(solution)/shard_map/gate_up/all_to_all | solution.py:111
  168.5 13.2 %collective-permute-start.25 = (bf16[96,2688]{1,0:T(8,128)(2,1)}, bf16[96,2688]{1,0:T(8,128)(2,1)S(1)}, u32[]{:S(2)}, u32[]{:S(2)}) collective-permute-start(bf16[96,2688]{1,0:T(8,128)(2,1)} %copy-done.7), channel_id=1, source_target_pairs={{0,96},{8,104},{16,112},{24,120},{32,0},{40,8},{48,16},{56,24},{64... | collective-permute-start | bytes 1548296 | tf_op jit(solution)/shard_map/gate_up/ppermute | solution.py:43
  169.3 14.4 %collective-permute-start.24 = (bf16[96,2688]{1,0:T(8,128)(2,1)}, bf16[96,2688]{1,0:T(8,128)(2,1)S(1)}, u32[]{:S(2)}, u32[]{:S(2)}) collective-permute-start(bf16[96,2688]{1,0:T(8,128)(2,1)} %copy-done.6), channel_id=1, source_target_pairs={{0,64},{8,72},{16,80},{24,88},{32,96},{40,104},{48,112},{56,120},{... | collective-permute-start | bytes 1548296 | tf_op jit(solution)/shard_map/gate_up/ppermute | solution.py:43
  170.0 25.8 %collective-permute-start.23 = (bf16[96,2688]{1,0:T(8,128)(2,1)S(1)}, bf16[96,2688]{1,0:T(8,128)(2,1)S(1)}, u32[]{:S(2)}, u32[]{:S(2)}) collective-permute-start(bf16[96,2688]{1,0:T(8,128)(2,1)S(1)} %get-tuple-element.90), channel_id=1, source_target_pairs={{0,32},{8,40},{16,48},{24,56},{32,64},{40,72},{48,80},{56,88},{64,... | collective-permute-start | bytes 1548296 | tf_op jit(solution)/shard_map/gate_up/ppermute | solution.py:43
  196.8 12.8 %all-to-all-start.4 = ((bf16[4,24,2688]{2,1,0:T(8,128)(2,1)}), bf16[4,24,2688]{2,1,0:T(8,128)(2,1)S(1)}, u32[]{:S(2)}, u32[]{:S(2)}) async-start(bf16[4,24,2688]{2,1,0:T(8,128)(2,1)} %bitcast.17), calls=%async_computation.4 | async-start | bytes 1032192 | tf_op jit(solution)/shard_map/gate_up/all_to_all | solution.py:111
  201.2 8.5 %collective-permute-start.22 = (bf16[24,2816]{1,0:T(8,128)(2,1)S(1)}, bf16[24,2816]{1,0:T(8,128)(2,1)S(1)}, u32[]{:S(2)}, u32[]{:S(2)}) collective-permute-start(bf16[24,2816]{1,0:T(8,128)(2,1)S(1)} %get-tuple-element.88), channel_id=1, source_target_pairs={{0,96},{8,104},{16,112},{24,120},{32,0},{40,8},{48,16},{56,24},{64... | collective-permute-start | bytes 405512 | tf_op jit(solution)/shard_map/gate_up/ppermute | solution.py:43
  201.3 8.4 %collective-permute-start.21 = (bf16[24,2816]{1,0:T(8,128)(2,1)S(1)}, bf16[24,2816]{1,0:T(8,128)(2,1)S(1)}, u32[]{:S(2)}, u32[]{:S(2)}) collective-permute-start(bf16[24,2816]{1,0:T(8,128)(2,1)S(1)} %get-tuple-element.87), channel_id=1, source_target_pairs={{0,64},{8,72},{16,80},{24,88},{32,96},{40,104},{48,112},{56,120},{... | collective-permute-start | bytes 405512 | tf_op jit(solution)/shard_map/gate_up/ppermute | solution.py:43
  202.1 8.8 %collective-permute-start.20 = (bf16[24,2816]{1,0:T(8,128)(2,1)S(1)}, bf16[24,2816]{1,0:T(8,128)(2,1)S(1)}, u32[]{:S(2)}, u32[]{:S(2)}) collective-permute-start(bf16[24,2816]{1,0:T(8,128)(2,1)S(1)} %get-tuple-element.86), channel_id=1, source_target_pairs={{0,32},{8,40},{16,48},{24,56},{32,64},{40,72},{48,80},{56,88},{64,... | collective-permute-start | bytes 405512 | tf_op jit(solution)/shard_map/gate_up/ppermute | solution.py:43
  249.9 6.7 %collective-permute-start.29 = (bf16[48,768]{1,0:T(8,128)(2,1)S(1)}, bf16[48,768]{1,0:T(8,128)(2,1)S(1)}, u32[]{:S(2)}, u32[]{:S(2)}) collective-permute-start(bf16[48,768]{1,0:T(8,128)(2,1)S(1)} %get-tuple-element.98), channel_id=1, source_target_pairs={{0,6},{1,7},{2,0},{3,1},{4,2},{5,3},{6,4},{7,5},{8,14},{9,15},{10,... | collective-permute-start | bytes 221192 | tf_op jit(solution)/shard_map/down_projection/ppermute | solution.py:48
  (32 other events, 260.8 us)

commit v3 on v2

--- a/solution.py
+++ b/solution.py
@@ -3,6 +3,7 @@
 
 import jax
 import jax.numpy as jnp
+import numpy as np
 from jax import lax
 from jax.experimental import pallas as pl
 from jax.experimental.pallas import tpu as pltpu
@@ -51,21 +52,6 @@
 def swap_cores(block):
     size = lax.axis_size("tensor")
     return lax.ppermute(block, "tensor", [(at, at ^ 1) for at in range(size)])
-
-
-def shift_both(first, second, first_minor):
-    side = len(first)
-    middle = side // 2
-    others = [count for count in range(1, side) if count != middle]
-    first_moved, second_moved = {0: first[0]}, {0: second[0]}
-    for count in others + [middle]:
-        first_moved[count] = shift_along(first[count], first_minor, count)
-    for count in others:
-        second_moved[count] = shift_along(second[count], 1 - first_minor, count)
-    second_moved[middle] = shift_along(
-        after(second[middle], second_moved[1]), 1 - first_minor, middle
-    )
-    return [first_moved[at] for at in range(side)], [second_moved[at] for at in range(side)]
 
 
 def fold_kernel(count, *refs):
@@ -96,15 +82,6 @@
     )(*sources)
 
 
-def add_over_batch(first, second, earlier):
-    side = len(first)
-    first, second = shift_both(first, second, 1)
-    first, second = after((first, second), earlier)
-    first, second = fold(first, side), fold(second, side)
-    first, second = shift_both(first, second, 0)
-    return [functools.reduce(lambda a, b: a + b.astype(jnp.float32), own) for own in (first, second)]
-
-
 def exchange_minor(blocks):
     side = math.isqrt(lax.axis_size("batch"))
     groups = [[major * side + minor for minor in range(side)] for major in range(side)]
@@ -172,7 +149,7 @@
 
 
 def project_kernel(
-    side, order_ref, parent_ref, input_ref, gain_ref, query_ref, keyval_ref, *out_refs
+    order_ref, parent_ref, input_ref, gain_ref, query_ref, keyval_ref, out_ref
 ):
     steps, count, width = input_ref.shape
     source = input_ref[...].reshape(steps * count, width)
@@ -197,25 +174,29 @@
         ],
         axis=1,
     ).astype(jnp.float32)
-    half = values.shape[1] // 2
-    rows = values.shape[0] // side
-    for place in range(side):
-        out_refs[place][...] = blocks_along(values[:, :half], side, place).astype(jnp.bfloat16)
-        out_refs[side + place][...] = values[place * rows : (place + 1) * rows, half:].astype(
-            jnp.bfloat16
-        )
-
-
-def project_rows(side, order, parents, layer_input, gain, query_weight, keyval_weight):
+    blocks, held, _ = out_ref.shape
+    rows = values.shape[0] // blocks
+    for block in range(blocks):
+        part = values[block * rows : (block + 1) * rows]
+        for at in range(held // (2 * rows)):
+            pair = [
+                part[:, (2 * at + side) * LANES : (2 * at + side + 1) * LANES] for side in range(2)
+            ]
+            out_ref[block, 2 * at * rows : 2 * (at + 1) * rows] = jnp.concatenate(
+                pair, axis=0
+            ).astype(jnp.bfloat16)
+
+
+def project_rows(batches, order, parents, layer_input, gain, query_weight, keyval_weight):
     total = order.shape[0]
     columns = query_weight.shape[1] + 3 * keyval_weight.shape[2] + LANES
-    block = jax.ShapeDtypeStruct((total // side, columns // 2), jnp.bfloat16)
+    held = total // batches * columns // LANES
     whole = pl.BlockSpec(memory_space=pltpu.VMEM)
     return pl.pallas_call(
-        functools.partial(project_kernel, side),
-        out_shape=[block] * (2 * side),
+        project_kernel,
+        out_shape=jax.ShapeDtypeStruct((batches, held, LANES), jnp.bfloat16),
         in_specs=[whole] * 6,
-        out_specs=[whole] * (2 * side),
+        out_specs=whole,
         compiler_params=pltpu.CompilerParams(vmem_limit_bytes=48 * MIB),
         cost_estimate=pl.CostEstimate(
             flops=2 * total * columns * gain.shape[0],
@@ -226,46 +207,83 @@
     )(order, parents, layer_input, gain.reshape(1, -1), query_weight, keyval_weight)
 
 
-def gate_up_kernel(side, tile, order_ref, near_ref, far_ref, gain_ref, weight_ref, *out_refs):
-    first_ref, second_refs = out_refs[0], out_refs[1:]
+def gate_up_kernel(side, spans, order_ref, near_ref, far_ref, gain_ref, weight_ref, *refs):
+    first_ref, second_refs = refs[0], refs[1 : 1 + side]
+    held_ref, first_held, second_held, in_sems, first_sems, second_sems = refs[1 + side :]
+    hidden = weight_ref.shape[2]
+    loads = {}
+    for half in (1, 0):
+        for at, (start, size) in enumerate(spans):
+            columns = pl.ds(start, size)
+            loads[half, at] = pltpu.make_async_copy(
+                weight_ref.at[half, :, columns],
+                held_ref.at[half, :, columns],
+                in_sems.at[half, at],
+            )
+            loads[half, at].start()
     lifted = jnp.concatenate([near_ref[...], far_ref[...]], axis=0)
     ordered = dot(one_hot(order_ref[...], lifted.shape[0]), lifted)
     plain = ordered * (1.0 / gain_ref[...].astype(jnp.float32))
     statistics = in_lanes(split_pair(jnp.sum(plain * plain, axis=1, keepdims=True)))
     ordered = ordered.astype(jnp.bfloat16)
-    hidden = weight_ref.shape[2]
     rows = ordered.shape[0] // side
+    stores = []
+    for at, (start, size) in enumerate(spans):
+        loads[1, at].wait()
+        ups = dot(ordered, held_ref[1, :, start : start + size])
+        for place in range(side):
+            second_held[place, :, start : start + size] = ups[
+                place * rows : (place + 1) * rows
+            ].astype(jnp.bfloat16)
     for place in range(side):
-        first_ref[place, :, hidden:] = blocks_along(statistics, side, place).astype(jnp.bfloat16)
-
-    def one_tile(columns):
-        gates = dot(ordered, weight_ref[0, :, columns])
+        stores.append(
+            pltpu.make_async_copy(
+                second_held.at[place], second_refs[place], second_sems.at[place]
+            )
+        )
+        stores[-1].start()
+    for at, (start, size) in enumerate(list(spans) + [(hidden, LANES)]):
+        if start < hidden:
+            loads[0, at].wait()
+            gates = dot(ordered, held_ref[0, :, start : start + size])
+        else:
+            gates = statistics
         for place in range(side):
-            first_ref[place, :, columns] = blocks_along(gates, side, place).astype(jnp.bfloat16)
-        ups = dot(ordered, weight_ref[1, :, columns])
-        for place in range(side):
-            second_refs[place][:, columns] = ups[place * rows : (place + 1) * rows].astype(
+            first_held[place, :, start : start + size] = blocks_along(gates, side, place).astype(
                 jnp.bfloat16
             )
-
-    @pl.loop(0, hidden // tile)
-    def _(step):
-        one_tile(pl.ds(pl.multiple_of(step * tile, LANES), tile))
-
-    if hidden % tile:
-        one_tile(pl.ds(hidden // tile * tile, hidden % tile))
+        columns = pl.ds(start, size)
+        stores.append(
+            pltpu.make_async_copy(
+                first_held.at[:, :, columns], first_ref.at[:, :, columns], first_sems.at[at]
+            )
+        )
+        stores[-1].start()
+    for store in stores:
+        store.wait()
 
 
 def gate_up(side, order, near, far, gain, weight, tile):
     total, width = order.shape[0], near.shape[1]
     hidden = weight.shape[2]
+    rows = total // side
+    spans = [(start, min(tile, hidden - start)) for start in range(0, hidden, tile)]
     whole = pl.BlockSpec(memory_space=pltpu.VMEM)
+    far_off = pl.BlockSpec(memory_space=pltpu.HBM)
     return pl.pallas_call(
-        functools.partial(gate_up_kernel, side, tile),
-        out_shape=[jax.ShapeDtypeStruct((side, total // side, hidden + LANES), jnp.bfloat16)]
-        + [jax.ShapeDtypeStruct((total // side, hidden), jnp.bfloat16)] * side,
-        in_specs=[whole] * 5,
-        out_specs=[whole] * (1 + side),
+        functools.partial(gate_up_kernel, side, spans),
+        out_shape=[jax.ShapeDtypeStruct((side, rows, hidden + LANES), jnp.bfloat16)]
+        + [jax.ShapeDtypeStruct((rows, hidden), jnp.bfloat16)] * side,
+        in_specs=[whole] * 4 + [far_off],
+        out_specs=[far_off] * (1 + side),
+        scratch_shapes=[
+            pltpu.VMEM(weight.shape, jnp.bfloat16),
+            pltpu.VMEM((side, rows, hidden + LANES), jnp.bfloat16),
+            pltpu.VMEM((side, rows, hidden), jnp.bfloat16),
+            pltpu.SemaphoreType.DMA((2, len(spans))),
+            pltpu.SemaphoreType.DMA((len(spans) + 1,)),
+            pltpu.SemaphoreType.DMA((side,)),
+        ],
         compiler_params=pltpu.CompilerParams(vmem_limit_bytes=48 * MIB),
         cost_estimate=pl.CostEstimate(
             flops=4 * total * width * hidden,
@@ -297,7 +315,7 @@
         in_specs=[pl.BlockSpec(memory_space=pltpu.SMEM), whole, whole],
         out_specs=[whole] * 2,
         scratch_shapes=[pltpu.VMEM((total, width), jnp.float32)],
-        compiler_params=pltpu.CompilerParams(vmem_limit_bytes=48 * MIB),
+        compiler_params=pltpu.CompilerParams(vmem_limit_bytes=20 * MIB),
         cost_estimate=pl.CostEstimate(
             flops=2 * total * weight.size,
             bytes_accessed=2 * weight.size + 2 * total * (weight.shape[0] + 4 * width),
@@ -307,43 +325,158 @@
     )(places, values, weight)
 
 
-def rotary(steps, first_position):
-    inverse = jnp.exp(
-        -math.log(rope_base) * jnp.arange(HD // 2, dtype=jnp.float32) * (2.0 / HD)
+def rotary(rows, first_position):
+    inverse = np.exp(-math.log(rope_base) * np.arange(HD // 2, dtype=np.float64) * (2.0 / HD))
+    angles = (first_position + np.repeat(np.arange(STEPS), rows))[:, None] * inverse[None, :]
+    cosine, sine = np.cos(angles), np.sin(angles)
+    return np.concatenate([cosine, cosine, -sine, sine], axis=1).astype(np.float32)
+
+
+def attend_kernel(heads, rows, model, table_ref, cache_ref, *refs):
+    out_ref, fresh_ref, kept_ref, query_ref, mix_ref, semaphores = refs
+    total = STEPS * rows
+    batches, span = kept_ref.shape[2:4]
+    edge = (heads + 3) * HD
+    stores = []
+    for row in range(rows):
+        for at in range(2):
+            stores.append(
+                pltpu.make_async_copy(
+                    cache_ref.at[:, pl.ds((2 * (rows + row) + at) * span, span)],
+                    kept_ref.at[at, row],
+                    semaphores.at[at, row],
+                )
+            )
+            stores[-1].start()
+    parts = []
+    for start in range(2 * total * span, cache_ref.shape[1], 2 * total):
+        pair = cache_ref[0, start : start + 2 * total].astype(jnp.float32)
+        for source in range(1, batches):
+            pair = pair + cache_ref[source, start : start + 2 * total].astype(jnp.float32)
+        parts += [pair[:total], pair[total:]]
+    values = jnp.concatenate(parts, axis=1)
+    cosine, sine = table_ref[:, :HD], table_ref[:, HD:]
+    scale = lax.rsqrt((values[:, edge : edge + 1] + values[:, edge + 1 : edge + 2]) / model + norm_eps)
+    parent_scale = lax.rsqrt(
+        (values[:, edge + 2 : edge + 3] + values[:, edge + 3 : edge + 4]) / model + norm_eps
     )
-    angles = (first_position + steps).astype(jnp.float32)[:, None] * inverse[None, :]
-    cosine, sine = jnp.cos(angles), jnp.sin(angles)
-    return jnp.concatenate([cosine, cosine], axis=1), jnp.concatenate([-sine, sine], axis=1)
-
-
-def rotate(heads, cosine, sine):
-    swapped = jnp.concatenate([heads[..., HD // 2 :], heads[..., : HD // 2]], axis=-1)
-    return heads * cosine + swapped * sine
-
-
-def pick_kernel(index_ref, table_ref, out_ref):
-    def body(row, carry):
-        out_ref[row] = table_ref[index_ref[row]]
-        return carry
-
-    lax.fori_loop(0, out_ref.shape[0], body, 0, unroll=8)
-
-
-def pick_rows(table, index):
+
+    def rotate(block, cosine, sine):
+        return block * cosine + pltpu.roll(block, HD // 2, 1) * sine
+
+    def rounded(block):
+        return block.astype(jnp.bfloat16).astype(jnp.float32)
+
+    query_ref[...] = jnp.zeros(query_ref.shape, jnp.float32)
+    for head in range(heads):
+        block = values[:, head * HD : (head + 1) * HD] * scale
+        query_ref[:, head, :] = rotate(block, cosine, sine)
+    keys = rounded(rotate(values[:, heads * HD : (heads + 1) * HD] * scale, cosine, sine))
+    news = rounded(values[:, (heads + 1) * HD : (heads + 2) * HD] * scale)
+    parents = values[:, (heads + 2) * HD : edge] * parent_scale
+    parent_keys = rounded(rotate(parents[:rows], cosine[:rows], sine[:rows]))
+    parent_news = rounded(parents[rows:])
+    fresh_ref[0] = jnp.concatenate([keys[:rows], parent_keys], axis=0)
+    fresh_ref[1] = keys
+    fresh_ref[2] = jnp.concatenate([news[:rows], parent_news], axis=0)
+    fresh_ref[3] = news
+    queries = query_ref[...].astype(jnp.bfloat16)
+    wide = queries.astype(jnp.float32)
+    scores = jnp.concatenate(
+        [
+            lax.dot_general(
+                queries[row],
+                cache_ref[:, 2 * row * span : (2 * row + 1) * span].reshape(-1, HD),
+                (((1,), (1,)), ((), ())),
+                preferred_element_type=jnp.float32,
+            )
+            for row in range(total)
+        ],
+        axis=0,
+    ).reshape(total, queries.shape[1], -1) * (1.0 / math.sqrt(HD))
+    extra = [
+        jnp.sum(wide * fresh_ref[at][:, None, :], axis=2, keepdims=True) * (1.0 / math.sqrt(HD))
+        for at in range(STEPS)
+    ]
+    later = lax.broadcasted_iota(jnp.int32, extra[1].shape, 0) >= rows
+    extra[1] = jnp.where(later, extra[1], -jnp.inf)
+    top = jnp.maximum(
+        jnp.max(scores, axis=2, keepdims=True), jnp.maximum(extra[0], extra[1])
+    )
+    weights = jnp.exp(scores - top)
+    extra = [jnp.exp(score - top) for score in extra]
+    whole = jnp.sum(weights, axis=2, keepdims=True) + extra[0] + extra[1]
+    weights = (weights / whole).astype(jnp.bfloat16)
+    extra = [rounded(weight / whole) for weight in extra]
+    for row in range(total):
+        mix_ref[row] = dot(weights[row], cache_ref[:, (2 * row + 1) * span : (2 * row + 2) * span].reshape(-1, HD))
+    mix_ref[...] = (
+        mix_ref[...]
+        + extra[0] * fresh_ref[2][:, None, :]
+        + extra[1] * fresh_ref[3][:, None, :]
+    )
+    for head in range(heads):
+        block = mix_ref[:, head, :].astype(jnp.bfloat16)
+        for copy in range(out_ref.shape[0]):
+            out_ref[copy, :, head * HD : (head + 1) * HD] = block
+    for store in stores:
+        store.wait()
+
+
+def attend(returned, heads, rows, past, model):
+    batches, total = returned.shape[0], STEPS * rows
+    padded = -(-heads // 8) * 8
+    whole = pl.BlockSpec(memory_space=pltpu.VMEM)
+    return pl.pallas_call(
+        functools.partial(attend_kernel, heads, rows, model),
+        out_shape=[
+            jax.ShapeDtypeStruct((batches, total, heads * HD), jnp.bfloat16),
+            jax.ShapeDtypeStruct((2 * STEPS, total, HD), jnp.float32),
+            jax.ShapeDtypeStruct((2, rows, batches, past // batches, HD), jnp.bfloat16),
+        ],
+        grid=(1,),
+        in_specs=[whole, pl.BlockSpec(returned.shape, lambda step: (0, 0, 0))],
+        out_specs=[whole] * 2 + [pl.BlockSpec(memory_space=pl.ANY)],
+        scratch_shapes=[pltpu.VMEM((total, padded, HD), jnp.float32)] * 2
+        + [pltpu.SemaphoreType.DMA((2, rows))],
+        compiler_params=pltpu.CompilerParams(vmem_limit_bytes=48 * MIB),
+        cost_estimate=pl.CostEstimate(
+            flops=4 * total * padded * past * HD,
+            bytes_accessed=4 * returned.size,
+            transcendentals=total * padded * past,
+        ),
+        name="attend",
+    )(jnp.asarray(rotary(rows, past)), returned)
+
+
+def pick_kernel(index_ref, table_ref, sum_ref, out_ref):
+    span = table_ref.shape[1]
+    count = index_ref.shape[0] // out_ref.shape[0]
+
+    @pl.loop(0, out_ref.shape[0])
+    def _(block):
+        for row in range(count):
+            out_ref[block, row * span : (row + 1) * span] = table_ref[
+                index_ref[block * count + row]
+            ]
+        out_ref[block, count * span :] = sum_ref[block]
+
+
+def pick_rows(table, index, sums):
+    batches, held, _ = sums.shape
+    count = index.shape[0] // batches * table.shape[1]
+    whole = pl.BlockSpec(memory_space=pltpu.VMEM)
     return pl.pallas_call(
         pick_kernel,
-        out_shape=jax.ShapeDtypeStruct((index.shape[0],) + table.shape[1:], table.dtype),
-        in_specs=[
-            pl.BlockSpec(memory_space=pltpu.SMEM),
-            pl.BlockSpec(memory_space=pltpu.VMEM),
-        ],
-        out_specs=pl.BlockSpec(memory_space=pltpu.VMEM),
+        out_shape=jax.ShapeDtypeStruct((batches, count + held, LANES), table.dtype),
+        in_specs=[pl.BlockSpec(memory_space=pltpu.SMEM), whole, whole],
+        out_specs=whole,
         compiler_params=pltpu.CompilerParams(vmem_limit_bytes=32 * MIB),
         cost_estimate=pl.CostEstimate(
-            flops=0, bytes_accessed=3 * index.shape[0] * table[0].size, transcendentals=0
+            flops=0, bytes_accessed=4 * batches * (count + held) * LANES, transcendentals=0
         ),
         name="pick_rows",
-    )(index, table)
+    )(index, table, sums)
 
 
 def on_device(
@@ -364,7 +497,7 @@
     chips = tensors // 2
     batch_index = lax.axis_index("batch")
     tensor_index = lax.axis_index("tensor")
-    my_major, my_minor = batch_index // side, batch_index % side
+    my_major = batch_index // side
     my_chip, my_core = tensor_index // 2, tensor_index % 2
     _, rows, past, kv_width = past_cache.shape
     width = layer_input.shape[2]
@@ -379,7 +512,7 @@
 
     with jax.named_scope("cache_spread"):
         pieces = past_cache.reshape(2, rows, batches, span, kv_width).transpose(2, 1, 0, 3, 4)
-        spread = exchange(pieces, "batch").reshape(batches * rows, 2, span, kv_width)
+        spread = exchange(pieces, "batch").reshape(batches * rows, 2 * span, kv_width)
 
     with jax.named_scope("places"):
         parents = parent_rows.reshape(STEPS, batches, rows)
@@ -387,9 +520,8 @@
         wanted = jnp.stack([parents[0], origin.reshape(batches, rows)], axis=1).reshape(total)
         place = jnp.arange(total, dtype=jnp.int32)
         inner = place % both
-        ahead = (my_major + place // (side * both)) % side * side
-        ahead = ahead + (my_minor + place // both) % side
-        input_order = ((inner // rows) * (batches * rows) + ahead * rows + inner % rows)[:, None]
+        near = place // both
+        input_order = ((inner // rows) * (batches * rows) + near * rows + inner % rows)[:, None]
         row = (my_major + place // (side * both)) % side * side + place // both % side
         row = row * both + inner
         owner = row // share
@@ -403,8 +535,8 @@
         targets = targets + block * both % share
 
     with jax.named_scope("project"):
-        blocks = project_rows(
-            side,
+        sums = project_rows(
+            batches,
             input_order,
             parent_rows[1][:, None],
             after(layer_input, pieces),
@@ -412,61 +544,16 @@
             query_weight,
             keyval_weight,
         )
-        picked = pick_rows(spread, wanted).reshape(batches, both, 2, span, kv_width)
-        summed = jnp.concatenate(add_over_batch(blocks[:side], blocks[side:], picked), axis=1)
 
     with jax.named_scope("cache_return"):
-        returned = exchange(picked, "batch").transpose(2, 1, 0, 3, 4)
-        caches = returned.reshape(2, both, past, kv_width)
-        cache_out = caches[:, rows:]
+        returned = exchange(pick_rows(spread, wanted, sums), "batch")
 
     with jax.named_scope("attention"):
-        edge = head_width + 3 * kv_width
-        mean = (summed[:, edge] + summed[:, edge + 1]) / model
-        parent_mean = (summed[:, edge + 2] + summed[:, edge + 3]) / model
-        scale = lax.rsqrt(mean + norm_eps)[:, None]
-        parent_scale = lax.rsqrt(parent_mean + norm_eps)[:, None]
-        step_of = jnp.arange(both, dtype=jnp.int32) // rows
-        cosine, sine = rotary(step_of, past)
-        queries = rotate(
-            (summed[:, :head_width] * scale).reshape(both, heads, HD),
-            cosine[:, None],
-            sine[:, None],
-        ).astype(jnp.bfloat16)
-        new_keys = rotate(
-            summed[:, head_width : head_width + kv_width] * scale, cosine, sine
-        ).astype(jnp.bfloat16)
-        new_values = (
-            summed[:, head_width + kv_width : head_width + 2 * kv_width] * scale
-        ).astype(jnp.bfloat16)
-        parent_sums = summed[:, head_width + 2 * kv_width : edge] * parent_scale
-        parent_keys = rotate(parent_sums[:rows], cosine[:rows], sine[:rows]).astype(jnp.bfloat16)
-        parent_values = parent_sums[rows:].astype(jnp.bfloat16)
-        fresh_keys = jnp.stack(
-            [jnp.concatenate([new_keys[:rows], parent_keys]), new_keys], axis=1
-        )
-        fresh_values = jnp.stack(
-            [jnp.concatenate([new_values[:rows], parent_values]), new_values], axis=1
-        )
-        fresh_out = jnp.stack([fresh_keys[rows:], fresh_values[rows:]])
-        old_scores = jnp.einsum(
-            "ngd,ntd->ngt", queries, caches[0], preferred_element_type=jnp.float32
-        )
-        fresh_scores = jnp.einsum(
-            "ngd,ntd->ngt", queries, fresh_keys, preferred_element_type=jnp.float32
-        )
-        scores = jnp.concatenate([old_scores, fresh_scores], axis=2) * (1.0 / math.sqrt(HD))
-        position = jnp.arange(past + STEPS, dtype=jnp.int32)
-        seen = position[None, :] <= (past + step_of)[:, None]
-        scores = jnp.where(seen[:, None, :], scores, -jnp.inf)
-        weights = jax.nn.softmax(scores, axis=-1).astype(jnp.bfloat16)
-        attended = jnp.einsum(
-            "ngt,ntd->ngd", weights[..., :past], caches[1], preferred_element_type=jnp.float32
-        ) + jnp.einsum(
-            "ngt,ntd->ngd", weights[..., past:], fresh_values, preferred_element_type=jnp.float32
-        )
-        attended = attended.astype(jnp.bfloat16).reshape(both, head_width)
-        attended = gather_all(attended, "batch")
+        attended, fresh, kept = attend(returned, heads, rows, past, model)
+        fresh_out = fresh.reshape(2, STEPS, both, kv_width)[:, :, rows:].transpose(0, 2, 1, 3)
+        fresh_out = fresh_out.astype(jnp.bfloat16)
+        cache_out = kept.reshape(2, rows, past, kv_width)
+        attended = exchange(attended, "batch").reshape(total, head_width)
 
     with jax.named_scope("output_projection"):
         own_inputs = lax.dynamic_slice_in_dim(

time: 259 us -> 249 us (0.961)
  blocking collectives: 29.8 us -> 87.7 us
  waiting for transfers between devices: 102 us -> 64 us
  starting transfers between devices: 70.6 us -> 54.8 us
  other arithmetic: 10.4 us -> 3.7 us
  local copies, waits for them, and re-layouts: 22.2 us -> 17 us
    all_to_all x1 -> x2, blocking collectives: 29.8 us -> 87.7 us  [exchange(): return lax.all_to_all(blocks, axis, split_axis=0, concat_axis=0, tiled=True)]
    ppermute x18 -> x6, waiting for transfers between devices: 47.3 us -> 26 us  [shift_along(): return lax.ppermute(block, 'batch', pairs)]
    all_to_all x3 -> x2, starting transfers between devices: 25.6 us -> 12.7 us  [exchange(): return lax.all_to_all(blocks, axis, split_axis=0, concat_axis=0, tiled=True)]
    ppermute x18 -> x6, starting transfers between devices: 17.3 us -> 6.65 us  [shift_along(): return lax.ppermute(block, 'batch', pairs)]
    all_to_all x3 -> x2, waiting for transfers between devices: 33.9 us -> 24.3 us  [exchange(): return lax.all_to_all(blocks, axis, split_axis=0, concat_axis=0, tiled=True)]
    ppermute x9, starting transfers between devices: 7.2 us -> 12.5 us  [shift_chips(): lax.ppermute(block, 'tensor', [(at, (at + 2 * count) % size) for at in ra...]
    slice x10 -> x1, local copies, waits for them, and re-layouts: 5.06 us -> 0.01 us  [on_device(): fresh.reshape(2, STEPS, both, kv_width)[:, :, rows:].transpose(0, 2, 1, 3)]
    sub x1 -> x0, other arithmetic: 4.34 us -> none  [on_device(): weights = jax.nn.softmax(scores, axis=-1).astype(jnp.bfloat16)]
  transfers between devices with their start and end apart: 35 -> 22, of which waited for: 21 -> 18; matrix products, arithmetic and copies ran while one was open for 5% -> 2% of each run, Pallas kernels for 3% -> 1%
where the time goes in v3:
time: 249 us; the launch traced here: 248 us
  blocking collectives  87.7 us (35%)
  waiting for transfers between devices  64 us (26%)
  starting transfers between devices  54.8 us (22%)
  Pallas kernels  19.7 us (8%)
  local copies, waits for them, and re-layouts  17 us (7%)
  other arithmetic  3.7 us (1%)
    all_to_all x2, blocking collectives, exchange(): return lax.all_to_all(blocks, axis, split_axis=0, concat_axis=0, tiled=True)  87.7 us
    ppermute x6, waiting for transfers between devices, shift_along(): return lax.ppermute(block, 'batch', pairs)  26 us
    all_to_all x2, waiting for transfers between devices, exchange(): return lax.all_to_all(blocks, axis, split_axis=0, concat_axis=0, tiled=True)  24.3 us
    ppermute x3, starting transfers between devices, swap_cores(): return lax.ppermute(block, 'tensor', [(at, at ^ 1) for at in range(size)])  15.6 us
    all_to_all x2, starting transfers between devices, exchange(): return lax.all_to_all(blocks, axis, split_axis=0, concat_axis=0, tiled=True)  12.7 us
    ppermute x9, starting transfers between devices, shift_chips(): lax.ppermute(block, 'tensor', [(at, (at + 2 * count) % size) for at in ra...  12.5 us
    unnamed x36, local copies, waits for them, and re-layouts  11.6 us
    pallas_call x1, Pallas kernels, gate_up(): pl.pallas_call(functools.partial(gate_up_kernel, side, spans), out_shape=...  8.6 us
  transfers between devices with their start and end apart: 22, of which 18 were waited for; matrix products, arithmetic and copies ran while one was open for 2% of the time, Pallas kernels for 1%

profile of v3, /device:TPU:1, one launch (start us, length us, event | category | flops | bytes accessed | tf_op | source)
XLA Modules:
  0.0 247.9 jit_solution(6348075845542719549)
XLA Ops:
  0.6 3.0 %copy.29 = bf16[2,12,16,16,128]{4,3,0,1,2:T(8,128)(2,1)} copy(bf16[2,12,16,16,128]{4,3,2,1,0:T(8,128)(2,1)} %bitcast.28) | data formatting | bytes 3145728 | tf_op jit(solution)/shard_map/cache_spread/reshape | solution.py:514
  3.6 8.7 %all-to-all-start = ((bf16[16,12,2,16,128]{4,3,2,1,0:T(8,128)(2,1)}), bf16[16,12,2,16,128]{4,3,2,1,0:T(8,128)(2,1)S(1)}, u32[]{:S(2)}, u32[]{:S(2)}) async-start(bf16[16,12,2,16,128]{4,3,2,1,0:T(8,128)(2,1)} %bitcast.22), calls=%async_computation | async-start | bytes 3145728 | tf_op jit(solution)/shard_map/cache_spread/all_to_all | solution.py:22
  18.6 2.6 %project_rows.1.sum_ref = bf16[16,384,128]{2,1,0:T(8,128)(2,1)S(1)} custom-call(s32[384,1]{1,0:T(8,128)S(1)} %fusion.9.order_ref, s32[192,1]{1,0:T(8,128)S(1)} %copy.22.parent_ref, bf16[2,192,768]{2,1,0:T(8,128)(2,1)S(1)} %copy-done.5, bf16[1,768]{1,0:T(2,128)(2,1)S(1)} %reshape.493.gain_ref, bf16[768,1536]{1,0:T(8,128)(2,1)S(1)} %copy-done.1, ...), custom_call_target="tpu_custom_call" | custom-call | flops 1207959552 | bytes 4718592 | tf_op jit(solution)/shard_map/project/project_rows/pallas_call | solution.py:195
  21.2 11.8 %all-to-all-done = bf16[16,12,2,16,128]{4,3,2,1,0:T(8,128)(2,1)S(1)} async-done(((bf16[16,12,2,16,128]{4,3,2,1,0:T(8,128)(2,1)}), bf16[16,12,2,16,128]{4,3,2,1,0:T(8,128)(2,1)S(1)}, u32[]{:S(2)}, u32[]{:S(2)}) %all-to-all-start) | async-done | bytes 1572896 | tf_op jit(solution)/shard_map/cache_spread/all_to_all | solution.py:22
  34.0 58.3 %all_to_all.30.cache_ref = bf16[16,1152,128]{2,1,0:T(8,128)(2,1)S(1)} all-to-all(bf16[16,1152,128]{2,1,0:T(8,128)(2,1)S(1)} %pick_rows.1), channel_id=1, replica_groups=mesh['batch'=16,'tensor'=8] {'batch'}, dimensions={0} | all-to-all | bytes 9437184 | tf_op jit(solution)/shard_map/cache_return/all_to_all | solution.py:22
  96.1 4.0 %all-to-all-start.2 = ((bf16[16,24,1536]{2,1,0:T(8,128)(2,1)}), bf16[16,24,1536]{2,1,0:T(8,128)(2,1)S(1)}, u32[]{:S(2)}, u32[]{:S(2)}) async-start(bf16[16,24,1536]{2,1,0:T(8,128)(2,1)} %copy-done.4), calls=%async_computation.2 | async-start | bytes 2359296 | tf_op jit(solution)/shard_map/attention/all_to_all | solution.py:22
  100.2 12.6 %all-to-all-done.2 = bf16[16,24,1536]{2,1,0:T(8,128)(2,1)S(1)} async-done(((bf16[16,24,1536]{2,1,0:T(8,128)(2,1)}), bf16[16,24,1536]{2,1,0:T(8,128)(2,1)S(1)}, u32[]{:S(2)}, u32[]{:S(2)}) %all-to-all-start.2) | async-done | bytes 1179680 | tf_op jit(solution)/shard_map/attention/all_to_all | solution.py:22
  112.7 2.5 %spread_dot.2 = (f32[192,768]{1,0:T(8,128)S(1)}, f32[192,768]{1,0:T(8,128)}) custom-call(s32[16]{0:T(128)S(1)} %fusion.41.place_ref, bf16[384,1536]{1,0:T(8,128)(2,1)S(1)} %bitcast.26, bf16[1536,768]{1,0:T(8,128)(2,1)S(1)} %copy-done.2), custom_call_target="tpu_custom_call" | custom-call | flops 905969664 | bytes 5898240 | tf_op jit(solution)/shard_map/output_projection/spread_dot/pallas_call | solution.py:312
  116.1 7.2 %collective-permute-start = (f32[192,768]{1,0:T(8,128)}, f32[192,768]{1,0:T(8,128)S(1)}, u32[]{:S(2)}, u32[]{:S(2)}) collective-permute-start(f32[192,768]{1,0:T(8,128)} %get-tuple-element.31), channel_id=1, source_target_pairs={{0,1},{1,0},{2,3},{3,2},{4,5},{5,4},{6,7},{7,6},{8,9},{9,8},{10,11... | collective-permute-start | bytes 1769480 | tf_op jit(solution)/shard_map/output_projection/ppermute | solution.py:54
  127.6 2.5 collective-permute-start.2
  133.8 3.2 %collective-permute-start.5 = (bf16[48,768]{1,0:T(8,128)(2,1)S(1)}, bf16[48,768]{1,0:T(8,128)(2,1)S(1)}, u32[]{:S(2)}, u32[]{:S(2)}) collective-permute-start(bf16[48,768]{1,0:T(8,128)(2,1)S(1)} %get-tuple-element.58), channel_id=1, source_target_pairs={{0,4},{1,5},{2,6},{3,7},{4,0},{5,1},{6,2},{7,3},{8,12},{9,13},{10,... | collective-permute-start | bytes 221192 | tf_op jit(solution)/shard_map/output_projection/ppermute | solution.py:49
  140.5 3.7 %collective-permute-start.7 = (bf16[192,768]{1,0:T(8,128)(2,1)S(1)}, bf16[192,768]{1,0:T(8,128)(2,1)S(1)}, u32[]{:S(2)}, u32[]{:S(2)}) collective-permute-start(bf16[192,768]{1,0:T(8,128)(2,1)S(1)} %pad_maximum_fusion.near_ref), channel_id=1, source_target_pairs={{0,1},{1,0},{2,3},{3,2},{4,5},{5,4},{6,7},{7,6},{8,9},{9,8},{10,11... | collective-permute-start | bytes 884744 | tf_op jit(solution)/shard_map/output_projection/ppermute | solution.py:54
  145.4 8.6 %gate_up.1 = (bf16[4,96,2816]{2,1,0:T(8,128)(2,1)S(1)}, bf16[96,2688]{1,0:T(8,128)(2,1)S(1)}, bf16[96,2688]{1,0:T(8,128)(2,1)S(1)}, bf16[96,2688]{1,0:T(8,128)(2,1)S(1)}, bf16[96,2688]{1,0:T(8,128)(2,1)S(1)}) custom-call(s32[384,1]{1,0:T(8,128)S(1)} %fusion.23.order_ref, bf16[192,768]{1,0:T(8,128)(2,1)S(1)} %pad_maximum_fusion.near_ref, ...), custom_call_target="tpu_custom_call" | custom-call | flops 3170893824 | bytes 12386304 | tf_op jit(solution)/shard_map/gate_up/gate_up/pallas_call | solution.py:273
  157.0 3.6 %all-to-all-start.3 = ((bf16[4,96,2816]{2,1,0:T(8,128)(2,1)}), bf16[4,96,2816]{2,1,0:T(8,128)(2,1)S(1)}, u32[]{:S(2)}, u32[]{:S(2)}) async-start(bf16[4,96,2816]{2,1,0:T(8,128)(2,1)} %copy-done.3), calls=%async_computation.3 | async-start | bytes 4325376 | tf_op jit(solution)/shard_map/gate_up/all_to_all | solution.py:88
  163.4 12.5 %collective-permute-done.11 = bf16[96,2688]{1,0:T(8,128)(2,1)S(1)} collective-permute-done((bf16[96,2688]{1,0:T(8,128)(2,1)}, bf16[96,2688]{1,0:T(8,128)(2,1)S(1)}, u32[]{:S(2)}, u32[]{:S(2)}) %collective-permute-start.11) | collective-permute-done | bytes 516128 | tf_op jit(solution)/shard_map/gate_up/ppermute | solution.py:44
  175.9 9.5 %collective-permute-done.12 = bf16[96,2688]{1,0:T(8,128)(2,1)S(1)} collective-permute-done((bf16[96,2688]{1,0:T(8,128)(2,1)}, bf16[96,2688]{1,0:T(8,128)(2,1)S(1)}, u32[]{:S(2)}, u32[]{:S(2)}) %collective-permute-start.12) | collective-permute-done | bytes 516128 | tf_op jit(solution)/shard_map/gate_up/ppermute | solution.py:44
  187.6 3.8 %all-to-all-start.4 = ((bf16[4,24,2688]{2,1,0:T(8,128)(2,1)}), bf16[4,24,2688]{2,1,0:T(8,128)(2,1)S(1)}, u32[]{:S(2)}, u32[]{:S(2)}) async-start(bf16[4,24,2688]{2,1,0:T(8,128)(2,1)} %bitcast.9), calls=%async_computation.4 | async-start | bytes 1032192 | tf_op jit(solution)/shard_map/gate_up/all_to_all | solution.py:88
  191.7 2.6 %collective-permute-start.10 = (bf16[24,2816]{1,0:T(8,128)(2,1)S(1)}, bf16[24,2816]{1,0:T(8,128)(2,1)S(1)}, u32[]{:S(2)}, u32[]{:S(2)}) collective-permute-start(bf16[24,2816]{1,0:T(8,128)(2,1)S(1)} %get-tuple-element.40), channel_id=1, source_target_pairs={{0,96},{8,104},{16,112},{24,120},{32,0},{40,8},{48,16},{56,24},{64... | collective-permute-start | bytes 405512 | tf_op jit(solution)/shard_map/gate_up/ppermute | solution.py:44
  195.6 2.9 %all-to-all-done.4 = bf16[4,24,2688]{2,1,0:T(8,128)(2,1)S(1)} async-done(((bf16[4,24,2688]{2,1,0:T(8,128)(2,1)}), bf16[4,24,2688]{2,1,0:T(8,128)(2,1)S(1)}, u32[]{:S(2)}, u32[]{:S(2)}) %all-to-all-start.4) | async-done | bytes 516128 | tf_op jit(solution)/shard_map/gate_up/all_to_all | solution.py:88
  198.6 2.8 %collective-permute-done.8 = bf16[24,2816]{1,0:T(8,128)(2,1)S(1)} collective-permute-done((bf16[24,2816]{1,0:T(8,128)(2,1)S(1)}, bf16[24,2816]{1,0:T(8,128)(2,1)S(1)}, u32[]{:S(2)}, u32[]{:S(2)}) %collective-permute-start.8) | collective-permute-done | bytes 135200 | tf_op jit(solution)/shard_map/gate_up/ppermute | solution.py:44
  202.0 29.3 %all_to_all.31 = bf16[16,24,2688]{2,1,0:T(8,128)(2,1)S(1)} all-to-all(bf16[16,24,2688]{2,1,0:T(8,128)(2,1)S(1)} %broadcast_in_dim.9), channel_id=1, replica_groups=mesh['batch'=16,'tensor'=8] {'batch'}, dimensions={0} | all-to-all | bytes 4128768 | tf_op jit(solution)/shard_map/gate_up/all_to_all | solution.py:22
  231.4 2.5 spread_dot.3
  233.8 4.6 %collective-permute-start.14 = (f32[192,768]{1,0:T(8,128)S(1)}, f32[192,768]{1,0:T(8,128)S(1)}, u32[]{:S(2)}, u32[]{:S(2)}) collective-permute-start(f32[192,768]{1,0:T(8,128)S(1)} %get-tuple-element.46), channel_id=1, source_target_pairs={{0,1},{1,0},{2,3},{3,2},{4,5},{5,4},{6,7},{7,6},{8,9},{9,8},{10,11... | collective-permute-start | bytes 1769480 | tf_op jit(solution)/shard_map/down_projection/ppermute | solution.py:54
  240.2 2.7 %collective-permute-start.16 = (bf16[48,768]{1,0:T(8,128)(2,1)S(1)}, bf16[48,768]{1,0:T(8,128)(2,1)S(1)}, u32[]{:S(2)}, u32[]{:S(2)}) collective-permute-start(bf16[48,768]{1,0:T(8,128)(2,1)S(1)} %get-tuple-element.49), channel_id=1, source_target_pairs={{0,4},{1,5},{2,6},{3,7},{4,0},{5,1},{6,2},{7,3},{8,12},{9,13},{10,... | collective-permute-start | bytes 221192 | tf_op jit(solution)/shard_map/down_projection/ppermute | solution.py:49
  (103 shorter events, 41.3 us)
Async XLA Ops:
  3.6 29.4 %all-to-all-start = ((bf16[16,12,2,16,128]{4,3,2,1,0:T(8,128)(2,1)}), bf16[16,12,2,16,128]{4,3,2,1,0:T(8,128)(2,1)S(1)}, u32[]{:S(2)}, u32[]{:S(2)}) async-start(bf16[16,12,2,16,128]{4,3,2,1,0:T(8,128)(2,1)} %bitcast.22), calls=%async_computation | async-start | bytes 3145728 | tf_op jit(solution)/shard_map/cache_spread/all_to_all | solution.py:22
  34.0 58.3 %copy-start.11 = (f32[24,256]{1,0:T(8,128)S(1)}, f32[24,256]{1,0:T(8,128)}, u32[]{:S(2)}) copy-start(f32[24,256]{1,0:T(8,128)} %constant.191.clone.table_ref) | copy-start | bytes 73732
  96.1 16.6 %all-to-all-start.2 = ((bf16[16,24,1536]{2,1,0:T(8,128)(2,1)}), bf16[16,24,1536]{2,1,0:T(8,128)(2,1)S(1)}, u32[]{:S(2)}, u32[]{:S(2)}) async-start(bf16[16,24,1536]{2,1,0:T(8,128)(2,1)} %copy-done.4), calls=%async_computation.2 | async-start | bytes 2359296 | tf_op jit(solution)/shard_map/attention/all_to_all | solution.py:22
  116.1 9.1 %collective-permute-start = (f32[192,768]{1,0:T(8,128)}, f32[192,768]{1,0:T(8,128)S(1)}, u32[]{:S(2)}, u32[]{:S(2)}) collective-permute-start(f32[192,768]{1,0:T(8,128)} %get-tuple-element.31), channel_id=1, source_target_pairs={{0,1},{1,0},{2,3},{3,2},{4,5},{5,4},{6,7},{7,6},{8,9},{9,8},{10,11... | collective-permute-start | bytes 1769480 | tf_op jit(solution)/shard_map/output_projection/ppermute | solution.py:54
  126.3 5.9 %collective-permute-start.1 = (bf16[48,768]{1,0:T(8,128)(2,1)S(1)}, bf16[48,768]{1,0:T(8,128)(2,1)S(1)}, u32[]{:S(2)}, u32[]{:S(2)}) collective-permute-start(bf16[48,768]{1,0:T(8,128)(2,1)S(1)} %get-tuple-element.33), channel_id=1, source_target_pairs={{0,2},{1,3},{2,4},{3,5},{4,6},{5,7},{6,0},{7,1},{8,10},{9,11},{10,... | collective-permute-start | bytes 221192 | tf_op jit(solution)/shard_map/output_projection/ppermute | solution.py:49
  127.6 5.8 %collective-permute-start.2 = (bf16[48,768]{1,0:T(8,128)(2,1)S(1)}, bf16[48,768]{1,0:T(8,128)(2,1)S(1)}, u32[]{:S(2)}, u32[]{:S(2)}) collective-permute-start(bf16[48,768]{1,0:T(8,128)(2,1)S(1)} %get-tuple-element.34), channel_id=1, source_target_pairs={{0,4},{1,5},{2,6},{3,7},{4,0},{5,1},{6,2},{7,3},{8,12},{9,13},{10,... | collective-permute-start | bytes 221192 | tf_op jit(solution)/shard_map/output_projection/ppermute | solution.py:49
  130.1 3.5 %collective-permute-start.3 = (bf16[48,768]{1,0:T(8,128)(2,1)S(1)}, bf16[48,768]{1,0:T(8,128)(2,1)S(1)}, u32[]{:S(2)}, u32[]{:S(2)}) collective-permute-start(bf16[48,768]{1,0:T(8,128)(2,1)S(1)} %get-tuple-element.35), channel_id=1, source_target_pairs={{0,6},{1,7},{2,0},{3,1},{4,2},{5,3},{6,4},{7,5},{8,14},{9,15},{10,... | collective-permute-start | bytes 221192 | tf_op jit(solution)/shard_map/output_projection/ppermute | solution.py:49
  133.6 4.5 %collective-permute-start.4 = (bf16[48,768]{1,0:T(8,128)(2,1)S(1)}, bf16[48,768]{1,0:T(8,128)(2,1)S(1)}, u32[]{:S(2)}, u32[]{:S(2)}) collective-permute-start(bf16[48,768]{1,0:T(8,128)(2,1)S(1)} %get-tuple-element.58), channel_id=1, source_target_pairs={{0,2},{1,3},{2,4},{3,5},{4,6},{5,7},{6,0},{7,1},{8,10},{9,11},{10,... | collective-permute-start | bytes 221192 | tf_op jit(solution)/shard_map/output_projection/ppermute | solution.py:49
  133.8 5.8 %collective-permute-start.5 = (bf16[48,768]{1,0:T(8,128)(2,1)S(1)}, bf16[48,768]{1,0:T(8,128)(2,1)S(1)}, u32[]{:S(2)}, u32[]{:S(2)}) collective-permute-start(bf16[48,768]{1,0:T(8,128)(2,1)S(1)} %get-tuple-element.58), channel_id=1, source_target_pairs={{0,4},{1,5},{2,6},{3,7},{4,0},{5,1},{6,2},{7,3},{8,12},{9,13},{10,... | collective-permute-start | bytes 221192 | tf_op jit(solution)/shard_map/output_projection/ppermute | solution.py:49
  137.0 3.5 %collective-permute-start.6 = (bf16[48,768]{1,0:T(8,128)(2,1)S(1)}, bf16[48,768]{1,0:T(8,128)(2,1)S(1)}, u32[]{:S(2)}, u32[]{:S(2)}) collective-permute-start(bf16[48,768]{1,0:T(8,128)(2,1)S(1)} %get-tuple-element.58), channel_id=1, source_target_pairs={{0,6},{1,7},{2,0},{3,1},{4,2},{5,3},{6,4},{7,5},{8,14},{9,15},{10,... | collective-permute-start | bytes 221192 | tf_op jit(solution)/shard_map/output_projection/ppermute | solution.py:49
  140.5 4.9 %collective-permute-start.7 = (bf16[192,768]{1,0:T(8,128)(2,1)S(1)}, bf16[192,768]{1,0:T(8,128)(2,1)S(1)}, u32[]{:S(2)}, u32[]{:S(2)}) collective-permute-start(bf16[192,768]{1,0:T(8,128)(2,1)S(1)} %pad_maximum_fusion.near_ref), channel_id=1, source_target_pairs={{0,1},{1,0},{2,3},{3,2},{4,5},{5,4},{6,7},{7,6},{8,9},{9,8},{10,11... | collective-permute-start | bytes 884744 | tf_op jit(solution)/shard_map/output_projection/ppermute | solution.py:54
  157.0 30.6 %all-to-all-start.3 = ((bf16[4,96,2816]{2,1,0:T(8,128)(2,1)}), bf16[4,96,2816]{2,1,0:T(8,128)(2,1)S(1)}, u32[]{:S(2)}, u32[]{:S(2)}) async-start(bf16[4,96,2816]{2,1,0:T(8,128)(2,1)} %copy-done.3), calls=%async_computation.3 | async-start | bytes 4325376 | tf_op jit(solution)/shard_map/gate_up/all_to_all | solution.py:88
  160.7 15.2 %collective-permute-start.11 = (bf16[96,2688]{1,0:T(8,128)(2,1)}, bf16[96,2688]{1,0:T(8,128)(2,1)S(1)}, u32[]{:S(2)}, u32[]{:S(2)}) collective-permute-start(bf16[96,2688]{1,0:T(8,128)(2,1)} %copy-done.13), channel_id=1, source_target_pairs={{0,32},{8,40},{16,48},{24,56},{32,64},{40,72},{48,80},{56,88},{64,... | collective-permute-start | bytes 1548296 | tf_op jit(solution)/shard_map/gate_up/ppermute | solution.py:44
  160.7 24.7 %collective-permute-start.12 = (bf16[96,2688]{1,0:T(8,128)(2,1)}, bf16[96,2688]{1,0:T(8,128)(2,1)S(1)}, u32[]{:S(2)}, u32[]{:S(2)}) collective-permute-start(bf16[96,2688]{1,0:T(8,128)(2,1)} %copy-done.12), channel_id=1, source_target_pairs={{0,64},{8,72},{16,80},{24,88},{32,96},{40,104},{48,112},{56,120},{... | collective-permute-start | bytes 1548296 | tf_op jit(solution)/shard_map/gate_up/ppermute | solution.py:44
  162.6 23.9 %collective-permute-start.13 = (bf16[96,2688]{1,0:T(8,128)(2,1)S(1)}, bf16[96,2688]{1,0:T(8,128)(2,1)S(1)}, u32[]{:S(2)}, u32[]{:S(2)}) collective-permute-start(bf16[96,2688]{1,0:T(8,128)(2,1)S(1)} %get-tuple-element.44), channel_id=1, source_target_pairs={{0,96},{8,104},{16,112},{24,120},{32,0},{40,8},{48,16},{56,24},{64... | collective-permute-start | bytes 1548296 | tf_op jit(solution)/shard_map/gate_up/ppermute | solution.py:44
  187.6 10.9 %all-to-all-start.4 = ((bf16[4,24,2688]{2,1,0:T(8,128)(2,1)}), bf16[4,24,2688]{2,1,0:T(8,128)(2,1)S(1)}, u32[]{:S(2)}, u32[]{:S(2)}) async-start(bf16[4,24,2688]{2,1,0:T(8,128)(2,1)} %bitcast.9), calls=%async_computation.4 | async-start | bytes 1032192 | tf_op jit(solution)/shard_map/gate_up/all_to_all | solution.py:88
  191.7 6.9 %collective-permute-start.10 = (bf16[24,2816]{1,0:T(8,128)(2,1)S(1)}, bf16[24,2816]{1,0:T(8,128)(2,1)S(1)}, u32[]{:S(2)}, u32[]{:S(2)}) collective-permute-start(bf16[24,2816]{1,0:T(8,128)(2,1)S(1)} %get-tuple-element.40), channel_id=1, source_target_pairs={{0,96},{8,104},{16,112},{24,120},{32,0},{40,8},{48,16},{56,24},{64... | collective-permute-start | bytes 405512 | tf_op jit(solution)/shard_map/gate_up/ppermute | solution.py:44
  194.3 7.1 %collective-permute-start.8 = (bf16[24,2816]{1,0:T(8,128)(2,1)S(1)}, bf16[24,2816]{1,0:T(8,128)(2,1)S(1)}, u32[]{:S(2)}, u32[]{:S(2)}) collective-permute-start(bf16[24,2816]{1,0:T(8,128)(2,1)S(1)} %get-tuple-element.38), channel_id=1, source_target_pairs={{0,32},{8,40},{16,48},{24,56},{32,64},{40,72},{48,80},{56,88},{64,... | collective-permute-start | bytes 405512 | tf_op jit(solution)/shard_map/gate_up/ppermute | solution.py:44
  194.4 7.1 %collective-permute-start.9 = (bf16[24,2816]{1,0:T(8,128)(2,1)S(1)}, bf16[24,2816]{1,0:T(8,128)(2,1)S(1)}, u32[]{:S(2)}, u32[]{:S(2)}) collective-permute-start(bf16[24,2816]{1,0:T(8,128)(2,1)S(1)} %get-tuple-element.39), channel_id=1, source_target_pairs={{0,64},{8,72},{16,80},{24,88},{32,96},{40,104},{48,112},{56,120},{... | collective-permute-start | bytes 405512 | tf_op jit(solution)/shard_map/gate_up/ppermute | solution.py:44
  202.0 29.4 %copy-start = (bf16[2688,768]{1,0:T(8,128)(2,1)S(1)}, bf16[2688,768]{1,0:T(8,128)(2,1)}, u32[]{:S(2)}) copy-start(bf16[2688,768]{1,0:T(8,128)(2,1)} %weight_ref.5) | copy-start | bytes 12386308
  233.8 6.2 %collective-permute-start.14 = (f32[192,768]{1,0:T(8,128)S(1)}, f32[192,768]{1,0:T(8,128)S(1)}, u32[]{:S(2)}, u32[]{:S(2)}) collective-permute-start(f32[192,768]{1,0:T(8,128)S(1)} %get-tuple-element.46), channel_id=1, source_target_pairs={{0,1},{1,0},{2,3},{3,2},{4,5},{5,4},{6,7},{7,6},{8,9},{9,8},{10,11... | collective-permute-start | bytes 1769480 | tf_op jit(solution)/shard_map/down_projection/ppermute | solution.py:54
  240.1 4.5 %collective-permute-start.15 = (bf16[48,768]{1,0:T(8,128)(2,1)S(1)}, bf16[48,768]{1,0:T(8,128)(2,1)S(1)}, u32[]{:S(2)}, u32[]{:S(2)}) collective-permute-start(bf16[48,768]{1,0:T(8,128)(2,1)S(1)} %get-tuple-element.48), channel_id=1, source_target_pairs={{0,2},{1,3},{2,4},{3,5},{4,6},{5,7},{6,0},{7,1},{8,10},{9,11},{10,... | collective-permute-start | bytes 221192 | tf_op jit(solution)/shard_map/down_projection/ppermute | solution.py:49
  240.2 6.0 %collective-permute-start.16 = (bf16[48,768]{1,0:T(8,128)(2,1)S(1)}, bf16[48,768]{1,0:T(8,128)(2,1)S(1)}, u32[]{:S(2)}, u32[]{:S(2)}) collective-permute-start(bf16[48,768]{1,0:T(8,128)(2,1)S(1)} %get-tuple-element.49), channel_id=1, source_target_pairs={{0,4},{1,5},{2,6},{3,7},{4,0},{5,1},{6,2},{7,3},{8,12},{9,13},{10,... | collective-permute-start | bytes 221192 | tf_op jit(solution)/shard_map/down_projection/ppermute | solution.py:49
  243.0 4.1 %collective-permute-start.17 = (bf16[48,768]{1,0:T(8,128)(2,1)S(1)}, bf16[48,768]{1,0:T(8,128)(2,1)S(1)}, u32[]{:S(2)}, u32[]{:S(2)}) collective-permute-start(bf16[48,768]{1,0:T(8,128)(2,1)S(1)} %get-tuple-element.50), channel_id=1, source_target_pairs={{0,6},{1,7},{2,0},{3,1},{4,2},{5,3},{6,4},{7,5},{8,14},{9,15},{10,... | collective-permute-start | bytes 221192 | tf_op jit(solution)/shard_map/down_projection/ppermute | solution.py:49
  (15 other events, 74.9 us)

commit v4 on v3

--- a/solution.py
+++ b/solution.py
@@ -220,7 +220,17 @@
                 held_ref.at[half, :, columns],
                 in_sems.at[half, at],
             )
-            loads[half, at].start()
+    order = [(half, at) for half in (1, 0) for at in range(len(spans))]
+    ahead = 4
+    for key in order[:ahead]:
+        loads[key].start()
+
+    def arrived(half, at):
+        step = order.index((half, at))
+        if step + ahead < len(order):
+            loads[order[step + ahead]].start()
+        loads[half, at].wait()
+
     lifted = jnp.concatenate([near_ref[...], far_ref[...]], axis=0)
     ordered = dot(one_hot(order_ref[...], lifted.shape[0]), lifted)
     plain = ordered * (1.0 / gain_ref[...].astype(jnp.float32))
@@ -229,7 +239,7 @@
     rows = ordered.shape[0] // side
     stores = []
     for at, (start, size) in enumerate(spans):
-        loads[1, at].wait()
+        arrived(1, at)
         ups = dot(ordered, held_ref[1, :, start : start + size])
         for place in range(side):
             second_held[place, :, start : start + size] = ups[
@@ -244,7 +254,7 @@
         stores[-1].start()
     for at, (start, size) in enumerate(list(spans) + [(hidden, LANES)]):
         if start < hidden:
-            loads[0, at].wait()
+            arrived(0, at)
             gates = dot(ordered, held_ref[0, :, start : start + size])
         else:
             gates = statistics
@@ -267,7 +277,8 @@
     total, width = order.shape[0], near.shape[1]
     hidden = weight.shape[2]
     rows = total // side
-    spans = [(start, min(tile, hidden - start)) for start in range(0, hidden, tile)]
+    edges = [0] + list(range(hidden % tile or tile, hidden + 1, tile))
+    spans = [(start, stop - start) for start, stop in zip(edges, edges[1:])]
     whole = pl.BlockSpec(memory_space=pltpu.VMEM)
     far_off = pl.BlockSpec(memory_space=pltpu.HBM)
     return pl.pallas_call(
@@ -284,7 +295,7 @@
             pltpu.SemaphoreType.DMA((len(spans) + 1,)),
             pltpu.SemaphoreType.DMA((side,)),
         ],
-        compiler_params=pltpu.CompilerParams(vmem_limit_bytes=48 * MIB),
+        compiler_params=pltpu.CompilerParams(vmem_limit_bytes=58 * MIB),
         cost_estimate=pl.CostEstimate(
             flops=4 * total * width * hidden,
             bytes_accessed=4 * hidden * (width + total),
@@ -546,7 +557,8 @@
         )
 
     with jax.named_scope("cache_return"):
-        returned = exchange(pick_rows(spread, wanted, sums), "batch")
+        ready = after(wanted, (lifted_order, targets))
+        returned = exchange(pick_rows(spread, ready, sums), "batch")
 
     with jax.named_scope("attention"):
         attended, fresh, kept = attend(returned, heads, rows, past, model)

time: 249 us -> 243 us (0.976)
  blocking collectives: 87.7 us -> 107 us
  waiting for transfers between devices: 64 us -> 51.1 us
  starting transfers between devices: 54.8 us -> 48.8 us
  local copies, waits for them, and re-layouts: 17 us -> 11.7 us
    all_to_all x2 -> x3, blocking collectives: 87.7 us -> 107 us  [exchange(): return lax.all_to_all(blocks, axis, split_axis=0, concat_axis=0, tiled=True)]
    all_to_all x2 -> x1, waiting for transfers between devices: 24.3 us -> 10.3 us  [exchange(): return lax.all_to_all(blocks, axis, split_axis=0, concat_axis=0, tiled=True)]
    unnamed x36 -> x28, local copies, waits for them, and re-layouts: 11.6 us -> 5.73 us
    all_to_all x2 -> x1, starting transfers between devices: 12.7 us -> 8.73 us  [exchange(): return lax.all_to_all(blocks, axis, split_axis=0, concat_axis=0, tiled=True)]
    ppermute x3, starting transfers between devices: 15.6 us -> 11.8 us  [swap_cores(): return lax.ppermute(block, 'tensor', [(at, at ^ 1) for at in range(size)])]
  transfers between devices with their start and end apart: 22 -> 21, of which waited for: 18 -> 17; matrix products, arithmetic and copies ran while one was open for 2% -> 3% of each run, Pallas kernels for 1% -> 1%
where the time goes in v4:
time: 243 us
  blocking collectives  107 us (44%)
  waiting for transfers between devices  51.1 us (21%)
  starting transfers between devices  48.8 us (20%)
  Pallas kernels  19 us (8%)
  local copies, waits for them, and re-layouts  11.7 us (5%)
  other arithmetic  4.4 us (2%)
    all_to_all x3, blocking collectives, exchange(): return lax.all_to_all(blocks, axis, split_axis=0, concat_axis=0, tiled=True)  107 us
    ppermute x6, waiting for transfers between devices, shift_along(): return lax.ppermute(block, 'batch', pairs)  27.7 us
    ppermute x9, starting transfers between devices, shift_chips(): lax.ppermute(block, 'tensor', [(at, (at + 2 * count) % size) for at in ra...  12.5 us
    ppermute x3, starting transfers between devices, swap_cores(): return lax.ppermute(block, 'tensor', [(at, at ^ 1) for at in range(size)])  11.8 us
    all_to_all x1, waiting for transfers between devices, exchange(): return lax.all_to_all(blocks, axis, split_axis=0, concat_axis=0, tiled=True)  10.3 us
    pallas_call x1, Pallas kernels, gate_up(): pl.pallas_call(functools.partial(gate_up_kernel, side, spans), out_shape=...  8.85 us
    all_to_all x1, starting transfers between devices, exchange(): return lax.all_to_all(blocks, axis, split_axis=0, concat_axis=0, tiled=True)  8.73 us
    ppermute x6, starting transfers between devices, shift_along(): return lax.ppermute(block, 'batch', pairs)  8 us
  transfers between devices with their start and end apart: 21, of which 17 were waited for; matrix products, arithmetic and copies ran while one was open for 3% of the time, Pallas kernels for 1%

profile of v4, /device:TPU:1, one launch (start us, length us, event | category | flops | bytes accessed | tf_op | source)
XLA Modules:
  0.0 242.7 jit_solution(5854566992317195914)
XLA Ops:
  0.6 3.0 %copy.29 = bf16[2,12,16,16,128]{4,3,0,1,2:T(8,128)(2,1)} copy(bf16[2,12,16,16,128]{4,3,2,1,0:T(8,128)(2,1)} %bitcast.28) | data formatting | bytes 3145728 | tf_op jit(solution)/shard_map/cache_spread/reshape | solution.py:525
  3.6 8.7 %all-to-all-start = ((bf16[16,12,2,16,128]{4,3,2,1,0:T(8,128)(2,1)}), bf16[16,12,2,16,128]{4,3,2,1,0:T(8,128)(2,1)S(1)}, u32[]{:S(2)}, u32[]{:S(2)}) async-start(bf16[16,12,2,16,128]{4,3,2,1,0:T(8,128)(2,1)} %bitcast.22), calls=%async_computation | async-start | bytes 3145728 | tf_op jit(solution)/shard_map/cache_spread/all_to_all | solution.py:22
  20.1 2.5 %project_rows.1.sum_ref = bf16[16,384,128]{2,1,0:T(8,128)(2,1)S(1)} custom-call(s32[384,1]{1,0:T(8,128)S(1)} %fusion.13.order_ref, s32[192,1]{1,0:T(8,128)S(1)} %copy.22.parent_ref, bf16[2,192,768]{2,1,0:T(8,128)(2,1)S(1)} %copy-done.3, bf16[1,768]{1,0:T(2,128)(2,1)S(1)} %reshape.493.gain_ref, bf16[768,1536]{1,0:T(8,128)(2,1)S(1)} %copy-done.1, ...), custom_call_target="tpu_custom_call" | custom-call | flops 1207959552 | bytes 4718592 | tf_op jit(solution)/shard_map/project/project_rows/pallas_call | solution.py:195
  22.6 10.3 %all-to-all-done = bf16[16,12,2,16,128]{4,3,2,1,0:T(8,128)(2,1)S(1)} async-done(((bf16[16,12,2,16,128]{4,3,2,1,0:T(8,128)(2,1)}), bf16[16,12,2,16,128]{4,3,2,1,0:T(8,128)(2,1)S(1)}, u32[]{:S(2)}, u32[]{:S(2)}) %all-to-all-start) | async-done | bytes 1572896 | tf_op jit(solution)/shard_map/cache_spread/all_to_all | solution.py:22
  34.0 58.3 %all_to_all.30.cache_ref = bf16[16,1152,128]{2,1,0:T(8,128)(2,1)S(1)} all-to-all(bf16[16,1152,128]{2,1,0:T(8,128)(2,1)S(1)} %pick_rows.1), channel_id=1, replica_groups=mesh['batch'=16,'tensor'=8] {'batch'}, dimensions={0} | all-to-all | bytes 9437184 | tf_op jit(solution)/shard_map/cache_return/all_to_all | solution.py:22
  92.3 2.1 attend.1
  94.5 18.1 %all_to_all.31 = bf16[16,24,1536]{2,1,0:T(8,128)(2,1)S(1)} all-to-all(bf16[16,24,1536]{2,1,0:T(8,128)(2,1)S(1)} %get-tuple-element.31), channel_id=1, replica_groups=mesh['batch'=16,'tensor'=8] {'batch'}, dimensions={0} | all-to-all | bytes 2359296 | tf_op jit(solution)/shard_map/attention/all_to_all | solution.py:22
  114.3 5.1 %collective-permute-start = (f32[192,768]{1,0:T(8,128)S(1)}, f32[192,768]{1,0:T(8,128)S(1)}, u32[]{:S(2)}, u32[]{:S(2)}) collective-permute-start(f32[192,768]{1,0:T(8,128)S(1)} %get-tuple-element.33), channel_id=1, source_target_pairs={{0,1},{1,0},{2,3},{3,2},{4,5},{5,4},{6,7},{7,6},{8,9},{9,8},{10,11... | collective-permute-start | bytes 1769480 | tf_op jit(solution)/shard_map/output_projection/ppermute | solution.py:54
  122.3 2.5 %collective-permute-start.2 = (bf16[48,768]{1,0:T(8,128)(2,1)S(1)}, bf16[48,768]{1,0:T(8,128)(2,1)S(1)}, u32[]{:S(2)}, u32[]{:S(2)}) collective-permute-start(bf16[48,768]{1,0:T(8,128)(2,1)S(1)} %get-tuple-element.36), channel_id=1, source_target_pairs={{0,4},{1,5},{2,6},{3,7},{4,0},{5,1},{6,2},{7,3},{8,12},{9,13},{10,... | collective-permute-start | bytes 221192 | tf_op jit(solution)/shard_map/output_projection/ppermute | solution.py:49
  128.5 3.2 %collective-permute-start.5 = (bf16[48,768]{1,0:T(8,128)(2,1)S(1)}, bf16[48,768]{1,0:T(8,128)(2,1)S(1)}, u32[]{:S(2)}, u32[]{:S(2)}) collective-permute-start(bf16[48,768]{1,0:T(8,128)(2,1)S(1)} %get-tuple-element.60), channel_id=1, source_target_pairs={{0,4},{1,5},{2,6},{3,7},{4,0},{5,1},{6,2},{7,3},{8,12},{9,13},{10,... | collective-permute-start | bytes 221192 | tf_op jit(solution)/shard_map/output_projection/ppermute | solution.py:49
  135.2 3.7 %collective-permute-start.7 = (bf16[192,768]{1,0:T(8,128)(2,1)S(1)}, bf16[192,768]{1,0:T(8,128)(2,1)S(1)}, u32[]{:S(2)}, u32[]{:S(2)}) collective-permute-start(bf16[192,768]{1,0:T(8,128)(2,1)S(1)} %pad_maximum_fusion.near_ref), channel_id=1, source_target_pairs={{0,1},{1,0},{2,3},{3,2},{4,5},{5,4},{6,7},{7,6},{8,9},{9,8},{10,11... | collective-permute-start | bytes 884744 | tf_op jit(solution)/shard_map/output_projection/ppermute | solution.py:54
  140.9 8.9 %gate_up.1 = (bf16[4,96,2816]{2,1,0:T(8,128)(2,1)}, bf16[96,2688]{1,0:T(8,128)(2,1)}, bf16[96,2688]{1,0:T(8,128)(2,1)}, bf16[96,2688]{1,0:T(8,128)(2,1)}, bf16[96,2688]{1,0:T(8,128)(2,1)}) custom-call(s32[384,1]{1,0:T(8,128)} %fusion.26.order_ref, bf16[192,768]{1,0:T(8,128)(2,1)} %copy-done.7, bf16[192,768]{1,0:T(8,128)(2,1)} %copy-done.12, ...), custom_call_target="tpu_custom_call" | custom-call | flops 3170893824 | bytes 12386304 | tf_op jit(solution)/shard_map/gate_up/gate_up/pallas_call | solution.py:284
  149.7 3.8 %all-to-all-start.3 = ((bf16[4,96,2816]{2,1,0:T(8,128)(2,1)}), bf16[4,96,2816]{2,1,0:T(8,128)(2,1)S(1)}, u32[]{:S(2)}, u32[]{:S(2)}) async-start(bf16[4,96,2816]{2,1,0:T(8,128)(2,1)} %get-tuple-element.38), calls=%async_computation.3 | async-start | bytes 4325376 | tf_op jit(solution)/shard_map/gate_up/all_to_all | solution.py:88
  153.8 1.8 collective-permute-start.12
  156.8 11.8 %collective-permute-done.11 = bf16[96,2688]{1,0:T(8,128)(2,1)S(1)} collective-permute-done((bf16[96,2688]{1,0:T(8,128)(2,1)}, bf16[96,2688]{1,0:T(8,128)(2,1)S(1)}, u32[]{:S(2)}, u32[]{:S(2)}) %collective-permute-start.11) | collective-permute-done | bytes 516128 | tf_op jit(solution)/shard_map/gate_up/ppermute | solution.py:44
  168.6 9.9 %collective-permute-done.12 = bf16[96,2688]{1,0:T(8,128)(2,1)S(1)} collective-permute-done((bf16[96,2688]{1,0:T(8,128)(2,1)}, bf16[96,2688]{1,0:T(8,128)(2,1)S(1)}, u32[]{:S(2)}, u32[]{:S(2)}) %collective-permute-start.12) | collective-permute-done | bytes 516128 | tf_op jit(solution)/shard_map/gate_up/ppermute | solution.py:44
  180.4 4.1 %all-to-all-start.4 = ((bf16[4,24,2688]{2,1,0:T(8,128)(2,1)}), bf16[4,24,2688]{2,1,0:T(8,128)(2,1)S(1)}, u32[]{:S(2)}, u32[]{:S(2)}) async-start(bf16[4,24,2688]{2,1,0:T(8,128)(2,1)} %bitcast.9), calls=%async_computation.4 | async-start | bytes 1032192 | tf_op jit(solution)/shard_map/gate_up/all_to_all | solution.py:88
  184.8 3.5 %collective-permute-start.10 = (bf16[24,2816]{1,0:T(8,128)(2,1)S(1)}, bf16[24,2816]{1,0:T(8,128)(2,1)S(1)}, u32[]{:S(2)}, u32[]{:S(2)}) collective-permute-start(bf16[24,2816]{1,0:T(8,128)(2,1)S(1)} %get-tuple-element.42), channel_id=1, source_target_pairs={{0,96},{8,104},{16,112},{24,120},{32,0},{40,8},{48,16},{56,24},{64... | collective-permute-start | bytes 405512 | tf_op jit(solution)/shard_map/gate_up/ppermute | solution.py:44
  189.6 2.3 all-to-all-done.4
  191.9 5.1 %collective-permute-done.8 = bf16[24,2816]{1,0:T(8,128)(2,1)S(1)} collective-permute-done((bf16[24,2816]{1,0:T(8,128)(2,1)S(1)}, bf16[24,2816]{1,0:T(8,128)(2,1)S(1)}, u32[]{:S(2)}, u32[]{:S(2)}) %collective-permute-start.8) | collective-permute-done | bytes 135200 | tf_op jit(solution)/shard_map/gate_up/ppermute | solution.py:44
  197.6 30.1 %all_to_all.32 = bf16[16,24,2688]{2,1,0:T(8,128)(2,1)S(1)} all-to-all(bf16[16,24,2688]{2,1,0:T(8,128)(2,1)S(1)} %broadcast_in_dim.9), channel_id=1, replica_groups=mesh['batch'=16,'tensor'=8] {'batch'}, dimensions={0} | all-to-all | bytes 4128768 | tf_op jit(solution)/shard_map/gate_up/all_to_all | solution.py:22
  227.7 2.5 %spread_dot.3 = (f32[192,768]{1,0:T(8,128)S(1)}, f32[192,768]{1,0:T(8,128)S(1)}) custom-call(s32[16]{0:T(128)S(1)} %fusion.39.place_ref, bf16[384,2688]{1,0:T(8,128)(2,1)S(1)} %bitcast.24, bf16[2688,768]{1,0:T(8,128)(2,1)S(1)} %copy-done), custom_call_target="tpu_custom_call" | custom-call | flops 1585446912 | bytes 8552448 | tf_op jit(solution)/shard_map/down_projection/spread_dot/pallas_call | solution.py:323
  230.2 3.0 %collective-permute-start.14 = (f32[192,768]{1,0:T(8,128)S(1)}, f32[192,768]{1,0:T(8,128)S(1)}, u32[]{:S(2)}, u32[]{:S(2)}) collective-permute-start(f32[192,768]{1,0:T(8,128)S(1)} %get-tuple-element.48), channel_id=1, source_target_pairs={{0,1},{1,0},{2,3},{3,2},{4,5},{5,4},{6,7},{7,6},{8,9},{9,8},{10,11... | collective-permute-start | bytes 1769480 | tf_op jit(solution)/shard_map/down_projection/ppermute | solution.py:54
  235.0 2.7 %collective-permute-start.16 = (bf16[48,768]{1,0:T(8,128)(2,1)S(1)}, bf16[48,768]{1,0:T(8,128)(2,1)S(1)}, u32[]{:S(2)}, u32[]{:S(2)}) collective-permute-start(bf16[48,768]{1,0:T(8,128)(2,1)S(1)} %get-tuple-element.51), channel_id=1, source_target_pairs={{0,4},{1,5},{2,6},{3,7},{4,0},{5,1},{6,2},{7,3},{8,12},{9,13},{10,... | collective-permute-start | bytes 221192 | tf_op jit(solution)/shard_map/down_projection/ppermute | solution.py:49
  (94 shorter events, 34.7 us)
Async XLA Ops:
  3.6 29.4 %all-to-all-start = ((bf16[16,12,2,16,128]{4,3,2,1,0:T(8,128)(2,1)}), bf16[16,12,2,16,128]{4,3,2,1,0:T(8,128)(2,1)S(1)}, u32[]{:S(2)}, u32[]{:S(2)}) async-start(bf16[16,12,2,16,128]{4,3,2,1,0:T(8,128)(2,1)} %bitcast.22), calls=%async_computation | async-start | bytes 3145728 | tf_op jit(solution)/shard_map/cache_spread/all_to_all | solution.py:22
  34.0 58.3 %copy-start.5 = (f32[24,256]{1,0:T(8,128)S(1)}, f32[24,256]{1,0:T(8,128)}, u32[]{:S(2)}) copy-start(f32[24,256]{1,0:T(8,128)} %constant.191.clone.table_ref) | copy-start | bytes 73732
  114.3 6.7 %collective-permute-start = (f32[192,768]{1,0:T(8,128)S(1)}, f32[192,768]{1,0:T(8,128)S(1)}, u32[]{:S(2)}, u32[]{:S(2)}) collective-permute-start(f32[192,768]{1,0:T(8,128)S(1)} %get-tuple-element.33), channel_id=1, source_target_pairs={{0,1},{1,0},{2,3},{3,2},{4,5},{5,4},{6,7},{7,6},{8,9},{9,8},{10,11... | collective-permute-start | bytes 1769480 | tf_op jit(solution)/shard_map/output_projection/ppermute | solution.py:54
  121.0 5.9 %collective-permute-start.1 = (bf16[48,768]{1,0:T(8,128)(2,1)S(1)}, bf16[48,768]{1,0:T(8,128)(2,1)S(1)}, u32[]{:S(2)}, u32[]{:S(2)}) collective-permute-start(bf16[48,768]{1,0:T(8,128)(2,1)S(1)} %get-tuple-element.35), channel_id=1, source_target_pairs={{0,2},{1,3},{2,4},{3,5},{4,6},{5,7},{6,0},{7,1},{8,10},{9,11},{10,... | collective-permute-start | bytes 221192 | tf_op jit(solution)/shard_map/output_projection/ppermute | solution.py:49
  122.3 5.8 %collective-permute-start.2 = (bf16[48,768]{1,0:T(8,128)(2,1)S(1)}, bf16[48,768]{1,0:T(8,128)(2,1)S(1)}, u32[]{:S(2)}, u32[]{:S(2)}) collective-permute-start(bf16[48,768]{1,0:T(8,128)(2,1)S(1)} %get-tuple-element.36), channel_id=1, source_target_pairs={{0,4},{1,5},{2,6},{3,7},{4,0},{5,1},{6,2},{7,3},{8,12},{9,13},{10,... | collective-permute-start | bytes 221192 | tf_op jit(solution)/shard_map/output_projection/ppermute | solution.py:49
  124.8 3.5 %collective-permute-start.3 = (bf16[48,768]{1,0:T(8,128)(2,1)S(1)}, bf16[48,768]{1,0:T(8,128)(2,1)S(1)}, u32[]{:S(2)}, u32[]{:S(2)}) collective-permute-start(bf16[48,768]{1,0:T(8,128)(2,1)S(1)} %get-tuple-element.37), channel_id=1, source_target_pairs={{0,6},{1,7},{2,0},{3,1},{4,2},{5,3},{6,4},{7,5},{8,14},{9,15},{10,... | collective-permute-start | bytes 221192 | tf_op jit(solution)/shard_map/output_projection/ppermute | solution.py:49
  128.4 4.5 %collective-permute-start.4 = (bf16[48,768]{1,0:T(8,128)(2,1)S(1)}, bf16[48,768]{1,0:T(8,128)(2,1)S(1)}, u32[]{:S(2)}, u32[]{:S(2)}) collective-permute-start(bf16[48,768]{1,0:T(8,128)(2,1)S(1)} %get-tuple-element.60), channel_id=1, source_target_pairs={{0,2},{1,3},{2,4},{3,5},{4,6},{5,7},{6,0},{7,1},{8,10},{9,11},{10,... | collective-permute-start | bytes 221192 | tf_op jit(solution)/shard_map/output_projection/ppermute | solution.py:49
  128.5 5.8 %collective-permute-start.5 = (bf16[48,768]{1,0:T(8,128)(2,1)S(1)}, bf16[48,768]{1,0:T(8,128)(2,1)S(1)}, u32[]{:S(2)}, u32[]{:S(2)}) collective-permute-start(bf16[48,768]{1,0:T(8,128)(2,1)S(1)} %get-tuple-element.60), channel_id=1, source_target_pairs={{0,4},{1,5},{2,6},{3,7},{4,0},{5,1},{6,2},{7,3},{8,12},{9,13},{10,... | collective-permute-start | bytes 221192 | tf_op jit(solution)/shard_map/output_projection/ppermute | solution.py:49
  131.7 3.5 %collective-permute-start.6 = (bf16[48,768]{1,0:T(8,128)(2,1)S(1)}, bf16[48,768]{1,0:T(8,128)(2,1)S(1)}, u32[]{:S(2)}, u32[]{:S(2)}) collective-permute-start(bf16[48,768]{1,0:T(8,128)(2,1)S(1)} %get-tuple-element.60), channel_id=1, source_target_pairs={{0,6},{1,7},{2,0},{3,1},{4,2},{5,3},{6,4},{7,5},{8,14},{9,15},{10,... | collective-permute-start | bytes 221192 | tf_op jit(solution)/shard_map/output_projection/ppermute | solution.py:49
  135.2 4.9 %collective-permute-start.7 = (bf16[192,768]{1,0:T(8,128)(2,1)S(1)}, bf16[192,768]{1,0:T(8,128)(2,1)S(1)}, u32[]{:S(2)}, u32[]{:S(2)}) collective-permute-start(bf16[192,768]{1,0:T(8,128)(2,1)S(1)} %pad_maximum_fusion.near_ref), channel_id=1, source_target_pairs={{0,1},{1,0},{2,3},{3,2},{4,5},{5,4},{6,7},{7,6},{8,9},{9,8},{10,11... | collective-permute-start | bytes 884744 | tf_op jit(solution)/shard_map/output_projection/ppermute | solution.py:54
  149.7 29.6 %copy-start.6 = (bf16[96,2688]{1,0:T(8,128)(2,1)S(1)}, bf16[96,2688]{1,0:T(8,128)(2,1)}, u32[]{:S(2)}) copy-start(bf16[96,2688]{1,0:T(8,128)(2,1)} %get-tuple-element.43) | copy-start | bytes 1548292
  149.7 30.7 %all-to-all-start.3 = ((bf16[4,96,2816]{2,1,0:T(8,128)(2,1)}), bf16[4,96,2816]{2,1,0:T(8,128)(2,1)S(1)}, u32[]{:S(2)}, u32[]{:S(2)}) async-start(bf16[4,96,2816]{2,1,0:T(8,128)(2,1)} %get-tuple-element.38), calls=%async_computation.3 | async-start | bytes 4325376 | tf_op jit(solution)/shard_map/gate_up/all_to_all | solution.py:88
  153.5 15.1 %collective-permute-start.11 = (bf16[96,2688]{1,0:T(8,128)(2,1)}, bf16[96,2688]{1,0:T(8,128)(2,1)S(1)}, u32[]{:S(2)}, u32[]{:S(2)}) collective-permute-start(bf16[96,2688]{1,0:T(8,128)(2,1)} %get-tuple-element.44), channel_id=1, source_target_pairs={{0,32},{8,40},{16,48},{24,56},{32,64},{40,72},{48,80},{56,88},{64,... | collective-permute-start | bytes 1548296 | tf_op jit(solution)/shard_map/gate_up/ppermute | solution.py:44
  153.8 24.6 %collective-permute-start.12 = (bf16[96,2688]{1,0:T(8,128)(2,1)}, bf16[96,2688]{1,0:T(8,128)(2,1)S(1)}, u32[]{:S(2)}, u32[]{:S(2)}) collective-permute-start(bf16[96,2688]{1,0:T(8,128)(2,1)} %get-tuple-element.45), channel_id=1, source_target_pairs={{0,64},{8,72},{16,80},{24,88},{32,96},{40,104},{48,112},{56,120},{... | collective-permute-start | bytes 1548296 | tf_op jit(solution)/shard_map/gate_up/ppermute | solution.py:44
  155.6 23.7 %collective-permute-start.13 = (bf16[96,2688]{1,0:T(8,128)(2,1)S(1)}, bf16[96,2688]{1,0:T(8,128)(2,1)S(1)}, u32[]{:S(2)}, u32[]{:S(2)}) collective-permute-start(bf16[96,2688]{1,0:T(8,128)(2,1)S(1)} %copy-done.11), channel_id=1, source_target_pairs={{0,96},{8,104},{16,112},{24,120},{32,0},{40,8},{48,16},{56,24},{64... | collective-permute-start | bytes 1548296 | tf_op jit(solution)/shard_map/gate_up/ppermute | solution.py:44
  180.4 11.4 %all-to-all-start.4 = ((bf16[4,24,2688]{2,1,0:T(8,128)(2,1)}), bf16[4,24,2688]{2,1,0:T(8,128)(2,1)S(1)}, u32[]{:S(2)}, u32[]{:S(2)}) async-start(bf16[4,24,2688]{2,1,0:T(8,128)(2,1)} %bitcast.9), calls=%async_computation.4 | async-start | bytes 1032192 | tf_op jit(solution)/shard_map/gate_up/all_to_all | solution.py:88
  184.8 7.1 %collective-permute-start.10 = (bf16[24,2816]{1,0:T(8,128)(2,1)S(1)}, bf16[24,2816]{1,0:T(8,128)(2,1)S(1)}, u32[]{:S(2)}, u32[]{:S(2)}) collective-permute-start(bf16[24,2816]{1,0:T(8,128)(2,1)S(1)} %get-tuple-element.42), channel_id=1, source_target_pairs={{0,96},{8,104},{16,112},{24,120},{32,0},{40,8},{48,16},{56,24},{64... | collective-permute-start | bytes 405512 | tf_op jit(solution)/shard_map/gate_up/ppermute | solution.py:44
  188.3 8.7 %collective-permute-start.8 = (bf16[24,2816]{1,0:T(8,128)(2,1)S(1)}, bf16[24,2816]{1,0:T(8,128)(2,1)S(1)}, u32[]{:S(2)}, u32[]{:S(2)}) collective-permute-start(bf16[24,2816]{1,0:T(8,128)(2,1)S(1)} %get-tuple-element.40), channel_id=1, source_target_pairs={{0,32},{8,40},{16,48},{24,56},{32,64},{40,72},{48,80},{56,88},{64,... | collective-permute-start | bytes 405512 | tf_op jit(solution)/shard_map/gate_up/ppermute | solution.py:44
  188.3 8.7 %collective-permute-start.9 = (bf16[24,2816]{1,0:T(8,128)(2,1)S(1)}, bf16[24,2816]{1,0:T(8,128)(2,1)S(1)}, u32[]{:S(2)}, u32[]{:S(2)}) collective-permute-start(bf16[24,2816]{1,0:T(8,128)(2,1)S(1)} %get-tuple-element.41), channel_id=1, source_target_pairs={{0,64},{8,72},{16,80},{24,88},{32,96},{40,104},{48,112},{56,120},{... | collective-permute-start | bytes 405512 | tf_op jit(solution)/shard_map/gate_up/ppermute | solution.py:44
  197.6 30.1 %copy-start = (bf16[2688,768]{1,0:T(8,128)(2,1)S(1)}, bf16[2688,768]{1,0:T(8,128)(2,1)}, u32[]{:S(2)}) copy-start(bf16[2688,768]{1,0:T(8,128)(2,1)} %weight_ref.5) | copy-start | bytes 12386308
  230.2 4.6 %collective-permute-start.14 = (f32[192,768]{1,0:T(8,128)S(1)}, f32[192,768]{1,0:T(8,128)S(1)}, u32[]{:S(2)}, u32[]{:S(2)}) collective-permute-start(f32[192,768]{1,0:T(8,128)S(1)} %get-tuple-element.48), channel_id=1, source_target_pairs={{0,1},{1,0},{2,3},{3,2},{4,5},{5,4},{6,7},{7,6},{8,9},{9,8},{10,11... | collective-permute-start | bytes 1769480 | tf_op jit(solution)/shard_map/down_projection/ppermute | solution.py:54
  234.9 4.5 %collective-permute-start.15 = (bf16[48,768]{1,0:T(8,128)(2,1)S(1)}, bf16[48,768]{1,0:T(8,128)(2,1)S(1)}, u32[]{:S(2)}, u32[]{:S(2)}) collective-permute-start(bf16[48,768]{1,0:T(8,128)(2,1)S(1)} %get-tuple-element.50), channel_id=1, source_target_pairs={{0,2},{1,3},{2,4},{3,5},{4,6},{5,7},{6,0},{7,1},{8,10},{9,11},{10,... | collective-permute-start | bytes 221192 | tf_op jit(solution)/shard_map/down_projection/ppermute | solution.py:49
  235.0 6.0 %collective-permute-start.16 = (bf16[48,768]{1,0:T(8,128)(2,1)S(1)}, bf16[48,768]{1,0:T(8,128)(2,1)S(1)}, u32[]{:S(2)}, u32[]{:S(2)}) collective-permute-start(bf16[48,768]{1,0:T(8,128)(2,1)S(1)} %get-tuple-element.51), channel_id=1, source_target_pairs={{0,4},{1,5},{2,6},{3,7},{4,0},{5,1},{6,2},{7,3},{8,12},{9,13},{10,... | collective-permute-start | bytes 221192 | tf_op jit(solution)/shard_map/down_projection/ppermute | solution.py:49
  237.7 4.1 %collective-permute-start.17 = (bf16[48,768]{1,0:T(8,128)(2,1)S(1)}, bf16[48,768]{1,0:T(8,128)(2,1)S(1)}, u32[]{:S(2)}, u32[]{:S(2)}) collective-permute-start(bf16[48,768]{1,0:T(8,128)(2,1)S(1)} %get-tuple-element.52), channel_id=1, source_target_pairs={{0,6},{1,7},{2,0},{3,1},{4,2},{5,3},{6,4},{7,5},{8,14},{9,15},{10,... | collective-permute-start | bytes 221192 | tf_op jit(solution)/shard_map/down_projection/ppermute | solution.py:49
  (10 other events, 67.3 us)

commit v5 on v4

--- a/solution.py
+++ b/solution.py
@@ -20,12 +20,6 @@
 
 def exchange(blocks, axis):
     return lax.all_to_all(blocks, axis, split_axis=0, concat_axis=0, tiled=True)
-
-
-def gather_all(block, axis):
-    copies = jnp.broadcast_to(block[None], (lax.axis_size(axis),) + block.shape)
-    gathered = exchange(lax.optimization_barrier(copies), axis)
-    return gathered.reshape((-1,) + block.shape[1:])
 
 
 def after(value, earlier):
@@ -90,20 +84,85 @@
     )
 
 
+def exchange_minor(blocks):
+    side = math.isqrt(lax.axis_size("batch"))
+    groups = [[major * side + minor for minor in range(side)] for major in range(side)]
+    return lax.all_to_all(
+        blocks, "batch", split_axis=0, concat_axis=0, tiled=True, axis_index_groups=groups
+    )
+
+
 def add_along(own, terms):
     return functools.reduce(lambda total, term: total + term.astype(jnp.float32), terms, own)
+
+
+def stack_kernel(*refs):
+    sources, target = refs[:-1], refs[-1]
+    total = sources[0][...].astype(jnp.float32)
+    for source in sources[1:]:
+        total = total + source[...].astype(jnp.float32)
+    rows = target.shape[1]
+    for place in range(target.shape[0]):
+        target[place] = total[place * rows : (place + 1) * rows].astype(target.dtype)
+
+
+def fold_stacked(sources):
+    rows, columns = sources[0].shape
+    shape = (len(sources), rows // len(sources), columns)
+    whole = pl.BlockSpec(memory_space=pltpu.VMEM)
+    return pl.pallas_call(
+        stack_kernel,
+        out_shape=jax.ShapeDtypeStruct(shape, jnp.bfloat16),
+        in_specs=[whole] * len(sources),
+        out_specs=whole,
+        compiler_params=pltpu.CompilerParams(vmem_limit_bytes=32 * MIB),
+        cost_estimate=pl.CostEstimate(flops=1, bytes_accessed=1, transcendentals=0),
+        name="fold_stacked",
+    )(*sources)
+
+
+def activate_kernel(model, own_ref, *refs):
+    terms, crossed_ref, out_ref = refs[:-2], refs[-2], refs[-1]
+    hidden = out_ref.shape[2]
+    gates = own_ref[...]
+    for term in terms:
+        gates = gates + term[...].astype(jnp.float32)
+    ups = crossed_ref[0].astype(jnp.float32)
+    for place in range(1, crossed_ref.shape[0]):
+        ups = ups + crossed_ref[place].astype(jnp.float32)
+    mean = (gates[:, hidden : hidden + 1] + gates[:, hidden + 1 : hidden + 2]) / model
+    scale = lax.rsqrt(mean + norm_eps)
+    gates, ups = gates[:, :hidden] * scale, ups * scale
+    activated = (gates / (1.0 + jnp.exp(-gates)) * ups).astype(jnp.bfloat16)
+    for copy in range(out_ref.shape[0]):
+        out_ref[copy] = activated
+
+
+def activate(own, terms, crossed, model, copies):
+    _, rows, hidden = crossed.shape
+    whole = pl.BlockSpec(memory_space=pltpu.VMEM)
+    return pl.pallas_call(
+        functools.partial(activate_kernel, model),
+        out_shape=jax.ShapeDtypeStruct((copies, rows, hidden), jnp.bfloat16),
+        in_specs=[whole] * (2 + len(terms)),
+        out_specs=whole,
+        compiler_params=pltpu.CompilerParams(vmem_limit_bytes=32 * MIB),
+        cost_estimate=pl.CostEstimate(
+            flops=8 * rows * hidden,
+            bytes_accessed=2 * copies * rows * hidden,
+            transcendentals=rows * hidden,
+        ),
+        name="activate",
+    )(own, *terms, crossed)
 
 
 def add_crossed(first, second):
     side = len(second)
     others = range(1, side)
     moved = [second[0]] + [shift_along(second[count], 0, count) for count in others]
-    arrived = exchange_minor(first)
-    summed = fold([arrived], side)
-    first = add_along(summed[0], [shift_along(summed[count], 0, count) for count in others])
-    crossed = add_along(moved[0].astype(jnp.float32), moved[1:]).astype(jnp.bfloat16)
-    crossed = exchange_minor(crossed.reshape((side, -1) + crossed.shape[1:]))
-    return first, jnp.sum(crossed.astype(jnp.float32), axis=0)
+    summed = fold([exchange_minor(first)], side)
+    terms = [shift_along(summed[count], 0, count) for count in others]
+    return summed[0], terms, exchange_minor(fold_stacked(moved))
 
 
 def add_over_tensor(kept, sent):
@@ -302,7 +361,7 @@
             transcendentals=0,
         ),
         name="gate_up",
-    )(order, near, far, gain.reshape(1, -1), weight)
+    )(order, near, far, gain, weight)
 
 
 def spread_dot_kernel(place_ref, rows_ref, weight_ref, kept_ref, sent_ref, total_ref):
@@ -314,7 +373,7 @@
         total_ref[target, :] = values[at * rows : (at + 1) * rows]
     half = kept_ref.shape[0]
     kept_ref[...] = total_ref[:half]
-    sent_ref[...] = total_ref[half:]
+    sent_ref[...] = total_ref[half:].astype(jnp.bfloat16)
 
 
 def spread_dot(places, values, weight):
@@ -322,7 +381,9 @@
     whole = pl.BlockSpec(memory_space=pltpu.VMEM)
     return pl.pallas_call(
         spread_dot_kernel,
-        out_shape=[jax.ShapeDtypeStruct((total // 2, width), jnp.float32)] * 2,
+        out_shape=[
+            jax.ShapeDtypeStruct((total // 2, width), kind) for kind in (jnp.float32, jnp.bfloat16)
+        ],
         in_specs=[pl.BlockSpec(memory_space=pltpu.SMEM), whole, whole],
         out_specs=[whole] * 2,
         scratch_shapes=[pltpu.VMEM((total, width), jnp.float32)],
@@ -557,7 +618,8 @@
         )
 
     with jax.named_scope("cache_return"):
-        ready = after(wanted, (lifted_order, targets))
+        lift_gain = ffn_gain.reshape(1, -1)
+        ready = after(wanted, (lifted_order, targets, lift_gain))
         returned = exchange(pick_rows(spread, ready, sums), "batch")
 
     with jax.named_scope("attention"):
@@ -585,13 +647,10 @@
         far = swap_cores(near)
 
     with jax.named_scope("gate_up"):
-        blocks = gate_up(side, lifted_order, near, far, ffn_gain, gateup_weight, 768)
-        gates, ups = add_crossed(blocks[0], blocks[1:])
-        mean = (gates[:, hidden] + gates[:, hidden + 1]) / model
-        scale = lax.rsqrt(mean + norm_eps)[:, None]
-        gates, ups = gates[:, :hidden] * scale, ups * scale
-        activated = (jax.nn.silu(gates) * ups).astype(jnp.bfloat16)
-        activated = gather_all(activated, "batch")
+        blocks = gate_up(side, lifted_order, near, far, lift_gain, gateup_weight, 768)
+        gates, terms, ups = add_crossed(blocks[0], blocks[1:])
+        activated = activate(gates, terms, ups, model, batches)
+        activated = exchange(activated, "batch").reshape(total, hidden)
 
     with jax.named_scope("down_projection"):
         lowered = add_over_tensor(*spread_dot(targets, activated, down_weight))

time: 243 us -> 242 us (level)
  transfers between devices with their start and end apart: 21 -> 21, of which waited for: 17 -> 17; matrix products, arithmetic and copies ran while one was open for 3% -> 3% of each run, Pallas kernels for 1% -> 2%
where the time goes in v5:
time: 242 us
  blocking collectives  107 us (44%)
  waiting for transfers between devices  50.4 us (21%)
  starting transfers between devices  48.8 us (20%)
  Pallas kernels  20.5 us (8%)
  local copies, waits for them, and re-layouts  11.6 us (5%)
  other arithmetic  2.79 us (1%)
    all_to_all x3, blocking collectives, exchange(): return lax.all_to_all(blocks, axis, split_axis=0, concat_axis=0, tiled=True)  107 us
    ppermute x6, waiting for transfers between devices, shift_along(): return lax.ppermute(block, 'batch', pairs)  27.8 us
    ppermute x9, starting transfers between devices, shift_chips(): lax.ppermute(block, 'tensor', [(at, (at + 2 * count) % size) for at in ra...  12.5 us
    ppermute x3, starting transfers between devices, swap_cores(): return lax.ppermute(block, 'tensor', [(at, at ^ 1) for at in range(size)])  11.8 us
    all_to_all x1, waiting for transfers between devices, exchange(): return lax.all_to_all(blocks, axis, split_axis=0, concat_axis=0, tiled=True)  9.76 us
    pallas_call x1, Pallas kernels, gate_up(): pl.pallas_call(functools.partial(gate_up_kernel, side, spans), out_shape=...  8.85 us
    all_to_all x1, starting transfers between devices, exchange(): return lax.all_to_all(blocks, axis, split_axis=0, concat_axis=0, tiled=True)  8.73 us
    ppermute x6, starting transfers between devices, shift_along(): return lax.ppermute(block, 'batch', pairs)  7.99 us
  transfers between devices with their start and end apart: 21, of which 17 were waited for; matrix products, arithmetic and copies ran while one was open for 3% of the time, Pallas kernels for 2%

profile of v5, /device:TPU:1, one launch (start us, length us, event | category | flops | bytes accessed | tf_op | source)
XLA Modules:
  0.0 241.6 jit_solution(4172870491782280694)
XLA Ops:
  0.6 3.0 %copy.29 = bf16[2,12,16,16,128]{4,3,0,1,2:T(8,128)(2,1)} copy(bf16[2,12,16,16,128]{4,3,2,1,0:T(8,128)(2,1)} %bitcast.27) | data formatting | bytes 3145728 | tf_op jit(solution)/shard_map/cache_spread/reshape | solution.py:586
  3.6 8.7 %all-to-all-start = ((bf16[16,12,2,16,128]{4,3,2,1,0:T(8,128)(2,1)}), bf16[16,12,2,16,128]{4,3,2,1,0:T(8,128)(2,1)S(1)}, u32[]{:S(2)}, u32[]{:S(2)}) async-start(bf16[16,12,2,16,128]{4,3,2,1,0:T(8,128)(2,1)} %bitcast.21), calls=%async_computation | async-start | bytes 3145728 | tf_op jit(solution)/shard_map/cache_spread/all_to_all | solution.py:22
  20.7 2.5 %project_rows.1.sum_ref = bf16[16,384,128]{2,1,0:T(8,128)(2,1)S(1)} custom-call(s32[384,1]{1,0:T(8,128)S(1)} %fusion.13.order_ref, s32[192,1]{1,0:T(8,128)S(1)} %copy.22.parent_ref, bf16[2,192,768]{2,1,0:T(8,128)(2,1)S(1)} %copy-done.3, bf16[1,768]{1,0:T(2,128)(2,1)S(1)} %reshape.490.gain_ref, bf16[768,1536]{1,0:T(8,128)(2,1)S(1)} %copy-done.1, ...), custom_call_target="tpu_custom_call" | custom-call | flops 1207959552 | bytes 4718592 | tf_op jit(solution)/shard_map/project/project_rows/pallas_call | solution.py:254
  23.2 9.8 %all-to-all-done = bf16[16,12,2,16,128]{4,3,2,1,0:T(8,128)(2,1)S(1)} async-done(((bf16[16,12,2,16,128]{4,3,2,1,0:T(8,128)(2,1)}), bf16[16,12,2,16,128]{4,3,2,1,0:T(8,128)(2,1)S(1)}, u32[]{:S(2)}, u32[]{:S(2)}) %all-to-all-start) | async-done | bytes 1572896 | tf_op jit(solution)/shard_map/cache_spread/all_to_all | solution.py:22
  34.0 58.3 %all_to_all.30.cache_ref = bf16[16,1152,128]{2,1,0:T(8,128)(2,1)S(1)} all-to-all(bf16[16,1152,128]{2,1,0:T(8,128)(2,1)S(1)} %pick_rows.1), channel_id=1, replica_groups=mesh['batch'=16,'tensor'=8] {'batch'}, dimensions={0} | all-to-all | bytes 9437184 | tf_op jit(solution)/shard_map/cache_return/all_to_all | solution.py:22
  92.3 2.1 attend.1
  94.5 18.1 %all_to_all.31 = bf16[16,24,1536]{2,1,0:T(8,128)(2,1)S(1)} all-to-all(bf16[16,24,1536]{2,1,0:T(8,128)(2,1)S(1)} %get-tuple-element.31), channel_id=1, replica_groups=mesh['batch'=16,'tensor'=8] {'batch'}, dimensions={0} | all-to-all | bytes 2359296 | tf_op jit(solution)/shard_map/attention/all_to_all | solution.py:22
  114.3 5.1 %collective-permute-start = (bf16[192,768]{1,0:T(8,128)(2,1)S(1)}, bf16[192,768]{1,0:T(8,128)(2,1)S(1)}, u32[]{:S(2)}, u32[]{:S(2)}) collective-permute-start(bf16[192,768]{1,0:T(8,128)(2,1)S(1)} %get-tuple-element.33), channel_id=1, source_target_pairs={{0,1},{1,0},{2,3},{3,2},{4,5},{5,4},{6,7},{7,6},{8,9},{9,8},{10,11... | collective-permute-start | bytes 884744 | tf_op jit(solution)/shard_map/output_projection/ppermute | solution.py:48
  121.9 2.4 %collective-permute-start.2 = (bf16[48,768]{1,0:T(8,128)(2,1)S(1)}, bf16[48,768]{1,0:T(8,128)(2,1)S(1)}, u32[]{:S(2)}, u32[]{:S(2)}) collective-permute-start(bf16[48,768]{1,0:T(8,128)(2,1)S(1)} %get-tuple-element.36), channel_id=1, source_target_pairs={{0,4},{1,5},{2,6},{3,7},{4,0},{5,1},{6,2},{7,3},{8,12},{9,13},{10,... | collective-permute-start | bytes 221192 | tf_op jit(solution)/shard_map/output_projection/ppermute | solution.py:43
  128.0 3.2 %collective-permute-start.5 = (bf16[48,768]{1,0:T(8,128)(2,1)S(1)}, bf16[48,768]{1,0:T(8,128)(2,1)S(1)}, u32[]{:S(2)}, u32[]{:S(2)}) collective-permute-start(bf16[48,768]{1,0:T(8,128)(2,1)S(1)} %get-tuple-element.60), channel_id=1, source_target_pairs={{0,4},{1,5},{2,6},{3,7},{4,0},{5,1},{6,2},{7,3},{8,12},{9,13},{10,... | collective-permute-start | bytes 221192 | tf_op jit(solution)/shard_map/output_projection/ppermute | solution.py:43
  134.8 3.7 %collective-permute-start.7 = (bf16[192,768]{1,0:T(8,128)(2,1)S(1)}, bf16[192,768]{1,0:T(8,128)(2,1)S(1)}, u32[]{:S(2)}, u32[]{:S(2)}) collective-permute-start(bf16[192,768]{1,0:T(8,128)(2,1)S(1)} %pad_maximum_fusion.near_ref), channel_id=1, source_target_pairs={{0,1},{1,0},{2,3},{3,2},{4,5},{5,4},{6,7},{7,6},{8,9},{9,8},{10,11... | collective-permute-start | bytes 884744 | tf_op jit(solution)/shard_map/output_projection/ppermute | solution.py:48
  140.4 8.9 %gate_up.1 = (bf16[4,96,2816]{2,1,0:T(8,128)(2,1)}, bf16[96,2688]{1,0:T(8,128)(2,1)}, bf16[96,2688]{1,0:T(8,128)(2,1)}, bf16[96,2688]{1,0:T(8,128)(2,1)}, bf16[96,2688]{1,0:T(8,128)(2,1)}) custom-call(s32[384,1]{1,0:T(8,128)} %fusion.26.order_ref, bf16[192,768]{1,0:T(8,128)(2,1)} %copy-done.7, bf16[192,768]{1,0:T(8,128)(2,1)} %copy-done.12, ...), custom_call_target="tpu_custom_call" | custom-call | flops 3170893824 | bytes 12386304 | tf_op jit(solution)/shard_map/gate_up/gate_up/pallas_call | solution.py:343
  149.3 3.8 %all-to-all-start.3 = ((bf16[4,96,2816]{2,1,0:T(8,128)(2,1)}), bf16[4,96,2816]{2,1,0:T(8,128)(2,1)S(1)}, u32[]{:S(2)}, u32[]{:S(2)}) async-start(bf16[4,96,2816]{2,1,0:T(8,128)(2,1)} %get-tuple-element.38), calls=%async_computation.3 | async-start | bytes 4325376 | tf_op jit(solution)/shard_map/gate_up/all_to_all | solution.py:90
  153.4 1.8 collective-permute-start.12
  156.3 11.8 %collective-permute-done.11.refs_1_ = bf16[96,2688]{1,0:T(8,128)(2,1)S(1)} collective-permute-done((bf16[96,2688]{1,0:T(8,128)(2,1)}, bf16[96,2688]{1,0:T(8,128)(2,1)S(1)}, u32[]{:S(2)}, u32[]{:S(2)}) %collective-permute-start.11) | collective-permute-done | bytes 516128 | tf_op jit(solution)/shard_map/gate_up/ppermute | solution.py:38
  168.1 9.9 %collective-permute-done.12.refs_2_ = bf16[96,2688]{1,0:T(8,128)(2,1)S(1)} collective-permute-done((bf16[96,2688]{1,0:T(8,128)(2,1)}, bf16[96,2688]{1,0:T(8,128)(2,1)S(1)}, u32[]{:S(2)}, u32[]{:S(2)}) %collective-permute-start.12) | collective-permute-done | bytes 516128 | tf_op jit(solution)/shard_map/gate_up/ppermute | solution.py:38
  180.0 4.0 %all-to-all-start.4 = ((bf16[4,24,2688]{2,1,0:T(8,128)(2,1)}), bf16[4,24,2688]{2,1,0:T(8,128)(2,1)S(1)}, u32[]{:S(2)}, u32[]{:S(2)}) async-start(bf16[4,24,2688]{2,1,0:T(8,128)(2,1)} %fold_stacked.1), calls=%async_computation.4 | async-start | bytes 1032192 | tf_op jit(solution)/shard_map/gate_up/all_to_all | solution.py:90
  184.3 3.5 %collective-permute-start.10 = (bf16[24,2816]{1,0:T(8,128)(2,1)S(1)}, bf16[24,2816]{1,0:T(8,128)(2,1)S(1)}, u32[]{:S(2)}, u32[]{:S(2)}) collective-permute-start(bf16[24,2816]{1,0:T(8,128)(2,1)S(1)} %get-tuple-element.42), channel_id=1, source_target_pairs={{0,96},{8,104},{16,112},{24,120},{32,0},{40,8},{48,16},{56,24},{64... | collective-permute-start | bytes 405512 | tf_op jit(solution)/shard_map/gate_up/ppermute | solution.py:38
  189.1 2.3 all-to-all-done.4.refs_3_
  191.3 5.2 %collective-permute-done.8.refs_0_ = bf16[24,2816]{1,0:T(8,128)(2,1)S(1)} collective-permute-done((bf16[24,2816]{1,0:T(8,128)(2,1)S(1)}, bf16[24,2816]{1,0:T(8,128)(2,1)S(1)}, u32[]{:S(2)}, u32[]{:S(2)}) %collective-permute-start.8) | collective-permute-done | bytes 135200 | tf_op jit(solution)/shard_map/gate_up/ppermute | solution.py:38
  197.0 30.1 %all_to_all.32 = bf16[16,24,2688]{2,1,0:T(8,128)(2,1)S(1)} all-to-all(bf16[16,24,2688]{2,1,0:T(8,128)(2,1)S(1)} %activate.1), channel_id=1, replica_groups=mesh['batch'=16,'tensor'=8] {'batch'}, dimensions={0} | all-to-all | bytes 4128768 | tf_op jit(solution)/shard_map/gate_up/all_to_all | solution.py:22
  227.1 2.4 %spread_dot.3 = (f32[192,768]{1,0:T(8,128)S(1)}, bf16[192,768]{1,0:T(8,128)(2,1)S(1)}) custom-call(s32[16]{0:T(128)S(1)} %fusion.35.place_ref, bf16[384,2688]{1,0:T(8,128)(2,1)S(1)} %bitcast.23, bf16[2688,768]{1,0:T(8,128)(2,1)S(1)} %copy-done), custom_call_target="tpu_custom_call" | custom-call | flops 1585446912 | bytes 8552448 | tf_op jit(solution)/shard_map/down_projection/spread_dot/pallas_call | solution.py:382
  229.5 3.0 %collective-permute-start.14 = (bf16[192,768]{1,0:T(8,128)(2,1)S(1)}, bf16[192,768]{1,0:T(8,128)(2,1)S(1)}, u32[]{:S(2)}, u32[]{:S(2)}) collective-permute-start(bf16[192,768]{1,0:T(8,128)(2,1)S(1)} %get-tuple-element.48), channel_id=1, source_target_pairs={{0,1},{1,0},{2,3},{3,2},{4,5},{5,4},{6,7},{7,6},{8,9},{9,8},{10,11... | collective-permute-start | bytes 884744 | tf_op jit(solution)/shard_map/down_projection/ppermute | solution.py:48
  233.9 2.8 %collective-permute-start.16 = (bf16[48,768]{1,0:T(8,128)(2,1)S(1)}, bf16[48,768]{1,0:T(8,128)(2,1)S(1)}, u32[]{:S(2)}, u32[]{:S(2)}) collective-permute-start(bf16[48,768]{1,0:T(8,128)(2,1)S(1)} %get-tuple-element.51), channel_id=1, source_target_pairs={{0,4},{1,5},{2,6},{3,7},{4,0},{5,1},{6,2},{7,3},{8,12},{9,13},{10,... | collective-permute-start | bytes 221192 | tf_op jit(solution)/shard_map/down_projection/ppermute | solution.py:43
  (90 shorter events, 34.2 us)
Async XLA Ops:
  3.6 29.4 %all-to-all-start = ((bf16[16,12,2,16,128]{4,3,2,1,0:T(8,128)(2,1)}), bf16[16,12,2,16,128]{4,3,2,1,0:T(8,128)(2,1)S(1)}, u32[]{:S(2)}, u32[]{:S(2)}) async-start(bf16[16,12,2,16,128]{4,3,2,1,0:T(8,128)(2,1)} %bitcast.21), calls=%async_computation | async-start | bytes 3145728 | tf_op jit(solution)/shard_map/cache_spread/all_to_all | solution.py:22
  34.0 58.3 %copy-start.6 = (f32[24,256]{1,0:T(8,128)S(1)}, f32[24,256]{1,0:T(8,128)}, u32[]{:S(2)}) copy-start(f32[24,256]{1,0:T(8,128)} %constant.181.clone.table_ref) | copy-start | bytes 73732
  114.3 6.3 %collective-permute-start = (bf16[192,768]{1,0:T(8,128)(2,1)S(1)}, bf16[192,768]{1,0:T(8,128)(2,1)S(1)}, u32[]{:S(2)}, u32[]{:S(2)}) collective-permute-start(bf16[192,768]{1,0:T(8,128)(2,1)S(1)} %get-tuple-element.33), channel_id=1, source_target_pairs={{0,1},{1,0},{2,3},{3,2},{4,5},{5,4},{6,7},{7,6},{8,9},{9,8},{10,11... | collective-permute-start | bytes 884744 | tf_op jit(solution)/shard_map/output_projection/ppermute | solution.py:48
  120.6 5.9 %collective-permute-start.1 = (bf16[48,768]{1,0:T(8,128)(2,1)S(1)}, bf16[48,768]{1,0:T(8,128)(2,1)S(1)}, u32[]{:S(2)}, u32[]{:S(2)}) collective-permute-start(bf16[48,768]{1,0:T(8,128)(2,1)S(1)} %get-tuple-element.35), channel_id=1, source_target_pairs={{0,2},{1,3},{2,4},{3,5},{4,6},{5,7},{6,0},{7,1},{8,10},{9,11},{10,... | collective-permute-start | bytes 221192 | tf_op jit(solution)/shard_map/output_projection/ppermute | solution.py:43
  121.9 5.8 %collective-permute-start.2 = (bf16[48,768]{1,0:T(8,128)(2,1)S(1)}, bf16[48,768]{1,0:T(8,128)(2,1)S(1)}, u32[]{:S(2)}, u32[]{:S(2)}) collective-permute-start(bf16[48,768]{1,0:T(8,128)(2,1)S(1)} %get-tuple-element.36), channel_id=1, source_target_pairs={{0,4},{1,5},{2,6},{3,7},{4,0},{5,1},{6,2},{7,3},{8,12},{9,13},{10,... | collective-permute-start | bytes 221192 | tf_op jit(solution)/shard_map/output_projection/ppermute | solution.py:43
  124.3 3.5 %collective-permute-start.3 = (bf16[48,768]{1,0:T(8,128)(2,1)S(1)}, bf16[48,768]{1,0:T(8,128)(2,1)S(1)}, u32[]{:S(2)}, u32[]{:S(2)}) collective-permute-start(bf16[48,768]{1,0:T(8,128)(2,1)S(1)} %get-tuple-element.37), channel_id=1, source_target_pairs={{0,6},{1,7},{2,0},{3,1},{4,2},{5,3},{6,4},{7,5},{8,14},{9,15},{10,... | collective-permute-start | bytes 221192 | tf_op jit(solution)/shard_map/output_projection/ppermute | solution.py:43
  127.9 4.5 %collective-permute-start.4 = (bf16[48,768]{1,0:T(8,128)(2,1)S(1)}, bf16[48,768]{1,0:T(8,128)(2,1)S(1)}, u32[]{:S(2)}, u32[]{:S(2)}) collective-permute-start(bf16[48,768]{1,0:T(8,128)(2,1)S(1)} %get-tuple-element.60), channel_id=1, source_target_pairs={{0,2},{1,3},{2,4},{3,5},{4,6},{5,7},{6,0},{7,1},{8,10},{9,11},{10,... | collective-permute-start | bytes 221192 | tf_op jit(solution)/shard_map/output_projection/ppermute | solution.py:43
  128.0 5.8 %collective-permute-start.5 = (bf16[48,768]{1,0:T(8,128)(2,1)S(1)}, bf16[48,768]{1,0:T(8,128)(2,1)S(1)}, u32[]{:S(2)}, u32[]{:S(2)}) collective-permute-start(bf16[48,768]{1,0:T(8,128)(2,1)S(1)} %get-tuple-element.60), channel_id=1, source_target_pairs={{0,4},{1,5},{2,6},{3,7},{4,0},{5,1},{6,2},{7,3},{8,12},{9,13},{10,... | collective-permute-start | bytes 221192 | tf_op jit(solution)/shard_map/output_projection/ppermute | solution.py:43
  131.3 3.5 %collective-permute-start.6 = (bf16[48,768]{1,0:T(8,128)(2,1)S(1)}, bf16[48,768]{1,0:T(8,128)(2,1)S(1)}, u32[]{:S(2)}, u32[]{:S(2)}) collective-permute-start(bf16[48,768]{1,0:T(8,128)(2,1)S(1)} %get-tuple-element.60), channel_id=1, source_target_pairs={{0,6},{1,7},{2,0},{3,1},{4,2},{5,3},{6,4},{7,5},{8,14},{9,15},{10,... | collective-permute-start | bytes 221192 | tf_op jit(solution)/shard_map/output_projection/ppermute | solution.py:43
  134.8 4.9 %collective-permute-start.7 = (bf16[192,768]{1,0:T(8,128)(2,1)S(1)}, bf16[192,768]{1,0:T(8,128)(2,1)S(1)}, u32[]{:S(2)}, u32[]{:S(2)}) collective-permute-start(bf16[192,768]{1,0:T(8,128)(2,1)S(1)} %pad_maximum_fusion.near_ref), channel_id=1, source_target_pairs={{0,1},{1,0},{2,3},{3,2},{4,5},{5,4},{6,7},{7,6},{8,9},{9,8},{10,11... | collective-permute-start | bytes 884744 | tf_op jit(solution)/shard_map/output_projection/ppermute | solution.py:48
  149.3 29.6 %copy-start.4 = (bf16[96,2688]{1,0:T(8,128)(2,1)S(1)}, bf16[96,2688]{1,0:T(8,128)(2,1)}, u32[]{:S(2)}) copy-start(bf16[96,2688]{1,0:T(8,128)(2,1)} %get-tuple-element.43.refs_0_) | copy-start | bytes 1548292
  149.3 30.7 %all-to-all-start.3 = ((bf16[4,96,2816]{2,1,0:T(8,128)(2,1)}), bf16[4,96,2816]{2,1,0:T(8,128)(2,1)S(1)}, u32[]{:S(2)}, u32[]{:S(2)}) async-start(bf16[4,96,2816]{2,1,0:T(8,128)(2,1)} %get-tuple-element.38), calls=%async_computation.3 | async-start | bytes 4325376 | tf_op jit(solution)/shard_map/gate_up/all_to_all | solution.py:90
  153.1 15.1 %collective-permute-start.11 = (bf16[96,2688]{1,0:T(8,128)(2,1)}, bf16[96,2688]{1,0:T(8,128)(2,1)S(1)}, u32[]{:S(2)}, u32[]{:S(2)}) collective-permute-start(bf16[96,2688]{1,0:T(8,128)(2,1)} %get-tuple-element.44), channel_id=1, source_target_pairs={{0,32},{8,40},{16,48},{24,56},{32,64},{40,72},{48,80},{56,88},{64,... | collective-permute-start | bytes 1548296 | tf_op jit(solution)/shard_map/gate_up/ppermute | solution.py:38
  153.4 24.6 %collective-permute-start.12 = (bf16[96,2688]{1,0:T(8,128)(2,1)}, bf16[96,2688]{1,0:T(8,128)(2,1)S(1)}, u32[]{:S(2)}, u32[]{:S(2)}) collective-permute-start(bf16[96,2688]{1,0:T(8,128)(2,1)} %get-tuple-element.45), channel_id=1, source_target_pairs={{0,64},{8,72},{16,80},{24,88},{32,96},{40,104},{48,112},{56,120},{... | collective-permute-start | bytes 1548296 | tf_op jit(solution)/shard_map/gate_up/ppermute | solution.py:38
  155.2 23.7 %collective-permute-start.13 = (bf16[96,2688]{1,0:T(8,128)(2,1)S(1)}, bf16[96,2688]{1,0:T(8,128)(2,1)S(1)}, u32[]{:S(2)}, u32[]{:S(2)}) collective-permute-start(bf16[96,2688]{1,0:T(8,128)(2,1)S(1)} %copy-done.11), channel_id=1, source_target_pairs={{0,96},{8,104},{16,112},{24,120},{32,0},{40,8},{48,16},{56,24},{64... | collective-permute-start | bytes 1548296 | tf_op jit(solution)/shard_map/gate_up/ppermute | solution.py:38
  180.0 11.3 %all-to-all-start.4 = ((bf16[4,24,2688]{2,1,0:T(8,128)(2,1)}), bf16[4,24,2688]{2,1,0:T(8,128)(2,1)S(1)}, u32[]{:S(2)}, u32[]{:S(2)}) async-start(bf16[4,24,2688]{2,1,0:T(8,128)(2,1)} %fold_stacked.1), calls=%async_computation.4 | async-start | bytes 1032192 | tf_op jit(solution)/shard_map/gate_up/all_to_all | solution.py:90
  184.3 7.0 %collective-permute-start.10 = (bf16[24,2816]{1,0:T(8,128)(2,1)S(1)}, bf16[24,2816]{1,0:T(8,128)(2,1)S(1)}, u32[]{:S(2)}, u32[]{:S(2)}) collective-permute-start(bf16[24,2816]{1,0:T(8,128)(2,1)S(1)} %get-tuple-element.42), channel_id=1, source_target_pairs={{0,96},{8,104},{16,112},{24,120},{32,0},{40,8},{48,16},{56,24},{64... | collective-permute-start | bytes 405512 | tf_op jit(solution)/shard_map/gate_up/ppermute | solution.py:38
  187.8 8.7 %collective-permute-start.8 = (bf16[24,2816]{1,0:T(8,128)(2,1)S(1)}, bf16[24,2816]{1,0:T(8,128)(2,1)S(1)}, u32[]{:S(2)}, u32[]{:S(2)}) collective-permute-start(bf16[24,2816]{1,0:T(8,128)(2,1)S(1)} %get-tuple-element.40), channel_id=1, source_target_pairs={{0,32},{8,40},{16,48},{24,56},{32,64},{40,72},{48,80},{56,88},{64,... | collective-permute-start | bytes 405512 | tf_op jit(solution)/shard_map/gate_up/ppermute | solution.py:38
  187.8 8.7 %collective-permute-start.9 = (bf16[24,2816]{1,0:T(8,128)(2,1)S(1)}, bf16[24,2816]{1,0:T(8,128)(2,1)S(1)}, u32[]{:S(2)}, u32[]{:S(2)}) collective-permute-start(bf16[24,2816]{1,0:T(8,128)(2,1)S(1)} %get-tuple-element.41), channel_id=1, source_target_pairs={{0,64},{8,72},{16,80},{24,88},{32,96},{40,104},{48,112},{56,120},{... | collective-permute-start | bytes 405512 | tf_op jit(solution)/shard_map/gate_up/ppermute | solution.py:38
  197.0 30.1 %copy-start = (bf16[2688,768]{1,0:T(8,128)(2,1)S(1)}, bf16[2688,768]{1,0:T(8,128)(2,1)}, u32[]{:S(2)}) copy-start(bf16[2688,768]{1,0:T(8,128)(2,1)} %weight_ref.5) | copy-start | bytes 12386308
  229.5 4.2 %collective-permute-start.14 = (bf16[192,768]{1,0:T(8,128)(2,1)S(1)}, bf16[192,768]{1,0:T(8,128)(2,1)S(1)}, u32[]{:S(2)}, u32[]{:S(2)}) collective-permute-start(bf16[192,768]{1,0:T(8,128)(2,1)S(1)} %get-tuple-element.48), channel_id=1, source_target_pairs={{0,1},{1,0},{2,3},{3,2},{4,5},{5,4},{6,7},{7,6},{8,9},{9,8},{10,11... | collective-permute-start | bytes 884744 | tf_op jit(solution)/shard_map/down_projection/ppermute | solution.py:48
  233.8 4.5 %collective-permute-start.15 = (bf16[48,768]{1,0:T(8,128)(2,1)S(1)}, bf16[48,768]{1,0:T(8,128)(2,1)S(1)}, u32[]{:S(2)}, u32[]{:S(2)}) collective-permute-start(bf16[48,768]{1,0:T(8,128)(2,1)S(1)} %get-tuple-element.50), channel_id=1, source_target_pairs={{0,2},{1,3},{2,4},{3,5},{4,6},{5,7},{6,0},{7,1},{8,10},{9,11},{10,... | collective-permute-start | bytes 221192 | tf_op jit(solution)/shard_map/down_projection/ppermute | solution.py:43
  233.9 6.1 %collective-permute-start.16 = (bf16[48,768]{1,0:T(8,128)(2,1)S(1)}, bf16[48,768]{1,0:T(8,128)(2,1)S(1)}, u32[]{:S(2)}, u32[]{:S(2)}) collective-permute-start(bf16[48,768]{1,0:T(8,128)(2,1)S(1)} %get-tuple-element.51), channel_id=1, source_target_pairs={{0,4},{1,5},{2,6},{3,7},{4,0},{5,1},{6,2},{7,3},{8,12},{9,13},{10,... | collective-permute-start | bytes 221192 | tf_op jit(solution)/shard_map/down_projection/ppermute | solution.py:43
  236.6 4.2 %collective-permute-start.17 = (bf16[48,768]{1,0:T(8,128)(2,1)S(1)}, bf16[48,768]{1,0:T(8,128)(2,1)S(1)}, u32[]{:S(2)}, u32[]{:S(2)}) collective-permute-start(bf16[48,768]{1,0:T(8,128)(2,1)S(1)} %get-tuple-element.52), channel_id=1, source_target_pairs={{0,6},{1,7},{2,0},{3,1},{4,2},{5,3},{6,4},{7,5},{8,14},{9,15},{10,... | collective-permute-start | bytes 221192 | tf_op jit(solution)/shard_map/down_projection/ppermute | solution.py:43
  (10 other events, 66.1 us)

commit v6 on v5

--- a/solution.py
+++ b/solution.py
@@ -279,7 +279,7 @@
                 held_ref.at[half, :, columns],
                 in_sems.at[half, at],
             )
-    order = [(half, at) for half in (1, 0) for at in range(len(spans))]
+    order = [(half, at) for half in (1, 0) for at in (range(len(spans)) if half else reversed(range(len(spans))))]
     ahead = 4
     for key in order[:ahead]:
         loads[key].start()
@@ -311,7 +311,7 @@
             )
         )
         stores[-1].start()
-    for at, (start, size) in enumerate(list(spans) + [(hidden, LANES)]):
+    for at, (start, size) in reversed(list(enumerate(list(spans) + [(hidden, LANES)]))):
         if start < hidden:
             arrived(0, at)
             gates = dot(ordered, held_ref[0, :, start : start + size])
@@ -521,6 +521,30 @@
     )(jnp.asarray(rotary(rows, past)), returned)
 
 
+def cut_kernel(cache_ref, out_ref):
+    blocks, rows, halves, span, _ = out_ref.shape
+    for block in range(blocks):
+        for half in range(halves):
+            out_ref[block, :, half] = cache_ref[half, :, block * span : (block + 1) * span]
+
+
+def cut_positions(cache, blocks):
+    halves, rows, past, width = cache.shape
+    shape = (blocks, rows, halves, past // blocks, width)
+    whole = pl.BlockSpec(memory_space=pltpu.VMEM)
+    return pl.pallas_call(
+        cut_kernel,
+        out_shape=jax.ShapeDtypeStruct(shape, cache.dtype),
+        in_specs=[whole],
+        out_specs=whole,
+        compiler_params=pltpu.CompilerParams(vmem_limit_bytes=58 * MIB),
+        cost_estimate=pl.CostEstimate(
+            flops=0, bytes_accessed=4 * cache.size, transcendentals=0
+        ),
+        name="cut_positions",
+    )(cache)
+
+
 def pick_kernel(index_ref, table_ref, sum_ref, out_ref):
     span = table_ref.shape[1]
     count = index_ref.shape[0] // out_ref.shape[0]
@@ -583,7 +607,7 @@
     span = past // batches
 
     with jax.named_scope("cache_spread"):
-        pieces = past_cache.reshape(2, rows, batches, span, kv_width).transpose(2, 1, 0, 3, 4)
+        pieces = cut_positions(past_cache, batches)
         spread = exchange(pieces, "batch").reshape(batches * rows, 2 * span, kv_width)
 
     with jax.named_scope("places"):

time: 242 us -> 242 us (level)
  local copies, waits for them, and re-layouts: 11.6 us -> 8.65 us
  Pallas kernels: 20.5 us -> 23 us
    reshape x1 -> x0, local copies, waits for them, and re-layouts: 2.96 us -> none  [on_device(): past_cache.reshape(2, rows, batches, span, kv_width)]
    pallas_call x0 -> x1, Pallas kernels: none -> 2.67 us  [cut_positions(): pl.pallas_call(cut_kernel, out_shape=jax.ShapeDtypeStruct(shape, cache.dt...]
where the time goes in v6:
time: 242 us; the launch traced here: 241 us
  blocking collectives  107 us (44%)
  waiting for transfers between devices  50.4 us (21%)
  starting transfers between devices  48.8 us (20%)
  Pallas kernels  23 us (10%)
  local copies, waits for them, and re-layouts  8.65 us (4%)
  other arithmetic  2.79 us (1%)
    all_to_all x3, blocking collectives, exchange(): return lax.all_to_all(blocks, axis, split_axis=0, concat_axis=0, tiled=True)  107 us
    ppermute x6, waiting for transfers between devices, shift_along(): return lax.ppermute(block, 'batch', pairs)  27.8 us
    ppermute x9, starting transfers between devices, shift_chips(): lax.ppermute(block, 'tensor', [(at, (at + 2 * count) % size) for at in ra...  12.5 us
    ppermute x3, starting transfers between devices, swap_cores(): return lax.ppermute(block, 'tensor', [(at, at ^ 1) for at in range(size)])  11.8 us
    all_to_all x1, waiting for transfers between devices, exchange(): return lax.all_to_all(blocks, axis, split_axis=0, concat_axis=0, tiled=True)  9.76 us
    all_to_all x1, starting transfers between devices, exchange(): return lax.all_to_all(blocks, axis, split_axis=0, concat_axis=0, tiled=True)  8.73 us
    pallas_call x1, Pallas kernels, gate_up(): pl.pallas_call(functools.partial(gate_up_kernel, side, spans), out_shape=...  8.67 us
    ppermute x6, starting transfers between devices, shift_along(): return lax.ppermute(block, 'batch', pairs)  8 us
  transfers between devices with their start and end apart: 21, of which 17 were waited for; matrix products, arithmetic and copies ran while one was open for 3% of the time, Pallas kernels for 2%

profile of v6, /device:TPU:1, one launch (start us, length us, event | category | flops | bytes accessed | tf_op | source)
XLA Modules:
  0.0 241.1 jit_solution(17320721888824356088)
XLA Ops:
  0.6 2.7 %cut_positions.1 = bf16[16,12,2,16,128]{4,3,2,1,0:T(8,128)(2,1)} custom-call(bf16[2,12,256,128]{3,2,1,0:T(8,128)(2,1)} %cache_ref.1), custom_call_target="tpu_custom_call" | custom-call | bytes 3145728 | tf_op jit(solution)/shard_map/cache_spread/cut_positions/pallas_call | solution.py:535
  3.3 8.7 %all-to-all-start = ((bf16[16,12,2,16,128]{4,3,2,1,0:T(8,128)(2,1)}), bf16[16,12,2,16,128]{4,3,2,1,0:T(8,128)(2,1)S(1)}, u32[]{:S(2)}, u32[]{:S(2)}) async-start(bf16[16,12,2,16,128]{4,3,2,1,0:T(8,128)(2,1)} %cut_positions.1), calls=%async_computation | async-start | bytes 3145728 | tf_op jit(solution)/shard_map/cache_spread/all_to_all | solution.py:22
  20.4 2.5 %project_rows.1.sum_ref = bf16[16,384,128]{2,1,0:T(8,128)(2,1)S(1)} custom-call(s32[384,1]{1,0:T(8,128)S(1)} %fusion.13.order_ref, s32[192,1]{1,0:T(8,128)S(1)} %copy.20.parent_ref, bf16[2,192,768]{2,1,0:T(8,128)(2,1)S(1)} %copy-done.3, bf16[1,768]{1,0:T(2,128)(2,1)S(1)} %reshape.486.gain_ref, bf16[768,1536]{1,0:T(8,128)(2,1)S(1)} %copy-done.1, ...), custom_call_target="tpu_custom_call" | custom-call | flops 1207959552 | bytes 4718592 | tf_op jit(solution)/shard_map/project/project_rows/pallas_call | solution.py:254
  22.9 9.8 %all-to-all-done = bf16[16,12,2,16,128]{4,3,2,1,0:T(8,128)(2,1)S(1)} async-done(((bf16[16,12,2,16,128]{4,3,2,1,0:T(8,128)(2,1)}), bf16[16,12,2,16,128]{4,3,2,1,0:T(8,128)(2,1)S(1)}, u32[]{:S(2)}, u32[]{:S(2)}) %all-to-all-start) | async-done | bytes 1572896 | tf_op jit(solution)/shard_map/cache_spread/all_to_all | solution.py:22
  33.7 58.3 %all_to_all.30.cache_ref = bf16[16,1152,128]{2,1,0:T(8,128)(2,1)S(1)} all-to-all(bf16[16,1152,128]{2,1,0:T(8,128)(2,1)S(1)} %pick_rows.1), channel_id=1, replica_groups=mesh['batch'=16,'tensor'=8] {'batch'}, dimensions={0} | all-to-all | bytes 9437184 | tf_op jit(solution)/shard_map/cache_return/all_to_all | solution.py:22
  92.0 2.1 attend.1
  94.2 18.1 %all_to_all.31 = bf16[16,24,1536]{2,1,0:T(8,128)(2,1)S(1)} all-to-all(bf16[16,24,1536]{2,1,0:T(8,128)(2,1)S(1)} %get-tuple-element.31), channel_id=1, replica_groups=mesh['batch'=16,'tensor'=8] {'batch'}, dimensions={0} | all-to-all | bytes 2359296 | tf_op jit(solution)/shard_map/attention/all_to_all | solution.py:22
  114.0 5.1 %collective-permute-start = (bf16[192,768]{1,0:T(8,128)(2,1)S(1)}, bf16[192,768]{1,0:T(8,128)(2,1)S(1)}, u32[]{:S(2)}, u32[]{:S(2)}) collective-permute-start(bf16[192,768]{1,0:T(8,128)(2,1)S(1)} %get-tuple-element.33), channel_id=1, source_target_pairs={{0,1},{1,0},{2,3},{3,2},{4,5},{5,4},{6,7},{7,6},{8,9},{9,8},{10,11... | collective-permute-start | bytes 884744 | tf_op jit(solution)/shard_map/output_projection/ppermute | solution.py:48
  121.6 2.5 %collective-permute-start.2 = (bf16[48,768]{1,0:T(8,128)(2,1)S(1)}, bf16[48,768]{1,0:T(8,128)(2,1)S(1)}, u32[]{:S(2)}, u32[]{:S(2)}) collective-permute-start(bf16[48,768]{1,0:T(8,128)(2,1)S(1)} %get-tuple-element.36), channel_id=1, source_target_pairs={{0,4},{1,5},{2,6},{3,7},{4,0},{5,1},{6,2},{7,3},{8,12},{9,13},{10,... | collective-permute-start | bytes 221192 | tf_op jit(solution)/shard_map/output_projection/ppermute | solution.py:43
  127.7 3.2 %collective-permute-start.5 = (bf16[48,768]{1,0:T(8,128)(2,1)S(1)}, bf16[48,768]{1,0:T(8,128)(2,1)S(1)}, u32[]{:S(2)}, u32[]{:S(2)}) collective-permute-start(bf16[48,768]{1,0:T(8,128)(2,1)S(1)} %get-tuple-element.60), channel_id=1, source_target_pairs={{0,4},{1,5},{2,6},{3,7},{4,0},{5,1},{6,2},{7,3},{8,12},{9,13},{10,... | collective-permute-start | bytes 221192 | tf_op jit(solution)/shard_map/output_projection/ppermute | solution.py:43
  134.5 3.7 %collective-permute-start.7 = (bf16[192,768]{1,0:T(8,128)(2,1)S(1)}, bf16[192,768]{1,0:T(8,128)(2,1)S(1)}, u32[]{:S(2)}, u32[]{:S(2)}) collective-permute-start(bf16[192,768]{1,0:T(8,128)(2,1)S(1)} %pad_maximum_fusion.near_ref), channel_id=1, source_target_pairs={{0,1},{1,0},{2,3},{3,2},{4,5},{5,4},{6,7},{7,6},{8,9},{9,8},{10,11... | collective-permute-start | bytes 884744 | tf_op jit(solution)/shard_map/output_projection/ppermute | solution.py:48
  140.1 8.7 %gate_up.1 = (bf16[4,96,2816]{2,1,0:T(8,128)(2,1)}, bf16[96,2688]{1,0:T(8,128)(2,1)}, bf16[96,2688]{1,0:T(8,128)(2,1)}, bf16[96,2688]{1,0:T(8,128)(2,1)}, bf16[96,2688]{1,0:T(8,128)(2,1)}) custom-call(s32[384,1]{1,0:T(8,128)} %fusion.26.order_ref, bf16[192,768]{1,0:T(8,128)(2,1)} %copy-done.7, bf16[192,768]{1,0:T(8,128)(2,1)} %copy-done.12, ...), custom_call_target="tpu_custom_call" | custom-call | flops 3170893824 | bytes 12386304 | tf_op jit(solution)/shard_map/gate_up/gate_up/pallas_call | solution.py:343
  148.8 3.8 %all-to-all-start.3 = ((bf16[4,96,2816]{2,1,0:T(8,128)(2,1)}), bf16[4,96,2816]{2,1,0:T(8,128)(2,1)S(1)}, u32[]{:S(2)}, u32[]{:S(2)}) async-start(bf16[4,96,2816]{2,1,0:T(8,128)(2,1)} %get-tuple-element.38), calls=%async_computation.3 | async-start | bytes 4325376 | tf_op jit(solution)/shard_map/gate_up/all_to_all | solution.py:90
  152.9 1.8 collective-permute-start.12
  155.9 11.8 %collective-permute-done.11.refs_1_ = bf16[96,2688]{1,0:T(8,128)(2,1)S(1)} collective-permute-done((bf16[96,2688]{1,0:T(8,128)(2,1)}, bf16[96,2688]{1,0:T(8,128)(2,1)S(1)}, u32[]{:S(2)}, u32[]{:S(2)}) %collective-permute-start.11) | collective-permute-done | bytes 516128 | tf_op jit(solution)/shard_map/gate_up/ppermute | solution.py:38
  167.7 9.9 %collective-permute-done.12.refs_2_ = bf16[96,2688]{1,0:T(8,128)(2,1)S(1)} collective-permute-done((bf16[96,2688]{1,0:T(8,128)(2,1)}, bf16[96,2688]{1,0:T(8,128)(2,1)S(1)}, u32[]{:S(2)}, u32[]{:S(2)}) %collective-permute-start.12) | collective-permute-done | bytes 516128 | tf_op jit(solution)/shard_map/gate_up/ppermute | solution.py:38
  179.5 4.1 %all-to-all-start.4 = ((bf16[4,24,2688]{2,1,0:T(8,128)(2,1)}), bf16[4,24,2688]{2,1,0:T(8,128)(2,1)S(1)}, u32[]{:S(2)}, u32[]{:S(2)}) async-start(bf16[4,24,2688]{2,1,0:T(8,128)(2,1)} %fold_stacked.1), calls=%async_computation.4 | async-start | bytes 1032192 | tf_op jit(solution)/shard_map/gate_up/all_to_all | solution.py:90
  183.9 3.5 %collective-permute-start.10 = (bf16[24,2816]{1,0:T(8,128)(2,1)S(1)}, bf16[24,2816]{1,0:T(8,128)(2,1)S(1)}, u32[]{:S(2)}, u32[]{:S(2)}) collective-permute-start(bf16[24,2816]{1,0:T(8,128)(2,1)S(1)} %get-tuple-element.42), channel_id=1, source_target_pairs={{0,96},{8,104},{16,112},{24,120},{32,0},{40,8},{48,16},{56,24},{64... | collective-permute-start | bytes 405512 | tf_op jit(solution)/shard_map/gate_up/ppermute | solution.py:38
  188.6 2.3 all-to-all-done.4.refs_3_
  190.9 5.2 %collective-permute-done.8.refs_0_ = bf16[24,2816]{1,0:T(8,128)(2,1)S(1)} collective-permute-done((bf16[24,2816]{1,0:T(8,128)(2,1)S(1)}, bf16[24,2816]{1,0:T(8,128)(2,1)S(1)}, u32[]{:S(2)}, u32[]{:S(2)}) %collective-permute-start.8) | collective-permute-done | bytes 135200 | tf_op jit(solution)/shard_map/gate_up/ppermute | solution.py:38
  196.5 30.1 %all_to_all.32 = bf16[16,24,2688]{2,1,0:T(8,128)(2,1)S(1)} all-to-all(bf16[16,24,2688]{2,1,0:T(8,128)(2,1)S(1)} %activate.1), channel_id=1, replica_groups=mesh['batch'=16,'tensor'=8] {'batch'}, dimensions={0} | all-to-all | bytes 4128768 | tf_op jit(solution)/shard_map/gate_up/all_to_all | solution.py:22
  226.6 2.4 %spread_dot.3 = (f32[192,768]{1,0:T(8,128)S(1)}, bf16[192,768]{1,0:T(8,128)(2,1)S(1)}) custom-call(s32[16]{0:T(128)S(1)} %fusion.35.place_ref, bf16[384,2688]{1,0:T(8,128)(2,1)S(1)} %bitcast.19, bf16[2688,768]{1,0:T(8,128)(2,1)S(1)} %copy-done), custom_call_target="tpu_custom_call" | custom-call | flops 1585446912 | bytes 8552448 | tf_op jit(solution)/shard_map/down_projection/spread_dot/pallas_call | solution.py:382
  229.1 3.0 %collective-permute-start.14 = (bf16[192,768]{1,0:T(8,128)(2,1)S(1)}, bf16[192,768]{1,0:T(8,128)(2,1)S(1)}, u32[]{:S(2)}, u32[]{:S(2)}) collective-permute-start(bf16[192,768]{1,0:T(8,128)(2,1)S(1)} %get-tuple-element.48), channel_id=1, source_target_pairs={{0,1},{1,0},{2,3},{3,2},{4,5},{5,4},{6,7},{7,6},{8,9},{9,8},{10,11... | collective-permute-start | bytes 884744 | tf_op jit(solution)/shard_map/down_projection/ppermute | solution.py:48
  233.4 2.8 %collective-permute-start.16 = (bf16[48,768]{1,0:T(8,128)(2,1)S(1)}, bf16[48,768]{1,0:T(8,128)(2,1)S(1)}, u32[]{:S(2)}, u32[]{:S(2)}) collective-permute-start(bf16[48,768]{1,0:T(8,128)(2,1)S(1)} %get-tuple-element.51), channel_id=1, source_target_pairs={{0,4},{1,5},{2,6},{3,7},{4,0},{5,1},{6,2},{7,3},{8,12},{9,13},{10,... | collective-permute-start | bytes 221192 | tf_op jit(solution)/shard_map/down_projection/ppermute | solution.py:43
  (90 shorter events, 34.2 us)
Async XLA Ops:
  3.3 29.4 %all-to-all-start = ((bf16[16,12,2,16,128]{4,3,2,1,0:T(8,128)(2,1)}), bf16[16,12,2,16,128]{4,3,2,1,0:T(8,128)(2,1)S(1)}, u32[]{:S(2)}, u32[]{:S(2)}) async-start(bf16[16,12,2,16,128]{4,3,2,1,0:T(8,128)(2,1)} %cut_positions.1), calls=%async_computation | async-start | bytes 3145728 | tf_op jit(solution)/shard_map/cache_spread/all_to_all | solution.py:22
  33.7 58.3 %copy-start.6 = (f32[24,256]{1,0:T(8,128)S(1)}, f32[24,256]{1,0:T(8,128)}, u32[]{:S(2)}) copy-start(f32[24,256]{1,0:T(8,128)} %constant.181.clone.table_ref) | copy-start | bytes 73732
  114.0 6.3 %collective-permute-start = (bf16[192,768]{1,0:T(8,128)(2,1)S(1)}, bf16[192,768]{1,0:T(8,128)(2,1)S(1)}, u32[]{:S(2)}, u32[]{:S(2)}) collective-permute-start(bf16[192,768]{1,0:T(8,128)(2,1)S(1)} %get-tuple-element.33), channel_id=1, source_target_pairs={{0,1},{1,0},{2,3},{3,2},{4,5},{5,4},{6,7},{7,6},{8,9},{9,8},{10,11... | collective-permute-start | bytes 884744 | tf_op jit(solution)/shard_map/output_projection/ppermute | solution.py:48
  120.3 5.9 %collective-permute-start.1 = (bf16[48,768]{1,0:T(8,128)(2,1)S(1)}, bf16[48,768]{1,0:T(8,128)(2,1)S(1)}, u32[]{:S(2)}, u32[]{:S(2)}) collective-permute-start(bf16[48,768]{1,0:T(8,128)(2,1)S(1)} %get-tuple-element.35), channel_id=1, source_target_pairs={{0,2},{1,3},{2,4},{3,5},{4,6},{5,7},{6,0},{7,1},{8,10},{9,11},{10,... | collective-permute-start | bytes 221192 | tf_op jit(solution)/shard_map/output_projection/ppermute | solution.py:43
  121.6 5.8 %collective-permute-start.2 = (bf16[48,768]{1,0:T(8,128)(2,1)S(1)}, bf16[48,768]{1,0:T(8,128)(2,1)S(1)}, u32[]{:S(2)}, u32[]{:S(2)}) collective-permute-start(bf16[48,768]{1,0:T(8,128)(2,1)S(1)} %get-tuple-element.36), channel_id=1, source_target_pairs={{0,4},{1,5},{2,6},{3,7},{4,0},{5,1},{6,2},{7,3},{8,12},{9,13},{10,... | collective-permute-start | bytes 221192 | tf_op jit(solution)/shard_map/output_projection/ppermute | solution.py:43
  124.0 3.5 %collective-permute-start.3 = (bf16[48,768]{1,0:T(8,128)(2,1)S(1)}, bf16[48,768]{1,0:T(8,128)(2,1)S(1)}, u32[]{:S(2)}, u32[]{:S(2)}) collective-permute-start(bf16[48,768]{1,0:T(8,128)(2,1)S(1)} %get-tuple-element.37), channel_id=1, source_target_pairs={{0,6},{1,7},{2,0},{3,1},{4,2},{5,3},{6,4},{7,5},{8,14},{9,15},{10,... | collective-permute-start | bytes 221192 | tf_op jit(solution)/shard_map/output_projection/ppermute | solution.py:43
  127.6 4.5 %collective-permute-start.4 = (bf16[48,768]{1,0:T(8,128)(2,1)S(1)}, bf16[48,768]{1,0:T(8,128)(2,1)S(1)}, u32[]{:S(2)}, u32[]{:S(2)}) collective-permute-start(bf16[48,768]{1,0:T(8,128)(2,1)S(1)} %get-tuple-element.60), channel_id=1, source_target_pairs={{0,2},{1,3},{2,4},{3,5},{4,6},{5,7},{6,0},{7,1},{8,10},{9,11},{10,... | collective-permute-start | bytes 221192 | tf_op jit(solution)/shard_map/output_projection/ppermute | solution.py:43
  127.7 5.8 %collective-permute-start.5 = (bf16[48,768]{1,0:T(8,128)(2,1)S(1)}, bf16[48,768]{1,0:T(8,128)(2,1)S(1)}, u32[]{:S(2)}, u32[]{:S(2)}) collective-permute-start(bf16[48,768]{1,0:T(8,128)(2,1)S(1)} %get-tuple-element.60), channel_id=1, source_target_pairs={{0,4},{1,5},{2,6},{3,7},{4,0},{5,1},{6,2},{7,3},{8,12},{9,13},{10,... | collective-permute-start | bytes 221192 | tf_op jit(solution)/shard_map/output_projection/ppermute | solution.py:43
  131.0 3.5 %collective-permute-start.6 = (bf16[48,768]{1,0:T(8,128)(2,1)S(1)}, bf16[48,768]{1,0:T(8,128)(2,1)S(1)}, u32[]{:S(2)}, u32[]{:S(2)}) collective-permute-start(bf16[48,768]{1,0:T(8,128)(2,1)S(1)} %get-tuple-element.60), channel_id=1, source_target_pairs={{0,6},{1,7},{2,0},{3,1},{4,2},{5,3},{6,4},{7,5},{8,14},{9,15},{10,... | collective-permute-start | bytes 221192 | tf_op jit(solution)/shard_map/output_projection/ppermute | solution.py:43
  134.5 4.9 %collective-permute-start.7 = (bf16[192,768]{1,0:T(8,128)(2,1)S(1)}, bf16[192,768]{1,0:T(8,128)(2,1)S(1)}, u32[]{:S(2)}, u32[]{:S(2)}) collective-permute-start(bf16[192,768]{1,0:T(8,128)(2,1)S(1)} %pad_maximum_fusion.near_ref), channel_id=1, source_target_pairs={{0,1},{1,0},{2,3},{3,2},{4,5},{5,4},{6,7},{7,6},{8,9},{9,8},{10,11... | collective-permute-start | bytes 884744 | tf_op jit(solution)/shard_map/output_projection/ppermute | solution.py:48
  148.8 29.6 %copy-start.4 = (bf16[96,2688]{1,0:T(8,128)(2,1)S(1)}, bf16[96,2688]{1,0:T(8,128)(2,1)}, u32[]{:S(2)}) copy-start(bf16[96,2688]{1,0:T(8,128)(2,1)} %get-tuple-element.43.refs_0_) | copy-start | bytes 1548292
  148.8 30.6 %all-to-all-start.3 = ((bf16[4,96,2816]{2,1,0:T(8,128)(2,1)}), bf16[4,96,2816]{2,1,0:T(8,128)(2,1)S(1)}, u32[]{:S(2)}, u32[]{:S(2)}) async-start(bf16[4,96,2816]{2,1,0:T(8,128)(2,1)} %get-tuple-element.38), calls=%async_computation.3 | async-start | bytes 4325376 | tf_op jit(solution)/shard_map/gate_up/all_to_all | solution.py:90
  152.6 15.1 %collective-permute-start.11 = (bf16[96,2688]{1,0:T(8,128)(2,1)}, bf16[96,2688]{1,0:T(8,128)(2,1)S(1)}, u32[]{:S(2)}, u32[]{:S(2)}) collective-permute-start(bf16[96,2688]{1,0:T(8,128)(2,1)} %get-tuple-element.44), channel_id=1, source_target_pairs={{0,32},{8,40},{16,48},{24,56},{32,64},{40,72},{48,80},{56,88},{64,... | collective-permute-start | bytes 1548296 | tf_op jit(solution)/shard_map/gate_up/ppermute | solution.py:38
  152.9 24.6 %collective-permute-start.12 = (bf16[96,2688]{1,0:T(8,128)(2,1)}, bf16[96,2688]{1,0:T(8,128)(2,1)S(1)}, u32[]{:S(2)}, u32[]{:S(2)}) collective-permute-start(bf16[96,2688]{1,0:T(8,128)(2,1)} %get-tuple-element.45), channel_id=1, source_target_pairs={{0,64},{8,72},{16,80},{24,88},{32,96},{40,104},{48,112},{56,120},{... | collective-permute-start | bytes 1548296 | tf_op jit(solution)/shard_map/gate_up/ppermute | solution.py:38
  154.8 23.7 %collective-permute-start.13 = (bf16[96,2688]{1,0:T(8,128)(2,1)S(1)}, bf16[96,2688]{1,0:T(8,128)(2,1)S(1)}, u32[]{:S(2)}, u32[]{:S(2)}) collective-permute-start(bf16[96,2688]{1,0:T(8,128)(2,1)S(1)} %copy-done.11), channel_id=1, source_target_pairs={{0,96},{8,104},{16,112},{24,120},{32,0},{40,8},{48,16},{56,24},{64... | collective-permute-start | bytes 1548296 | tf_op jit(solution)/shard_map/gate_up/ppermute | solution.py:38
  179.5 11.4 %all-to-all-start.4 = ((bf16[4,24,2688]{2,1,0:T(8,128)(2,1)}), bf16[4,24,2688]{2,1,0:T(8,128)(2,1)S(1)}, u32[]{:S(2)}, u32[]{:S(2)}) async-start(bf16[4,24,2688]{2,1,0:T(8,128)(2,1)} %fold_stacked.1), calls=%async_computation.4 | async-start | bytes 1032192 | tf_op jit(solution)/shard_map/gate_up/all_to_all | solution.py:90
  183.9 7.0 %collective-permute-start.10 = (bf16[24,2816]{1,0:T(8,128)(2,1)S(1)}, bf16[24,2816]{1,0:T(8,128)(2,1)S(1)}, u32[]{:S(2)}, u32[]{:S(2)}) collective-permute-start(bf16[24,2816]{1,0:T(8,128)(2,1)S(1)} %get-tuple-element.42), channel_id=1, source_target_pairs={{0,96},{8,104},{16,112},{24,120},{32,0},{40,8},{48,16},{56,24},{64... | collective-permute-start | bytes 405512 | tf_op jit(solution)/shard_map/gate_up/ppermute | solution.py:38
  187.3 8.7 %collective-permute-start.8 = (bf16[24,2816]{1,0:T(8,128)(2,1)S(1)}, bf16[24,2816]{1,0:T(8,128)(2,1)S(1)}, u32[]{:S(2)}, u32[]{:S(2)}) collective-permute-start(bf16[24,2816]{1,0:T(8,128)(2,1)S(1)} %get-tuple-element.40), channel_id=1, source_target_pairs={{0,32},{8,40},{16,48},{24,56},{32,64},{40,72},{48,80},{56,88},{64,... | collective-permute-start | bytes 405512 | tf_op jit(solution)/shard_map/gate_up/ppermute | solution.py:38
  187.3 8.7 %collective-permute-start.9 = (bf16[24,2816]{1,0:T(8,128)(2,1)S(1)}, bf16[24,2816]{1,0:T(8,128)(2,1)S(1)}, u32[]{:S(2)}, u32[]{:S(2)}) collective-permute-start(bf16[24,2816]{1,0:T(8,128)(2,1)S(1)} %get-tuple-element.41), channel_id=1, source_target_pairs={{0,64},{8,72},{16,80},{24,88},{32,96},{40,104},{48,112},{56,120},{... | collective-permute-start | bytes 405512 | tf_op jit(solution)/shard_map/gate_up/ppermute | solution.py:38
  196.5 30.1 %copy-start = (bf16[2688,768]{1,0:T(8,128)(2,1)S(1)}, bf16[2688,768]{1,0:T(8,128)(2,1)}, u32[]{:S(2)}) copy-start(bf16[2688,768]{1,0:T(8,128)(2,1)} %weight_ref.5) | copy-start | bytes 12386308
  229.1 4.2 %collective-permute-start.14 = (bf16[192,768]{1,0:T(8,128)(2,1)S(1)}, bf16[192,768]{1,0:T(8,128)(2,1)S(1)}, u32[]{:S(2)}, u32[]{:S(2)}) collective-permute-start(bf16[192,768]{1,0:T(8,128)(2,1)S(1)} %get-tuple-element.48), channel_id=1, source_target_pairs={{0,1},{1,0},{2,3},{3,2},{4,5},{5,4},{6,7},{7,6},{8,9},{9,8},{10,11... | collective-permute-start | bytes 884744 | tf_op jit(solution)/shard_map/down_projection/ppermute | solution.py:48
  233.3 4.5 %collective-permute-start.15 = (bf16[48,768]{1,0:T(8,128)(2,1)S(1)}, bf16[48,768]{1,0:T(8,128)(2,1)S(1)}, u32[]{:S(2)}, u32[]{:S(2)}) collective-permute-start(bf16[48,768]{1,0:T(8,128)(2,1)S(1)} %get-tuple-element.50), channel_id=1, source_target_pairs={{0,2},{1,3},{2,4},{3,5},{4,6},{5,7},{6,0},{7,1},{8,10},{9,11},{10,... | collective-permute-start | bytes 221192 | tf_op jit(solution)/shard_map/down_projection/ppermute | solution.py:43
  233.4 6.1 %collective-permute-start.16 = (bf16[48,768]{1,0:T(8,128)(2,1)S(1)}, bf16[48,768]{1,0:T(8,128)(2,1)S(1)}, u32[]{:S(2)}, u32[]{:S(2)}) collective-permute-start(bf16[48,768]{1,0:T(8,128)(2,1)S(1)} %get-tuple-element.51), channel_id=1, source_target_pairs={{0,4},{1,5},{2,6},{3,7},{4,0},{5,1},{6,2},{7,3},{8,12},{9,13},{10,... | collective-permute-start | bytes 221192 | tf_op jit(solution)/shard_map/down_projection/ppermute | solution.py:43
  236.2 4.2 %collective-permute-start.17 = (bf16[48,768]{1,0:T(8,128)(2,1)S(1)}, bf16[48,768]{1,0:T(8,128)(2,1)S(1)}, u32[]{:S(2)}, u32[]{:S(2)}) collective-permute-start(bf16[48,768]{1,0:T(8,128)(2,1)S(1)} %get-tuple-element.52), channel_id=1, source_target_pairs={{0,6},{1,7},{2,0},{3,1},{4,2},{5,3},{6,4},{7,5},{8,14},{9,15},{10,... | collective-permute-start | bytes 221192 | tf_op jit(solution)/shard_map/down_projection/ppermute | solution.py:43
  (10 other events, 66.1 us)

commit v7 on v6

--- a/solution.py
+++ b/solution.py
@@ -671,7 +671,7 @@
         far = swap_cores(near)
 
     with jax.named_scope("gate_up"):
-        blocks = gate_up(side, lifted_order, near, far, lift_gain, gateup_weight, 768)
+        blocks = gate_up(side, lifted_order, near, far, lift_gain, gateup_weight, 1280)
         gates, terms, ups = add_crossed(blocks[0], blocks[1:])
         activated = activate(gates, terms, ups, model, batches)
         activated = exchange(activated, "batch").reshape(total, hidden)

time: 242 us -> 241 us (level)
  no operation moved by 1% of the time
where the time goes in v7:
time: 241 us
  blocking collectives  107 us (44%)
  waiting for transfers between devices  50.4 us (21%)
  starting transfers between devices  48.8 us (20%)
  Pallas kernels  22.6 us (9%)
  local copies, waits for them, and re-layouts  8.65 us (4%)
  other arithmetic  2.79 us (1%)
    all_to_all x3, blocking collectives, exchange(): return lax.all_to_all(blocks, axis, split_axis=0, concat_axis=0, tiled=True)  107 us
    ppermute x6, waiting for transfers between devices, shift_along(): return lax.ppermute(block, 'batch', pairs)  27.7 us
    ppermute x9, starting transfers between devices, shift_chips(): lax.ppermute(block, 'tensor', [(at, (at + 2 * count) % size) for at in ra...  12.5 us
    ppermute x3, starting transfers between devices, swap_cores(): return lax.ppermute(block, 'tensor', [(at, at ^ 1) for at in range(size)])  11.8 us
    all_to_all x1, waiting for transfers between devices, exchange(): return lax.all_to_all(blocks, axis, split_axis=0, concat_axis=0, tiled=True)  9.76 us
    all_to_all x1, starting transfers between devices, exchange(): return lax.all_to_all(blocks, axis, split_axis=0, concat_axis=0, tiled=True)  8.73 us
    pallas_call x1, Pallas kernels, gate_up(): pl.pallas_call(functools.partial(gate_up_kernel, side, spans), out_shape=...  8.34 us
    ppermute x6, starting transfers between devices, shift_along(): return lax.ppermute(block, 'batch', pairs)  8 us
  transfers between devices with their start and end apart: 21, of which 17 were waited for; matrix products, arithmetic and copies ran while one was open for 3% of the time, Pallas kernels for 2%

profile of v7, /device:TPU:1, one launch (start us, length us, event | category | flops | bytes accessed | tf_op | source)
XLA Modules:
  0.0 240.8 jit_solution(5396767830318637039)
XLA Ops:
  0.6 2.7 %cut_positions.1 = bf16[16,12,2,16,128]{4,3,2,1,0:T(8,128)(2,1)} custom-call(bf16[2,12,256,128]{3,2,1,0:T(8,128)(2,1)} %cache_ref.1), custom_call_target="tpu_custom_call" | custom-call | bytes 3145728 | tf_op jit(solution)/shard_map/cache_spread/cut_positions/pallas_call | solution.py:535
  3.3 8.7 %all-to-all-start = ((bf16[16,12,2,16,128]{4,3,2,1,0:T(8,128)(2,1)}), bf16[16,12,2,16,128]{4,3,2,1,0:T(8,128)(2,1)S(1)}, u32[]{:S(2)}, u32[]{:S(2)}) async-start(bf16[16,12,2,16,128]{4,3,2,1,0:T(8,128)(2,1)} %cut_positions.1), calls=%async_computation | async-start | bytes 3145728 | tf_op jit(solution)/shard_map/cache_spread/all_to_all | solution.py:22
  20.4 2.5 %project_rows.1.sum_ref = bf16[16,384,128]{2,1,0:T(8,128)(2,1)S(1)} custom-call(s32[384,1]{1,0:T(8,128)S(1)} %fusion.13.order_ref, s32[192,1]{1,0:T(8,128)S(1)} %copy.20.parent_ref, bf16[2,192,768]{2,1,0:T(8,128)(2,1)S(1)} %copy-done.3, bf16[1,768]{1,0:T(2,128)(2,1)S(1)} %reshape.486.gain_ref, bf16[768,1536]{1,0:T(8,128)(2,1)S(1)} %copy-done.1, ...), custom_call_target="tpu_custom_call" | custom-call | flops 1207959552 | bytes 4718592 | tf_op jit(solution)/shard_map/project/project_rows/pallas_call | solution.py:254
  22.9 9.8 %all-to-all-done = bf16[16,12,2,16,128]{4,3,2,1,0:T(8,128)(2,1)S(1)} async-done(((bf16[16,12,2,16,128]{4,3,2,1,0:T(8,128)(2,1)}), bf16[16,12,2,16,128]{4,3,2,1,0:T(8,128)(2,1)S(1)}, u32[]{:S(2)}, u32[]{:S(2)}) %all-to-all-start) | async-done | bytes 1572896 | tf_op jit(solution)/shard_map/cache_spread/all_to_all | solution.py:22
  33.7 58.3 %all_to_all.30.cache_ref = bf16[16,1152,128]{2,1,0:T(8,128)(2,1)S(1)} all-to-all(bf16[16,1152,128]{2,1,0:T(8,128)(2,1)S(1)} %pick_rows.1), channel_id=1, replica_groups=mesh['batch'=16,'tensor'=8] {'batch'}, dimensions={0} | all-to-all | bytes 9437184 | tf_op jit(solution)/shard_map/cache_return/all_to_all | solution.py:22
  92.0 2.1 attend.1
  94.2 18.1 %all_to_all.31 = bf16[16,24,1536]{2,1,0:T(8,128)(2,1)S(1)} all-to-all(bf16[16,24,1536]{2,1,0:T(8,128)(2,1)S(1)} %get-tuple-element.31), channel_id=1, replica_groups=mesh['batch'=16,'tensor'=8] {'batch'}, dimensions={0} | all-to-all | bytes 2359296 | tf_op jit(solution)/shard_map/attention/all_to_all | solution.py:22
  114.0 5.1 %collective-permute-start = (bf16[192,768]{1,0:T(8,128)(2,1)S(1)}, bf16[192,768]{1,0:T(8,128)(2,1)S(1)}, u32[]{:S(2)}, u32[]{:S(2)}) collective-permute-start(bf16[192,768]{1,0:T(8,128)(2,1)S(1)} %get-tuple-element.33), channel_id=1, source_target_pairs={{0,1},{1,0},{2,3},{3,2},{4,5},{5,4},{6,7},{7,6},{8,9},{9,8},{10,11... | collective-permute-start | bytes 884744 | tf_op jit(solution)/shard_map/output_projection/ppermute | solution.py:48
  121.6 2.5 %collective-permute-start.2 = (bf16[48,768]{1,0:T(8,128)(2,1)S(1)}, bf16[48,768]{1,0:T(8,128)(2,1)S(1)}, u32[]{:S(2)}, u32[]{:S(2)}) collective-permute-start(bf16[48,768]{1,0:T(8,128)(2,1)S(1)} %get-tuple-element.36), channel_id=1, source_target_pairs={{0,4},{1,5},{2,6},{3,7},{4,0},{5,1},{6,2},{7,3},{8,12},{9,13},{10,... | collective-permute-start | bytes 221192 | tf_op jit(solution)/shard_map/output_projection/ppermute | solution.py:43
  127.7 3.2 %collective-permute-start.5 = (bf16[48,768]{1,0:T(8,128)(2,1)S(1)}, bf16[48,768]{1,0:T(8,128)(2,1)S(1)}, u32[]{:S(2)}, u32[]{:S(2)}) collective-permute-start(bf16[48,768]{1,0:T(8,128)(2,1)S(1)} %get-tuple-element.60), channel_id=1, source_target_pairs={{0,4},{1,5},{2,6},{3,7},{4,0},{5,1},{6,2},{7,3},{8,12},{9,13},{10,... | collective-permute-start | bytes 221192 | tf_op jit(solution)/shard_map/output_projection/ppermute | solution.py:43
  134.5 3.7 %collective-permute-start.7 = (bf16[192,768]{1,0:T(8,128)(2,1)S(1)}, bf16[192,768]{1,0:T(8,128)(2,1)S(1)}, u32[]{:S(2)}, u32[]{:S(2)}) collective-permute-start(bf16[192,768]{1,0:T(8,128)(2,1)S(1)} %pad_maximum_fusion.near_ref), channel_id=1, source_target_pairs={{0,1},{1,0},{2,3},{3,2},{4,5},{5,4},{6,7},{7,6},{8,9},{9,8},{10,11... | collective-permute-start | bytes 884744 | tf_op jit(solution)/shard_map/output_projection/ppermute | solution.py:48
  140.1 8.3 %gate_up.1 = (bf16[4,96,2816]{2,1,0:T(8,128)(2,1)}, bf16[96,2688]{1,0:T(8,128)(2,1)}, bf16[96,2688]{1,0:T(8,128)(2,1)}, bf16[96,2688]{1,0:T(8,128)(2,1)}, bf16[96,2688]{1,0:T(8,128)(2,1)}) custom-call(s32[384,1]{1,0:T(8,128)} %fusion.26.order_ref, bf16[192,768]{1,0:T(8,128)(2,1)} %copy-done.7, bf16[192,768]{1,0:T(8,128)(2,1)} %copy-done.12, ...), custom_call_target="tpu_custom_call" | custom-call | flops 3170893824 | bytes 12386304 | tf_op jit(solution)/shard_map/gate_up/gate_up/pallas_call | solution.py:343
  148.5 3.8 %all-to-all-start.3 = ((bf16[4,96,2816]{2,1,0:T(8,128)(2,1)}), bf16[4,96,2816]{2,1,0:T(8,128)(2,1)S(1)}, u32[]{:S(2)}, u32[]{:S(2)}) async-start(bf16[4,96,2816]{2,1,0:T(8,128)(2,1)} %get-tuple-element.38), calls=%async_computation.3 | async-start | bytes 4325376 | tf_op jit(solution)/shard_map/gate_up/all_to_all | solution.py:90
  152.6 1.8 collective-permute-start.12
  155.5 11.8 %collective-permute-done.11.refs_1_ = bf16[96,2688]{1,0:T(8,128)(2,1)S(1)} collective-permute-done((bf16[96,2688]{1,0:T(8,128)(2,1)}, bf16[96,2688]{1,0:T(8,128)(2,1)S(1)}, u32[]{:S(2)}, u32[]{:S(2)}) %collective-permute-start.11) | collective-permute-done | bytes 516128 | tf_op jit(solution)/shard_map/gate_up/ppermute | solution.py:38
  167.3 9.9 %collective-permute-done.12.refs_2_ = bf16[96,2688]{1,0:T(8,128)(2,1)S(1)} collective-permute-done((bf16[96,2688]{1,0:T(8,128)(2,1)}, bf16[96,2688]{1,0:T(8,128)(2,1)S(1)}, u32[]{:S(2)}, u32[]{:S(2)}) %collective-permute-start.12) | collective-permute-done | bytes 516128 | tf_op jit(solution)/shard_map/gate_up/ppermute | solution.py:38
  179.2 4.1 %all-to-all-start.4 = ((bf16[4,24,2688]{2,1,0:T(8,128)(2,1)}), bf16[4,24,2688]{2,1,0:T(8,128)(2,1)S(1)}, u32[]{:S(2)}, u32[]{:S(2)}) async-start(bf16[4,24,2688]{2,1,0:T(8,128)(2,1)} %fold_stacked.1), calls=%async_computation.4 | async-start | bytes 1032192 | tf_op jit(solution)/shard_map/gate_up/all_to_all | solution.py:90
  183.5 3.5 %collective-permute-start.10 = (bf16[24,2816]{1,0:T(8,128)(2,1)S(1)}, bf16[24,2816]{1,0:T(8,128)(2,1)S(1)}, u32[]{:S(2)}, u32[]{:S(2)}) collective-permute-start(bf16[24,2816]{1,0:T(8,128)(2,1)S(1)} %get-tuple-element.42), channel_id=1, source_target_pairs={{0,96},{8,104},{16,112},{24,120},{32,0},{40,8},{48,16},{56,24},{64... | collective-permute-start | bytes 405512 | tf_op jit(solution)/shard_map/gate_up/ppermute | solution.py:38
  188.3 2.3 all-to-all-done.4.refs_3_
  190.6 5.2 %collective-permute-done.8.refs_0_ = bf16[24,2816]{1,0:T(8,128)(2,1)S(1)} collective-permute-done((bf16[24,2816]{1,0:T(8,128)(2,1)S(1)}, bf16[24,2816]{1,0:T(8,128)(2,1)S(1)}, u32[]{:S(2)}, u32[]{:S(2)}) %collective-permute-start.8) | collective-permute-done | bytes 135200 | tf_op jit(solution)/shard_map/gate_up/ppermute | solution.py:38
  196.2 30.1 %all_to_all.32 = bf16[16,24,2688]{2,1,0:T(8,128)(2,1)S(1)} all-to-all(bf16[16,24,2688]{2,1,0:T(8,128)(2,1)S(1)} %activate.1), channel_id=1, replica_groups=mesh['batch'=16,'tensor'=8] {'batch'}, dimensions={0} | all-to-all | bytes 4128768 | tf_op jit(solution)/shard_map/gate_up/all_to_all | solution.py:22
  226.3 2.4 %spread_dot.3 = (f32[192,768]{1,0:T(8,128)S(1)}, bf16[192,768]{1,0:T(8,128)(2,1)S(1)}) custom-call(s32[16]{0:T(128)S(1)} %fusion.35.place_ref, bf16[384,2688]{1,0:T(8,128)(2,1)S(1)} %bitcast.19, bf16[2688,768]{1,0:T(8,128)(2,1)S(1)} %copy-done), custom_call_target="tpu_custom_call" | custom-call | flops 1585446912 | bytes 8552448 | tf_op jit(solution)/shard_map/down_projection/spread_dot/pallas_call | solution.py:382
  228.7 3.0 %collective-permute-start.14 = (bf16[192,768]{1,0:T(8,128)(2,1)S(1)}, bf16[192,768]{1,0:T(8,128)(2,1)S(1)}, u32[]{:S(2)}, u32[]{:S(2)}) collective-permute-start(bf16[192,768]{1,0:T(8,128)(2,1)S(1)} %get-tuple-element.48), channel_id=1, source_target_pairs={{0,1},{1,0},{2,3},{3,2},{4,5},{5,4},{6,7},{7,6},{8,9},{9,8},{10,11... | collective-permute-start | bytes 884744 | tf_op jit(solution)/shard_map/down_projection/ppermute | solution.py:48
  233.1 2.8 %collective-permute-start.16 = (bf16[48,768]{1,0:T(8,128)(2,1)S(1)}, bf16[48,768]{1,0:T(8,128)(2,1)S(1)}, u32[]{:S(2)}, u32[]{:S(2)}) collective-permute-start(bf16[48,768]{1,0:T(8,128)(2,1)S(1)} %get-tuple-element.51), channel_id=1, source_target_pairs={{0,4},{1,5},{2,6},{3,7},{4,0},{5,1},{6,2},{7,3},{8,12},{9,13},{10,... | collective-permute-start | bytes 221192 | tf_op jit(solution)/shard_map/down_projection/ppermute | solution.py:43
  (90 shorter events, 34.2 us)
Async XLA Ops:
  3.3 29.4 %all-to-all-start = ((bf16[16,12,2,16,128]{4,3,2,1,0:T(8,128)(2,1)}), bf16[16,12,2,16,128]{4,3,2,1,0:T(8,128)(2,1)S(1)}, u32[]{:S(2)}, u32[]{:S(2)}) async-start(bf16[16,12,2,16,128]{4,3,2,1,0:T(8,128)(2,1)} %cut_positions.1), calls=%async_computation | async-start | bytes 3145728 | tf_op jit(solution)/shard_map/cache_spread/all_to_all | solution.py:22
  33.7 58.3 %copy-start.6 = (f32[24,256]{1,0:T(8,128)S(1)}, f32[24,256]{1,0:T(8,128)}, u32[]{:S(2)}) copy-start(f32[24,256]{1,0:T(8,128)} %constant.181.clone.table_ref) | copy-start | bytes 73732
  114.0 6.3 %collective-permute-start = (bf16[192,768]{1,0:T(8,128)(2,1)S(1)}, bf16[192,768]{1,0:T(8,128)(2,1)S(1)}, u32[]{:S(2)}, u32[]{:S(2)}) collective-permute-start(bf16[192,768]{1,0:T(8,128)(2,1)S(1)} %get-tuple-element.33), channel_id=1, source_target_pairs={{0,1},{1,0},{2,3},{3,2},{4,5},{5,4},{6,7},{7,6},{8,9},{9,8},{10,11... | collective-permute-start | bytes 884744 | tf_op jit(solution)/shard_map/output_projection/ppermute | solution.py:48
  120.3 5.9 %collective-permute-start.1 = (bf16[48,768]{1,0:T(8,128)(2,1)S(1)}, bf16[48,768]{1,0:T(8,128)(2,1)S(1)}, u32[]{:S(2)}, u32[]{:S(2)}) collective-permute-start(bf16[48,768]{1,0:T(8,128)(2,1)S(1)} %get-tuple-element.35), channel_id=1, source_target_pairs={{0,2},{1,3},{2,4},{3,5},{4,6},{5,7},{6,0},{7,1},{8,10},{9,11},{10,... | collective-permute-start | bytes 221192 | tf_op jit(solution)/shard_map/output_projection/ppermute | solution.py:43
  121.6 5.8 %collective-permute-start.2 = (bf16[48,768]{1,0:T(8,128)(2,1)S(1)}, bf16[48,768]{1,0:T(8,128)(2,1)S(1)}, u32[]{:S(2)}, u32[]{:S(2)}) collective-permute-start(bf16[48,768]{1,0:T(8,128)(2,1)S(1)} %get-tuple-element.36), channel_id=1, source_target_pairs={{0,4},{1,5},{2,6},{3,7},{4,0},{5,1},{6,2},{7,3},{8,12},{9,13},{10,... | collective-permute-start | bytes 221192 | tf_op jit(solution)/shard_map/output_projection/ppermute | solution.py:43
  124.0 3.5 %collective-permute-start.3 = (bf16[48,768]{1,0:T(8,128)(2,1)S(1)}, bf16[48,768]{1,0:T(8,128)(2,1)S(1)}, u32[]{:S(2)}, u32[]{:S(2)}) collective-permute-start(bf16[48,768]{1,0:T(8,128)(2,1)S(1)} %get-tuple-element.37), channel_id=1, source_target_pairs={{0,6},{1,7},{2,0},{3,1},{4,2},{5,3},{6,4},{7,5},{8,14},{9,15},{10,... | collective-permute-start | bytes 221192 | tf_op jit(solution)/shard_map/output_projection/ppermute | solution.py:43
  127.6 4.5 %collective-permute-start.4 = (bf16[48,768]{1,0:T(8,128)(2,1)S(1)}, bf16[48,768]{1,0:T(8,128)(2,1)S(1)}, u32[]{:S(2)}, u32[]{:S(2)}) collective-permute-start(bf16[48,768]{1,0:T(8,128)(2,1)S(1)} %get-tuple-element.60), channel_id=1, source_target_pairs={{0,2},{1,3},{2,4},{3,5},{4,6},{5,7},{6,0},{7,1},{8,10},{9,11},{10,... | collective-permute-start | bytes 221192 | tf_op jit(solution)/shard_map/output_projection/ppermute | solution.py:43
  127.7 5.8 %collective-permute-start.5 = (bf16[48,768]{1,0:T(8,128)(2,1)S(1)}, bf16[48,768]{1,0:T(8,128)(2,1)S(1)}, u32[]{:S(2)}, u32[]{:S(2)}) collective-permute-start(bf16[48,768]{1,0:T(8,128)(2,1)S(1)} %get-tuple-element.60), channel_id=1, source_target_pairs={{0,4},{1,5},{2,6},{3,7},{4,0},{5,1},{6,2},{7,3},{8,12},{9,13},{10,... | collective-permute-start | bytes 221192 | tf_op jit(solution)/shard_map/output_projection/ppermute | solution.py:43
  131.0 3.5 %collective-permute-start.6 = (bf16[48,768]{1,0:T(8,128)(2,1)S(1)}, bf16[48,768]{1,0:T(8,128)(2,1)S(1)}, u32[]{:S(2)}, u32[]{:S(2)}) collective-permute-start(bf16[48,768]{1,0:T(8,128)(2,1)S(1)} %get-tuple-element.60), channel_id=1, source_target_pairs={{0,6},{1,7},{2,0},{3,1},{4,2},{5,3},{6,4},{7,5},{8,14},{9,15},{10,... | collective-permute-start | bytes 221192 | tf_op jit(solution)/shard_map/output_projection/ppermute | solution.py:43
  134.5 4.9 %collective-permute-start.7 = (bf16[192,768]{1,0:T(8,128)(2,1)S(1)}, bf16[192,768]{1,0:T(8,128)(2,1)S(1)}, u32[]{:S(2)}, u32[]{:S(2)}) collective-permute-start(bf16[192,768]{1,0:T(8,128)(2,1)S(1)} %pad_maximum_fusion.near_ref), channel_id=1, source_target_pairs={{0,1},{1,0},{2,3},{3,2},{4,5},{5,4},{6,7},{7,6},{8,9},{9,8},{10,11... | collective-permute-start | bytes 884744 | tf_op jit(solution)/shard_map/output_projection/ppermute | solution.py:48
  148.5 29.6 %copy-start.4 = (bf16[96,2688]{1,0:T(8,128)(2,1)S(1)}, bf16[96,2688]{1,0:T(8,128)(2,1)}, u32[]{:S(2)}) copy-start(bf16[96,2688]{1,0:T(8,128)(2,1)} %get-tuple-element.43.refs_0_) | copy-start | bytes 1548292
  148.5 30.6 %all-to-all-start.3 = ((bf16[4,96,2816]{2,1,0:T(8,128)(2,1)}), bf16[4,96,2816]{2,1,0:T(8,128)(2,1)S(1)}, u32[]{:S(2)}, u32[]{:S(2)}) async-start(bf16[4,96,2816]{2,1,0:T(8,128)(2,1)} %get-tuple-element.38), calls=%async_computation.3 | async-start | bytes 4325376 | tf_op jit(solution)/shard_map/gate_up/all_to_all | solution.py:90
  152.3 15.0 %collective-permute-start.11 = (bf16[96,2688]{1,0:T(8,128)(2,1)}, bf16[96,2688]{1,0:T(8,128)(2,1)S(1)}, u32[]{:S(2)}, u32[]{:S(2)}) collective-permute-start(bf16[96,2688]{1,0:T(8,128)(2,1)} %get-tuple-element.44), channel_id=1, source_target_pairs={{0,32},{8,40},{16,48},{24,56},{32,64},{40,72},{48,80},{56,88},{64,... | collective-permute-start | bytes 1548296 | tf_op jit(solution)/shard_map/gate_up/ppermute | solution.py:38
  152.6 24.6 %collective-permute-start.12 = (bf16[96,2688]{1,0:T(8,128)(2,1)}, bf16[96,2688]{1,0:T(8,128)(2,1)S(1)}, u32[]{:S(2)}, u32[]{:S(2)}) collective-permute-start(bf16[96,2688]{1,0:T(8,128)(2,1)} %get-tuple-element.45), channel_id=1, source_target_pairs={{0,64},{8,72},{16,80},{24,88},{32,96},{40,104},{48,112},{56,120},{... | collective-permute-start | bytes 1548296 | tf_op jit(solution)/shard_map/gate_up/ppermute | solution.py:38
  154.4 23.7 %collective-permute-start.13 = (bf16[96,2688]{1,0:T(8,128)(2,1)S(1)}, bf16[96,2688]{1,0:T(8,128)(2,1)S(1)}, u32[]{:S(2)}, u32[]{:S(2)}) collective-permute-start(bf16[96,2688]{1,0:T(8,128)(2,1)S(1)} %copy-done.11), channel_id=1, source_target_pairs={{0,96},{8,104},{16,112},{24,120},{32,0},{40,8},{48,16},{56,24},{64... | collective-permute-start | bytes 1548296 | tf_op jit(solution)/shard_map/gate_up/ppermute | solution.py:38
  179.2 11.4 %all-to-all-start.4 = ((bf16[4,24,2688]{2,1,0:T(8,128)(2,1)}), bf16[4,24,2688]{2,1,0:T(8,128)(2,1)S(1)}, u32[]{:S(2)}, u32[]{:S(2)}) async-start(bf16[4,24,2688]{2,1,0:T(8,128)(2,1)} %fold_stacked.1), calls=%async_computation.4 | async-start | bytes 1032192 | tf_op jit(solution)/shard_map/gate_up/all_to_all | solution.py:90
  183.5 7.0 %collective-permute-start.10 = (bf16[24,2816]{1,0:T(8,128)(2,1)S(1)}, bf16[24,2816]{1,0:T(8,128)(2,1)S(1)}, u32[]{:S(2)}, u32[]{:S(2)}) collective-permute-start(bf16[24,2816]{1,0:T(8,128)(2,1)S(1)} %get-tuple-element.42), channel_id=1, source_target_pairs={{0,96},{8,104},{16,112},{24,120},{32,0},{40,8},{48,16},{56,24},{64... | collective-permute-start | bytes 405512 | tf_op jit(solution)/shard_map/gate_up/ppermute | solution.py:38
  187.0 8.7 %collective-permute-start.8 = (bf16[24,2816]{1,0:T(8,128)(2,1)S(1)}, bf16[24,2816]{1,0:T(8,128)(2,1)S(1)}, u32[]{:S(2)}, u32[]{:S(2)}) collective-permute-start(bf16[24,2816]{1,0:T(8,128)(2,1)S(1)} %get-tuple-element.40), channel_id=1, source_target_pairs={{0,32},{8,40},{16,48},{24,56},{32,64},{40,72},{48,80},{56,88},{64,... | collective-permute-start | bytes 405512 | tf_op jit(solution)/shard_map/gate_up/ppermute | solution.py:38
  187.0 8.7 %collective-permute-start.9 = (bf16[24,2816]{1,0:T(8,128)(2,1)S(1)}, bf16[24,2816]{1,0:T(8,128)(2,1)S(1)}, u32[]{:S(2)}, u32[]{:S(2)}) collective-permute-start(bf16[24,2816]{1,0:T(8,128)(2,1)S(1)} %get-tuple-element.41), channel_id=1, source_target_pairs={{0,64},{8,72},{16,80},{24,88},{32,96},{40,104},{48,112},{56,120},{... | collective-permute-start | bytes 405512 | tf_op jit(solution)/shard_map/gate_up/ppermute | solution.py:38
  196.2 30.1 %copy-start = (bf16[2688,768]{1,0:T(8,128)(2,1)S(1)}, bf16[2688,768]{1,0:T(8,128)(2,1)}, u32[]{:S(2)}) copy-start(bf16[2688,768]{1,0:T(8,128)(2,1)} %weight_ref.5) | copy-start | bytes 12386308
  228.7 4.2 %collective-permute-start.14 = (bf16[192,768]{1,0:T(8,128)(2,1)S(1)}, bf16[192,768]{1,0:T(8,128)(2,1)S(1)}, u32[]{:S(2)}, u32[]{:S(2)}) collective-permute-start(bf16[192,768]{1,0:T(8,128)(2,1)S(1)} %get-tuple-element.48), channel_id=1, source_target_pairs={{0,1},{1,0},{2,3},{3,2},{4,5},{5,4},{6,7},{7,6},{8,9},{9,8},{10,11... | collective-permute-start | bytes 884744 | tf_op jit(solution)/shard_map/down_projection/ppermute | solution.py:48
  233.0 4.5 %collective-permute-start.15 = (bf16[48,768]{1,0:T(8,128)(2,1)S(1)}, bf16[48,768]{1,0:T(8,128)(2,1)S(1)}, u32[]{:S(2)}, u32[]{:S(2)}) collective-permute-start(bf16[48,768]{1,0:T(8,128)(2,1)S(1)} %get-tuple-element.50), channel_id=1, source_target_pairs={{0,2},{1,3},{2,4},{3,5},{4,6},{5,7},{6,0},{7,1},{8,10},{9,11},{10,... | collective-permute-start | bytes 221192 | tf_op jit(solution)/shard_map/down_projection/ppermute | solution.py:43
  233.1 6.1 %collective-permute-start.16 = (bf16[48,768]{1,0:T(8,128)(2,1)S(1)}, bf16[48,768]{1,0:T(8,128)(2,1)S(1)}, u32[]{:S(2)}, u32[]{:S(2)}) collective-permute-start(bf16[48,768]{1,0:T(8,128)(2,1)S(1)} %get-tuple-element.51), channel_id=1, source_target_pairs={{0,4},{1,5},{2,6},{3,7},{4,0},{5,1},{6,2},{7,3},{8,12},{9,13},{10,... | collective-permute-start | bytes 221192 | tf_op jit(solution)/shard_map/down_projection/ppermute | solution.py:43
  235.8 4.2 %collective-permute-start.17 = (bf16[48,768]{1,0:T(8,128)(2,1)S(1)}, bf16[48,768]{1,0:T(8,128)(2,1)S(1)}, u32[]{:S(2)}, u32[]{:S(2)}) collective-permute-start(bf16[48,768]{1,0:T(8,128)(2,1)S(1)} %get-tuple-element.52), channel_id=1, source_target_pairs={{0,6},{1,7},{2,0},{3,1},{4,2},{5,3},{6,4},{7,5},{8,14},{9,15},{10,... | collective-permute-start | bytes 221192 | tf_op jit(solution)/shard_map/down_projection/ppermute | solution.py:43
  (10 other events, 66.1 us)
